TPU v7x, 256 devices: a whole 4x4x8 slice. The times are simulated.
256 devices in a mesh: wide: 64 (over z, y, core), narrow: 4 (over x).
Axes of the slice: x: 4, y: 4, z: 8, core: 2. Of those that a mesh axis runs over, the one named last changes fastest.
Arguments:
- tokens: bfloat16 [32768, 1024], P('wide'), may hold values from -1.5 to 1.5
- w_qk1: bfloat16 [1024, 1024], P(None, 'narrow')
- w_value1: bfloat16 [1024, 1024], P(None, 'narrow'), may hold values from -0.1875 to 0.1875
- w_out1: bfloat16 [1024, 1024], P('narrow'), may hold values from -0.1875 to 0.1875
- w_qk2: bfloat16 [1024, 1024], P(None, 'narrow')
- w_value2: bfloat16 [1024, 1024], P(None, 'narrow'), may hold values from -0.1875 to 0.1875
- w_out2: bfloat16 [1024, 1024], P('narrow'), may hold values from -0.5 to 0.5
- cluster_ids: int32 [8, 32768], P('narrow', 'wide'), may hold values from 0 to 31, as said below
Outputs:
- layer_out: float32 [32768, 1024], P('wide', 'narrow')
Inputs may be any that keep to these rules, and one draw needn't show every extreme that they name: `cluster_ids`: within the 512 tokens of one index of wide, for each head, a quarter of the clusters hold 32 tokens each, half hold 12 and a quarter hold 8; which clusters are which is the same in every such block of one head.
All inputs are finite; a program needn't handle non-finite values.
Results may differ from a plain program's by a relative error of at most 0.022.
Values may be sent and summed in bfloat16 or wider, within the bound.
No kernel may reach another device: no remote copies, remote signals or barrier semaphores. Data moves between devices by JAX's collectives and lax.ppermute only.
A program may use at most 64 MiB of HBM per device.

v0:
```python
import math

import jax
import jax.numpy as jnp
from jax import lax
from jax.sharding import PartitionSpec as P

HEAD_DIM = 128
WINDOW = 256


EPS = 1e-06


def from_behind(value, axis, steps):
    count = lax.axis_size(axis)
    initial, last = (max(0, -steps), min(count, count - steps))
    return lax.ppermute(value, axis, [(source, source + steps) for source in range(initial, last)])


def rms_round(rows):
    values = rows.astype(jnp.float32)
    factor = lax.rsqrt(jnp.mean(values * values, axis=-1, keepdims=True) + EPS)
    return (values * factor).astype(jnp.bfloat16)


def project(normed, weight):
    return jnp.dot(normed, weight, preferred_element_type=jnp.float32).astype(jnp.bfloat16)


def window_attention(query, keys, values, first_pos):
    length = query.shape[0]
    block = min(512, length)
    heads = query.shape[1] // HEAD_DIM
    factor = 1.0 / math.sqrt(HEAD_DIM)

    def one_block(start):
        q = query.reshape(block, heads, HEAD_DIM)
        k = keys.reshape(block + WINDOW, heads, HEAD_DIM)
        v = values.reshape(block + WINDOW, heads, HEAD_DIM)
        scores = jnp.einsum("qhd,khd->hqk", q, k, preferred_element_type=jnp.float32) * factor
        qpos = first_pos + start + jnp.arange(block, dtype=jnp.int32)
        kpos = first_pos + start - WINDOW + jnp.arange(block + WINDOW, dtype=jnp.int32)
        gap = qpos[:, None] - kpos[None, :]
        keep = (gap > 0) & (gap < WINDOW) & (kpos[None, :] >= 0) | (gap == 0) & (qpos[:, None] == 0)
        scores = jnp.where(keep[None], scores, -1e30)
        top = jnp.max(scores, axis=-1, keepdims=True)
        weights = jnp.exp(scores - top)
        totals = jnp.sum(weights, axis=-1)
        mixed = jnp.einsum(
            "hqk,khd->qhd", weights.astype(jnp.bfloat16), v, preferred_element_type=jnp.float32
        )
        mixed = mixed / jnp.transpose(totals)[:, :, None]
        return mixed.reshape(block, heads * HEAD_DIM).astype(jnp.bfloat16)

    starts = jnp.arange(length // block, dtype=jnp.int32) * block
    return lax.map(one_block, starts).reshape(length, heads * HEAD_DIM)


def owner_softmax(query_rows, key_rows, value_rows, live, start):
    factor = 1.0 / math.sqrt(HEAD_DIM)
    scores = (
        lax.dot_general(
            query_rows, key_rows, (((1,), (1,)), ((), ())), preferred_element_type=jnp.float32
        )
        * factor
    )
    rows_here = start + jnp.arange(query_rows.shape[0], dtype=jnp.int32)
    order = jnp.arange(key_rows.shape[0], dtype=jnp.int32)
    earlier = order[None, :] < rows_here[:, None]
    alone = (order[None, :] == rows_here[:, None]) & (rows_here[:, None] == 0)
    keep = (earlier | alone) & live[None, :]
    scores = jnp.where(keep, scores, -1e30)
    top = jnp.max(scores, axis=-1, keepdims=True)
    weights = jnp.exp(scores - top)
    totals = jnp.sum(weights, axis=-1)
    mixed = jnp.dot(weights.astype(jnp.bfloat16), value_rows, preferred_element_type=jnp.float32)
    return (mixed / totals[:, None]).astype(jnp.bfloat16)


def by_head(matrix, heads):
    length = matrix.shape[0]
    return jnp.transpose(matrix.reshape(length, heads, HEAD_DIM), (1, 0, 2))


def shards(tokens, w_qk1, w_value1, w_out1, w_qk2, w_value2, w_out2, cluster_ids):
    length = tokens.shape[0]
    first_pos = lax.axis_index("wide") * length
    normed = rms_round(tokens)
    qk1 = project(normed, w_qk1)
    value1 = project(normed, w_value1)
    tails = jnp.stack([qk1[length - WINDOW :], value1[length - WINDOW :]])
    before = from_behind(tails, "wide", 1)
    keys = jnp.concatenate([before[0], qk1], axis=0)
    values = jnp.concatenate([before[1], value1], axis=0)
    attended1 = window_attention(qk1, keys, values, first_pos)
    partial_value = jnp.dot(attended1, w_out1, preferred_element_type=jnp.float32)
    summed = lax.psum(partial_value.astype(jnp.bfloat16), "narrow").astype(jnp.float32)
    hidden = (tokens.astype(jnp.float32) + summed).astype(jnp.bfloat16)
    normed2 = rms_round(hidden)
    qk2 = project(normed2, w_qk2)
    value2 = project(normed2, w_value2)
    heads = qk2.shape[1] // HEAD_DIM
    width_count = lax.axis_size("wide")
    capacity = 2 * length * heads // width_count
    clusters = width_count // heads
    match = cluster_ids[:, :, None] == jnp.arange(clusters, dtype=jnp.int32)[None, None, :]
    running = jnp.cumsum(match.astype(jnp.int32), axis=1)
    place = jnp.sum(jnp.where(match, running, 0), axis=2) - 1
    owner = cluster_ids + jnp.arange(heads, dtype=jnp.int32)[:, None] * clusters
    target = (owner * capacity + place).reshape(-1)
    items = jnp.concatenate([by_head(qk2, heads), by_head(value2, heads)], axis=2).reshape(
        heads * length, 2 * HEAD_DIM
    )
    outgoing = jnp.zeros((width_count * capacity, 2 * HEAD_DIM), jnp.bfloat16).at[target].set(items)
    outgoing = outgoing.reshape(width_count, capacity, 2 * HEAD_DIM)
    sent = jnp.sum(
        (owner.reshape(-1)[:, None] == jnp.arange(width_count, dtype=jnp.int32)[None, :]).astype(
            jnp.int32
        ),
        axis=0,
    ).reshape(width_count, 1)
    arrived, arrived_counts = (
        lax.all_to_all(outgoing, "wide", split_axis=0, concat_axis=0, tiled=True),
        lax.all_to_all(sent, "wide", split_axis=0, concat_axis=0, tiled=True),
    )
    slots = width_count * capacity
    flat = arrived.reshape(slots, 2 * HEAD_DIM)
    key_rows = flat[:, :HEAD_DIM]
    value_rows = flat[:, HEAD_DIM:]
    live = (jnp.arange(capacity, dtype=jnp.int32)[None, :] < arrived_counts).reshape(slots)
    block = min(512, slots)

    def dense_block(start):
        rows_now = lax.dynamic_slice_in_dim(key_rows, start, block, 0)
        return owner_softmax(rows_now, key_rows, value_rows, live, start)

    starts = jnp.arange(slots // block, dtype=jnp.int32) * block
    answers = lax.map(dense_block, starts).reshape(slots, HEAD_DIM)
    returned = lax.all_to_all(
        answers.reshape(width_count, capacity, HEAD_DIM),
        "wide",
        split_axis=0,
        concat_axis=0,
        tiled=True,
    )
    picked = returned.reshape(slots, HEAD_DIM)[target].reshape(heads, length, HEAD_DIM)
    attended2 = jnp.transpose(picked, (1, 0, 2)).reshape(length, heads * HEAD_DIM)
    partial2 = jnp.dot(attended2, w_out2, preferred_element_type=jnp.float32)
    share2 = lax.psum_scatter(
        partial2.astype(jnp.bfloat16), "narrow", scatter_dimension=1, tiled=True
    ).astype(jnp.float32)
    width_out = share2.shape[1]
    own_hidden = lax.dynamic_slice_in_dim(
        hidden, lax.axis_index("narrow") * width_out, width_out, 1
    )
    return own_hidden.astype(jnp.float32) + share2


def solution(mesh):
    placed = (
        P("wide", None),
        P(None, "narrow"),
        P(None, "narrow"),
        P("narrow", None),
        P(None, "narrow"),
        P(None, "narrow"),
        P("narrow", None),
        P("narrow", "wide"),
    )
    return jax.shard_map(
        shards, mesh=mesh, in_specs=placed, out_specs=P("wide", "narrow"), check_vma=False
    )
```

profile of v0, /device:TPU:1, one launch (start us, length us, event | category | flops | bytes accessed | tf_op | source)
XLA Modules:
  0.0 226.9 jit_solution(778882510403868357)
XLA Ops:
  6.5 1.7 fusion.29
  8.2 1.9 convolution_convert_fusion.4
  10.8 4.6 %collective-permute-start = (bf16[2,256,256]{1,2,0:T(8,128)(2,1)S(1)}, bf16[2,256,256]{1,2,0:T(8,128)(2,1)S(1)}, u32[]{:S(2)}, u32[]{:S(2)}) collective-permute-start(bf16[2,256,256]{1,2,0:T(8,128)(2,1)S(1)} %pad_maximum_fusion.1), channel_id=1, source_target_pairs={{0,4},{4,8},{8,12},{12,16},{16,20},{20,24},{24,28},{28,32},{32,36}... | collective-permute-start | bytes 786440 | tf_op jit(solution)/shard_map/ppermute | solution.py:18
  15.7 0.7 fusion.36
  16.4 2.3 %collective-permute-done = bf16[2,256,256]{1,2,0:T(8,128)(2,1)S(1)} collective-permute-done((bf16[2,256,256]{1,2,0:T(8,128)(2,1)S(1)}, bf16[2,256,256]{1,2,0:T(8,128)(2,1)S(1)}, u32[]{:S(2)}, u32[]{:S(2)}) %collective-permute-start) | collective-permute-done | bytes 262176 | tf_op jit(solution)/shard_map/ppermute | solution.py:18
  18.8 1.0 fusion.24
  19.8 0.9 fusion.25
  20.7 1.2 fusion.45
  22.0 1.5 convolution_convert_fusion.1
  23.5 2.3 %reduce-window.6 = s32[2,32,4,128]{3,1,2,0:T(8,128)S(1)} reduce-window(s32[2,32,4,128]{3,1,2,0:T(8,128)S(1)} %fusion.63, s32[]{:T(128)} %constant.49.clone.1), window={size=1x1x1x128 pad=0_0x0_0x0_0x127_0}, to_apply=%region_4.5 | reduce-window | flops 4161536 | bytes 262148 | tf_op jit(solution)/shard_map/reduce-window
  26.6 0.7 copy.41
  27.3 13.6 %all-to-all-start = ((s32[64,1,1]{2,1,0:T(1,128)}), s32[64,1,1]{2,1,0:T(1,128)S(1)}, u32[]{:S(2)}, u32[]{:S(2)}) async-start(s32[64,1,1]{2,1,0:T(1,128)} %copy.41), calls=%async_computation | async-start | bytes 65536 | tf_op jit(solution)/shard_map/all_to_all | solution.py:125
  40.9 36.5 %all-reduce.2.cloned.1.call-done = bf16[512,1024]{1,0:T(8,128)(2,1)} async-done(((bf16[512,1024]{1,0:T(8,128)(2,1)}), bf16[512,1024]{1,0:T(8,128)(2,1)}) %all-reduce.2.cloned.1.call-update) | async-done | bytes 1048592 | tf_op jit(solution)/shard_map/psum | solution.py:98
  77.5 1.7 fusion.27
  79.2 1.6 convolution_convert_fusion.3
  80.9 1.6 convolution_convert_fusion.2
  82.8 6.0 %scatter_custom_fusion = bf16[2048,256]{1,0:T(8,128)(2,1)} fusion(s32[1024]{0:T(1024)S(1)} %bitcast.93, bf16[1024,256]{1,0:T(8,128)(2,1)S(1)} %bitcast.86, bf16[]{:T(256)} %constant.65.clone.1), kind=kCustom, calls=%fused_computation.58 | custom fusion | bytes 1048578 | tf_op jit(solution)/shard_map/scatter | solution.py:115
  88.8 12.1 %all-to-all-start.1 = ((bf16[64,32,256]{2,1,0:T(8,128)(2,1)}), bf16[64,32,256]{2,1,0:T(8,128)(2,1)S(1)}, u32[]{:S(2)}, u32[]{:S(2)}) async-start(bf16[64,32,256]{2,1,0:T(8,128)(2,1)} %bitcast.16), calls=%async_computation.1 | async-start | bytes 2097152 | tf_op jit(solution)/shard_map/all_to_all | solution.py:124
  100.9 1.2 reduce.1
  102.2 26.7 %all-to-all-done.1 = bf16[64,32,256]{2,1,0:T(8,128)(2,1)S(1)} async-done(((bf16[64,32,256]{2,1,0:T(8,128)(2,1)}), bf16[64,32,256]{2,1,0:T(8,128)(2,1)S(1)}, u32[]{:S(2)}, u32[]{:S(2)}) %all-to-all-start.1) | async-done | bytes 1048608 | tf_op jit(solution)/shard_map/all_to_all | solution.py:124
  128.9 0.9 fusion.70
  129.8 38.6 %while.3 = (s32[]{:T(128)}, bf16[4,512,128]{2,1,0:T(8,128)(2,1)}, s32[4]{0:T(128)S(1)}, bf16[2048,128]{1,0:T(8,128)(2,1)}, bf16[2048,128]{1,0:T(8,128)(2,1)S(1)}...) while((s32[]{:T(128)}, bf16[4,512,128]{2,1,0:T(8,128)(2,1)}, s32[4]{0:T(128)S(1)}, ...), condition=%wide.region_13.14_spmd.clone, body=%wide.region_10.13_spmd.clone.sunk | while | flops 549587456 | bytes 13918103 | solution.py:139
  132.5 0.7 iota_add_fusion.4
  133.2 0.7 broadcast_compare_fusion.4
  134.1 3.2 %fusion.92 = (f32[512]{0:T(512)S(1)}, f32[512,2048]{1,0:T(8,128)S(1)}) fusion(bf16[2048,128]{1,0:T(8,128)(2,1)} %get-tuple-element.159, s32[]{:T(128)S(6)} %select_n.58, pred[2048]{0:T(1024)(128)(4,1)S(1)} %and.92, pred[512]{0:T(512)(128)(4,1)S(1)} %broadcast_compare_fusion.4, s32[512]{0:T(512)S(1)} %iota_add_fusion.4), kind=kOutput, calls=%fused_computation.96.clone.1 | convolution fusion | flops 276823552 | bytes 4856324 | tf_op jit(solution)/shard_map/while/body/eval_jaxpr/dot_general | solution.py:63
  137.2 0.7 fusion.93
  138.0 1.5 fusion.94
  142.1 0.7 iota_add_fusion.4
  142.8 0.7 broadcast_compare_fusion.4
  143.7 3.2 %fusion.92 = (f32[512]{0:T(512)S(1)}, f32[512,2048]{1,0:T(8,128)S(1)}) fusion(bf16[2048,128]{1,0:T(8,128)(2,1)} %get-tuple-element.159, s32[]{:T(128)S(6)} %select_n.58, pred[2048]{0:T(1024)(128)(4,1)S(1)} %and.92, pred[512]{0:T(512)(128)(4,1)S(1)} %broadcast_compare_fusion.4, s32[512]{0:T(512)S(1)} %iota_add_fusion.4), kind=kOutput, calls=%fused_computation.96.clone.1 | convolution fusion | flops 276823552 | bytes 4856324 | tf_op jit(solution)/shard_map/while/body/eval_jaxpr/dot_general | solution.py:63
  146.9 0.7 fusion.93
  147.6 1.5 fusion.94
  151.8 0.7 iota_add_fusion.4
  152.5 0.7 broadcast_compare_fusion.4
  153.4 3.2 %fusion.92 = (f32[512]{0:T(512)S(1)}, f32[512,2048]{1,0:T(8,128)S(1)}) fusion(bf16[2048,128]{1,0:T(8,128)(2,1)} %get-tuple-element.159, s32[]{:T(128)S(6)} %select_n.58, pred[2048]{0:T(1024)(128)(4,1)S(1)} %and.92, pred[512]{0:T(512)(128)(4,1)S(1)} %broadcast_compare_fusion.4, s32[512]{0:T(512)S(1)} %iota_add_fusion.4), kind=kOutput, calls=%fused_computation.96.clone.1 | convolution fusion | flops 276823552 | bytes 4856324 | tf_op jit(solution)/shard_map/while/body/eval_jaxpr/dot_general | solution.py:63
  156.5 0.7 fusion.93
  157.3 1.5 fusion.94
  161.4 0.7 iota_add_fusion.4
  162.1 0.7 broadcast_compare_fusion.4
  163.0 3.2 %fusion.92 = (f32[512]{0:T(512)S(1)}, f32[512,2048]{1,0:T(8,128)S(1)}) fusion(bf16[2048,128]{1,0:T(8,128)(2,1)} %get-tuple-element.159, s32[]{:T(128)S(6)} %select_n.58, pred[2048]{0:T(1024)(128)(4,1)S(1)} %and.92, pred[512]{0:T(512)(128)(4,1)S(1)} %broadcast_compare_fusion.4, s32[512]{0:T(512)S(1)} %iota_add_fusion.4), kind=kOutput, calls=%fused_computation.96.clone.1 | convolution fusion | flops 276823552 | bytes 4856324 | tf_op jit(solution)/shard_map/while/body/eval_jaxpr/dot_general | solution.py:63
  166.2 0.7 fusion.93
  166.9 1.5 fusion.94
  168.4 6.6 %all-to-all-start.2 = ((bf16[64,32,128]{2,1,0:T(8,128)(2,1)}), bf16[64,32,128]{2,1,0:T(8,128)(2,1)S(1)}, u32[]{:S(2)}, u32[]{:S(2)}) async-start(bf16[64,32,128]{2,1,0:T(8,128)(2,1)} %bitcast.19), calls=%async_computation.2 | async-start | bytes 1048576 | tf_op jit(solution)/shard_map/all_to_all | solution.py:140
  175.0 17.7 %all-to-all-done.2 = bf16[64,32,128]{2,1,0:T(8,128)(2,1)S(1)} async-done(((bf16[64,32,128]{2,1,0:T(8,128)(2,1)}), bf16[64,32,128]{2,1,0:T(8,128)(2,1)S(1)}, u32[]{:S(2)}, u32[]{:S(2)}) %all-to-all-start.2) | async-done | bytes 524320 | tf_op jit(solution)/shard_map/all_to_all | solution.py:140
  192.7 3.2 %gather_fusion = bf16[1024,128]{1,0:T(8,128)(2,1)S(1)} fusion(bf16[2048,128]{1,0:T(8,128)(2,1)S(1)} %bitcast.78, s32[1024]{0:T(1024)S(1)} %broadcast_clamp_fusion), kind=kCustom, calls=%fused_computation | custom fusion | bytes 528384 | tf_op jit(solution)/shard_map/gather | solution.py:147
  196.1 1.4 convolution_convert_fusion
  197.5 20.7 %reduce-scatter.2.cloned.1.call-done = bf16[512,256]{1,0:T(8,128)(2,1)} async-done(((bf16[512,1024]{1,0:T(8,128)(2,1)}), bf16[512,256]{1,0:T(8,128)(2,1)}) %reduce-scatter.2.cloned.1.call-update) | async-done | bytes 262160 | tf_op jit(solution)/shard_map/reduce_scatter | solution.py:150
  218.2 1.8 convert_add_fusion.1
  (58 shorter events, 5.6 us)
Async XLA Ops:
  6.5 15.5 %copy-start = (bf16[256,1024]{1,0:T(8,128)(2,1)S(1)}, bf16[256,1024]{1,0:T(8,128)(2,1)}, u32[]{:S(2)}) copy-start(bf16[256,1024]{1,0:T(8,128)(2,1)} %param.13) | copy-start | bytes 1572868
  6.5 3.6 %copy-start.1 = (bf16[512,1024]{1,0:T(8,128)(2,1)S(1)}, bf16[512,1024]{1,0:T(8,128)(2,1)}, u32[]{:S(2)}) copy-start(bf16[512,1024]{1,0:T(8,128)(2,1)} %param.10) | copy-start | bytes 3145732
  6.5 3.6 %copy-start.4 = (bf16[1024,256]{1,0:T(8,128)(2,1)S(1)}, bf16[1024,256]{1,0:T(8,128)(2,1)}, u32[]{:S(2)}) copy-start(bf16[1024,256]{1,0:T(8,128)(2,1)} %param.11) | copy-start | bytes 1572868
  6.5 70.9 %all-reduce.2.cloned.1.call-start = ((), (), s32[]{:S(2)}) async-start(), calls=%async_computation.4 | async-start | bytes 2097152 | tf_op jit(solution)/shard_map/psum | solution.py:98
  8.2 7.4 %copy-start.3 = (s32[2,512]{1,0:T(2,128)S(1)}, s32[2,512]{1,0:T(2,128)}, u32[]{:S(2)}) copy-start(s32[2,512]{1,0:T(2,128)} %param.17) | copy-start | bytes 12292
  10.8 7.9 %collective-permute-start = (bf16[2,256,256]{1,2,0:T(8,128)(2,1)S(1)}, bf16[2,256,256]{1,2,0:T(8,128)(2,1)S(1)}, u32[]{:S(2)}, u32[]{:S(2)}) collective-permute-start(bf16[2,256,256]{1,2,0:T(8,128)(2,1)S(1)} %pad_maximum_fusion.1), channel_id=1, source_target_pairs={{0,4},{4,8},{8,12},{12,16},{16,20},{20,24},{24,28},{28,32},{32,36}... | collective-permute-start | bytes 786440 | tf_op jit(solution)/shard_map/ppermute | solution.py:18
  27.3 61.6 %all-to-all-start = ((s32[64,1,1]{2,1,0:T(1,128)}), s32[64,1,1]{2,1,0:T(1,128)S(1)}, u32[]{:S(2)}, u32[]{:S(2)}) async-start(s32[64,1,1]{2,1,0:T(1,128)} %copy.41), calls=%async_computation | async-start | bytes 65536 | tf_op jit(solution)/shard_map/all_to_all | solution.py:125
  88.8 40.1 %all-to-all-start.1 = ((bf16[64,32,256]{2,1,0:T(8,128)(2,1)}), bf16[64,32,256]{2,1,0:T(8,128)(2,1)S(1)}, u32[]{:S(2)}, u32[]{:S(2)}) async-start(bf16[64,32,256]{2,1,0:T(8,128)(2,1)} %bitcast.16), calls=%async_computation.1 | async-start | bytes 2097152 | tf_op jit(solution)/shard_map/all_to_all | solution.py:124
  168.4 27.7 %copy-start.2 = (bf16[256,1024]{1,0:T(8,128)(2,1)S(1)}, bf16[256,1024]{1,0:T(8,128)(2,1)}, u32[]{:S(2)}) copy-start(bf16[256,1024]{1,0:T(8,128)(2,1)} %param.16) | copy-start | bytes 1572868
  168.4 24.3 %all-to-all-start.2 = ((bf16[64,32,128]{2,1,0:T(8,128)(2,1)}), bf16[64,32,128]{2,1,0:T(8,128)(2,1)S(1)}, u32[]{:S(2)}, u32[]{:S(2)}) async-start(bf16[64,32,128]{2,1,0:T(8,128)(2,1)} %bitcast.19), calls=%async_computation.2 | async-start | bytes 1048576 | tf_op jit(solution)/shard_map/all_to_all | solution.py:140
  175.0 43.3 %reduce-scatter.2.cloned.1.call-start = ((), (), s32[]{:S(2)}) async-start(), calls=%async_computation.5 | async-start | bytes 1310720 | tf_op jit(solution)/shard_map/reduce_scatter | solution.py:150
Sparse Core Ops, SparseCore 0:
  23.6 53.7 all-reduce.1
  197.6 20.5 reduce-scatter.1
where the time goes:
time: 228 us; the launch traced here: 227 us
  waiting for transfers between devices  104 us (46%)
  starting transfers between devices  36.9 us (16%)
  matrix products  29.4 us (13%)
  other arithmetic  19.5 us (9%)
  local copies, waits for them, and re-layouts  15 us (7%)
  between operations  13.7 us (6%)
  loops' own time  8.37 us (4%)
    psum x1, waiting for transfers between devices, shards(): lax.psum(partial_value.astype(jnp.bfloat16), 'narrow').astype(jnp.float32)  36.5 us
    all_to_all x1, waiting for transfers between devices, shards(): lax.all_to_all(outgoing, 'wide', split_axis=0, concat_axis=0, tiled=True)  26.7 us
    reduce_scatter x1, waiting for transfers between devices, shards(): lax.psum_scatter(partial2.astype(jnp.bfloat16), 'narrow', scatter_dimensi...  20.7 us
    all_to_all x1, waiting for transfers between devices, shards(): lax.all_to_all(answers.reshape(width_count, capacity, HEAD_DIM), 'wide',...  17.7 us
    all_to_all x1, starting transfers between devices, shards(): lax.all_to_all(sent, 'wide', split_axis=0, concat_axis=0, tiled=True)  13.6 us
    dot_general x4, matrix products, owner_softmax(): lax.dot_general(query_rows, key_rows, (((1,), (1,)), ((), ())), preferred...  12.7 us
    all_to_all x1, starting transfers between devices, shards(): lax.all_to_all(outgoing, 'wide', split_axis=0, concat_axis=0, tiled=True)  12.1 us
    another operation x1, loops' own time, shards(): answers = lax.map(dense_block, starts).reshape(slots, HEAD_DIM)  8.37 us
  transfers between devices with their start and end apart: 6, of which 5 were waited for; matrix products, arithmetic and copies ran while one was open for 8% of the time, Pallas kernels for 0%

commit v1 on v0

v1 whole, which is shorter than its diff:
```python
import functools
import math

import jax
import jax.numpy as jnp
from jax import lax
from jax.experimental import pallas as pl
from jax.experimental.pallas import tpu as pltpu
from jax.sharding import PartitionSpec as P

HEAD_DIM = 128
WINDOW = 256
EPS = 1e-06
MASKED = -1e30
EXP2_FACTOR = math.log2(math.e) / math.sqrt(HEAD_DIM)
CLUSTERS = 32
SLOTS = 512
BF16 = jnp.bfloat16
F32 = jnp.float32


def call(body, outs, args, scratch=(), prefetch=0, flops=0, bytes_accessed=0):
    whole = [pl.BlockSpec(memory_space=pltpu.SMEM)] * prefetch + [
        pl.BlockSpec(memory_space=pltpu.VMEM)
    ] * (len(args) - prefetch)
    return pl.pallas_call(
        body,
        out_shape=outs,
        in_specs=whole,
        out_specs=jax.tree.map(lambda _: pl.BlockSpec(memory_space=pltpu.VMEM), outs),
        scratch_shapes=list(scratch),
        compiler_params=pltpu.CompilerParams(vmem_limit_bytes=40 * 2**20),
        cost_estimate=pl.CostEstimate(
            flops=flops, bytes_accessed=bytes_accessed, transcendentals=0
        ),
    )(*args)


def rms_round(values):
    factor = lax.rsqrt(jnp.mean(values * values, axis=-1, keepdims=True) + EPS)
    return (values * factor).astype(BF16)


def matmul(left, right):
    return jnp.dot(left, right, preferred_element_type=F32)


def scores_of(query, keys):
    return lax.dot_general(query, keys, (((1,), (1,)), ((), ())), preferred_element_type=F32)


def front_body(tokens_ref, w_qk_ref, w_value_ref, qk_ref, value_ref, tail_ref):
    normed = rms_round(tokens_ref[...].astype(F32))
    qk = matmul(normed, w_qk_ref[...]).astype(BF16)
    value = matmul(normed, w_value_ref[...]).astype(BF16)
    length = qk.shape[0]
    qk_ref[...] = qk
    value_ref[...] = value
    tail_ref[0] = qk[length - WINDOW :]
    tail_ref[1] = value[length - WINDOW :]


def window_body(first_ref, qk_ref, value_ref, before_ref, out_ref):
    tile = WINDOW
    row = lax.broadcasted_iota(jnp.int32, (tile, 2 * tile), 0)
    col = lax.broadcasted_iota(jnp.int32, (tile, 2 * tile), 1)
    band = (col > row) & (col < row + WINDOW)
    at_start = first_ref[0] == 0
    opening = (band & (col >= tile)) | ((row == 0) & (col == tile))
    first_band = (jnp.logical_not(at_start) & band) | (at_start & opening)
    length = qk_ref.shape[0]
    ones = jnp.ones((2 * tile, HEAD_DIM), BF16)
    for head in range(2):
        cols = slice(head * HEAD_DIM, (head + 1) * HEAD_DIM)
        for part in range(length // tile):
            query = qk_ref[part * tile : (part + 1) * tile, cols]
            if part == 0:
                keys = jnp.concatenate([before_ref[0, :, cols], query], axis=0)
                values = jnp.concatenate([before_ref[1, :, cols], value_ref[:tile, cols]], axis=0)
            else:
                keys = qk_ref[(part - 1) * tile : (part + 1) * tile, cols]
                values = value_ref[(part - 1) * tile : (part + 1) * tile, cols]
            scores = jnp.where(first_band if part == 0 else band, scores_of(query, keys), MASKED)
            top = jnp.max(scores, axis=-1, keepdims=True)
            weights = jnp.exp2((scores - top) * EXP2_FACTOR).astype(BF16)
            mixed = matmul(weights, jnp.concatenate([values, ones], axis=1))
            out_ref[head, part * tile : (part + 1) * tile] = (
                mixed[:, :HEAD_DIM] / mixed[:, HEAD_DIM:]
            ).astype(BF16)


def place_body(ids_ref, place_ref, place_col_ref):
    length = ids_ref.shape[1]
    earlier = (
        lax.broadcasted_iota(jnp.int32, (length, length), 0)
        < lax.broadcasted_iota(jnp.int32, (length, length), 1)
    ).astype(F32).astype(BF16)
    same = lax.broadcasted_iota(jnp.int32, (length, length), 0) == lax.broadcasted_iota(
        jnp.int32, (length, length), 1
    )
    lower = (
        lax.broadcasted_iota(jnp.int32, (CLUSTERS, CLUSTERS), 1)
        < lax.broadcasted_iota(jnp.int32, (CLUSTERS, CLUSTERS), 0)
    ).astype(F32).astype(BF16)
    for head in range(2):
        ids = ids_ref[head : head + 1, :]
        match = (
            lax.broadcasted_iota(jnp.int32, (CLUSTERS, length), 0) == ids
        ).astype(F32)
        rank = matmul(match.astype(BF16), earlier)
        count = jnp.sum(match, axis=1, keepdims=True)
        count = jnp.broadcast_to(count, (CLUSTERS, 128))
        large = count > 20.0
        small = count < 10.0
        middle = jnp.logical_not(large | small)
        one = lambda kind: matmul(lower, kind.astype(F32).astype(BF16))
        at_large = one(large) * 32.0
        nth = one(middle)
        pair = jnp.floor(nth * 0.5)
        at_middle = 256.0 + pair * 32.0 + (nth - 2.0 * pair) * 12.0
        at_small = 256.0 + one(small) * 32.0 + 24.0
        base = jnp.where(large, at_large, jnp.where(small, at_small, at_middle))[:, :1]
        place = jnp.sum(match * (rank + base), axis=0, keepdims=True)
        place_ref[head : head + 1, :] = place.astype(jnp.int32)
        column = jnp.sum(jnp.where(same, place, 0.0), axis=1, keepdims=True)
        place_col_ref[:, head : head + 1] = column.astype(jnp.int32)


def middle_body(
    core_ref,
    tokens_ref,
    own_ref,
    left_ref,
    right_ref,
    far0_ref,
    far1_ref,
    w_own_ref,
    w_left_ref,
    w_right_ref,
    w_far_ref,
    x_own_ref,
    x_left_ref,
    x_right_ref,
    x_far_ref,
    w_qk_ref,
    w_value_ref,
    place_ref,
    hidden_ref,
    out_ref,
    far_ref,
):
    core = core_ref[0]
    far_ref[0] = far0_ref[...]
    far_ref[1] = far1_ref[...]
    left_side = []
    right_side = []
    for att, mine, other in (
        (own_ref, w_own_ref, x_own_ref),
        (left_ref, w_left_ref, x_left_ref),
        (right_ref, w_right_ref, x_right_ref),
        (far_ref, w_far_ref, x_far_ref),
    ):
        left_side += [att[core], att[1 - core]]
        right_side += [mine[...], other[...]]
    mixed = matmul(jnp.concatenate(left_side, axis=1), jnp.concatenate(right_side, axis=0))
    hidden = (tokens_ref[...].astype(F32) + mixed).astype(BF16)
    hidden_ref[...] = hidden
    normed = rms_round(hidden.astype(F32))
    qk = matmul(normed, w_qk_ref[...]).astype(BF16)
    value = matmul(normed, w_value_ref[...]).astype(BF16)
    length = qk.shape[0]
    for head in range(2):
        cols = slice(head * HEAD_DIM, (head + 1) * HEAD_DIM)
        spot = lax.broadcasted_iota(jnp.int32, (SLOTS, length), 0)
        pick = (spot == place_ref[head : head + 1, :]).astype(F32).astype(BF16)
        rows = jnp.concatenate([qk[:, cols], value[:, cols]], axis=1)
        out_ref[head] = matmul(pick, rows).astype(BF16)


def cluster_body(info_ref, mine_ref, other_ref, out_ref, keys_ref, values_ref, query_ref):
    core = info_ref[0]
    whole = info_ref[1] == 1
    rows = mine_ref.shape[0]
    lane = lax.broadcasted_iota(jnp.int32, (rows, HEAD_DIM), 1)
    row = lax.broadcasted_iota(jnp.int32, (rows, HEAD_DIM), 0) & 15

    def segment(which):
        slot = row + 16 * which
        found = jnp.where(slot >= 24, 2, jnp.where(slot >= 12, 1, 0))
        return jnp.where(whole, 0, found)

    seg_mine = segment(core)
    seg_other = segment(1 - core)
    query_ref[:, :HEAD_DIM] = mine_ref[:, :HEAD_DIM]
    query_ref[:, HEAD_DIM:] = jnp.where(lane == seg_mine, 0.0, MASKED).astype(BF16)
    for side, (source, seg) in enumerate(((mine_ref, seg_mine), (other_ref, seg_other))):
        keys_ref[side, :, :HEAD_DIM] = source[:, :HEAD_DIM]
        keys_ref[side, :, HEAD_DIM:] = jnp.where(lane == seg, 1.0, 0.0).astype(BF16)
        values_ref[side, :, :HEAD_DIM] = source[:, HEAD_DIM:]
        values_ref[side, :, HEAD_DIM:] = jnp.ones((rows, HEAD_DIM), BF16)
    tile = 256
    near_row = lax.broadcasted_iota(jnp.int32, (tile, tile), 0)
    near_col = lax.broadcasted_iota(jnp.int32, (tile, tile), 1)
    earlier = near_col < near_row
    block_row = near_row >> 4
    block_col = near_col >> 4
    earlier_other = block_col < block_row + core
    slot = (near_row & 15) + 16 * core
    opens = (slot == 0) | (jnp.logical_not(whole) & ((slot == 12) | (slot == 24)))
    alone = (near_row == near_col) & opens & (near_row < 16)
    for part in range(rows // tile):
        here = slice(part * tile, (part + 1) * tile)
        query = query_ref[here, :]
        keep = (earlier | alone) if part == 0 else earlier
        groups = []
        for side in range(2):
            if part > 0:
                past = slice(0, part * tile)
                groups.append((scores_of(query, keys_ref[side, past, :]), side, past))
            near = scores_of(query, keys_ref[side, here, :])
            near = jnp.where(keep if side == 0 else earlier_other, near, MASKED)
            groups.append((near, side, here))
        top = functools.reduce(
            jnp.maximum, [jnp.max(scores, axis=-1, keepdims=True) for scores, _, _ in groups]
        )
        mixed = jnp.zeros((tile, 2 * HEAD_DIM), F32)
        for scores, side, span in groups:
            weights = jnp.exp2((scores - top) * EXP2_FACTOR).astype(BF16)
            mixed += matmul(weights, values_ref[side, span, :])
        out_ref[here, :] = (mixed[:, :HEAD_DIM] / mixed[:, HEAD_DIM:]).astype(BF16)


def back_body(returned_ref, place_col_ref, out_ref):
    length = place_col_ref.shape[0]
    for head in range(2):
        spot = lax.broadcasted_iota(jnp.int32, (length, SLOTS), 1)
        pick = (spot == place_col_ref[:, head : head + 1]).astype(F32).astype(BF16)
        out_ref[head] = matmul(pick, returned_ref[head]).astype(BF16)


def last_body(
    own_ref, left_ref, right_ref, far0_ref, far1_ref, w_own_ref, w_left_ref, w_right_ref,
    w_far_ref, hidden_ref, out_ref,
):
    left_side = [
        own_ref[0], own_ref[1], left_ref[0], left_ref[1],
        right_ref[0], right_ref[1], far0_ref[...], far1_ref[...],
    ]
    right_side = [w_own_ref[...], w_left_ref[...], w_right_ref[...], w_far_ref[...]]
    mixed = matmul(jnp.concatenate(left_side, axis=1), jnp.concatenate(right_side, axis=0))
    out_ref[...] = hidden_ref[...].astype(F32) + mixed


def around(value, steps):
    count = lax.axis_size("narrow")
    return lax.ppermute(value, "narrow", [(i, (i + steps) % count) for i in range(count)])


def swap_cores(value):
    count = lax.axis_size("wide")
    return lax.ppermute(value, "wide", [(i, i ^ 1) for i in range(count)])


def gather_pair(value):
    left = around(value, 1)
    right = around(value, -1)
    far0 = around(left[0], 1)
    far1 = around(right[1], -1)
    return left, right, far0, far1


def shards(tokens, w_qk1, w_value1, w_out1, w_qk2, w_value2, w_out2, cluster_ids):
    length, width = tokens.shape
    shape = jax.ShapeDtypeStruct
    wide = lax.axis_index("wide")
    narrow = lax.axis_index("narrow")
    wide_count = lax.axis_size("wide")
    groups = lax.axis_size("narrow")
    core = wide % 2
    group_width = w_qk1.shape[1]

    half = lax.dynamic_slice_in_dim(w_out1, core * HEAD_DIM, HEAD_DIM, 0)
    half = half.reshape(2, HEAD_DIM // 2, width)
    w_left, w_right, w_far0, w_far1 = gather_pair(half)
    w_mine = [
        item.reshape(HEAD_DIM, width)
        for item in (half, w_left, w_right, jnp.stack([w_far0, w_far1]))
    ]

    qk1, value1, tails = call(
        front_body,
        (
            shape((length, group_width), BF16),
            shape((length, group_width), BF16),
            shape((2, WINDOW, group_width), BF16),
        ),
        (tokens, w_qk1, w_value1),
        flops=2 * length * width * group_width * 2,
        bytes_accessed=3 * 2**20,
    )
    before = lax.ppermute(tails, "wide", [(i, i + 1) for i in range(wide_count - 1)])
    place, place_col = call(
        place_body,
        (shape((2, length), jnp.int32), shape((length, 2), jnp.int32)),
        (cluster_ids,),
        flops=2**26,
        bytes_accessed=2**18,
    )
    attended1 = call(
        window_body,
        shape((2, length, HEAD_DIM), BF16),
        (wide.reshape(1), qk1, value1, before),
        prefetch=1,
        flops=2**28,
        bytes_accessed=2**20,
    )
    w_other = [swap_cores(item) for item in w_mine]
    left, right, far0, far1 = gather_pair(attended1)
    hidden, outgoing = call(
        middle_body,
        (shape((length, width), BF16), shape((2, SLOTS, 2 * HEAD_DIM), BF16)),
        (
            core.reshape(1), tokens, attended1, left, right, far0, far1,
            *w_mine, *w_other, w_qk2, w_value2, place,
        ),
        scratch=(pltpu.VMEM((2, length, HEAD_DIM), BF16),),
        prefetch=1,
        flops=2**31,
        bytes_accessed=2**23,
    )
    per_pair = 2 * SLOTS // wide_count
    arrived = lax.all_to_all(
        outgoing.reshape(wide_count, per_pair, 2 * HEAD_DIM), "wide", 0, 0, tiled=True
    ).reshape(2 * SLOTS, 2 * HEAD_DIM)
    other = swap_cores(arrived)
    info = jnp.stack([core, ((wide // 2) % 16 < 8).astype(jnp.int32)])
    rows = 2 * SLOTS
    answers = call(
        cluster_body,
        shape((rows, HEAD_DIM), BF16),
        (info, arrived, other),
        scratch=(
            pltpu.VMEM((2, rows, 2 * HEAD_DIM), BF16),
            pltpu.VMEM((2, rows, 2 * HEAD_DIM), BF16),
            pltpu.VMEM((rows, 2 * HEAD_DIM), BF16),
        ),
        prefetch=1,
        flops=2**30,
        bytes_accessed=2**21,
    )
    returned = lax.all_to_all(
        answers.reshape(wide_count, per_pair, HEAD_DIM), "wide", 0, 0, tiled=True
    ).reshape(2, SLOTS, HEAD_DIM)
    attended2 = call(
        back_body,
        shape((2, length, HEAD_DIM), BF16),
        (returned, place_col),
        flops=2**27,
        bytes_accessed=2**20,
    )
    left, right, far0, far1 = gather_pair(attended2)

    def columns_for(steps):
        target = (narrow + steps) % groups
        return lax.dynamic_slice_in_dim(w_out2, target * group_width, group_width, 1)

    w_own2 = columns_for(0)
    w_left2 = around(columns_for(1), 1)
    w_right2 = around(columns_for(-1), -1)
    w_far2 = around(columns_for(2), 2)
    hidden_own = lax.dynamic_slice_in_dim(hidden, narrow * group_width, group_width, 1)
    return call(
        last_body,
        shape((length, group_width), F32),
        (
            attended2, left, right, far0, far1, w_own2, w_left2, w_right2, w_far2, hidden_own,
        ),
        flops=2**29,
        bytes_accessed=2**21,
    )


def solution(mesh):
    placed = (
        P("wide", None),
        P(None, "narrow"),
        P(None, "narrow"),
        P("narrow", None),
        P(None, "narrow"),
        P(None, "narrow"),
        P("narrow", None),
        P("narrow", "wide"),
    )
    return jax.shard_map(
        shards, mesh=mesh, in_specs=placed, out_specs=P("wide", "narrow"), check_vma=False
    )
```

time: 228 us -> 113 us (0.50)
  waiting for transfers between devices: 104 us -> 19.8 us
  blocking collectives: 0 us -> 50.6 us
  matrix products: 29.4 us -> 0 us
  other arithmetic: 19.5 us -> 0.1 us
  between operations: 13.7 us -> 0.27 us
  local copies, waits for them, and re-layouts: 15 us -> 4.27 us
  Pallas kernels: 0 us -> 9.93 us
  starting transfers between devices: 36.9 us -> 28.1 us
  loops' own time: 8.37 us -> 0 us
    all_to_all x0 -> x2, blocking collectives: none -> 50.6 us  [the longest x1 32 us: shards(): lax.all_to_all(outgoing.reshape(wide_count, per_pair, 2 * HEAD_DIM), 'wid...]
    all_to_all x3 -> x0, waiting for transfers between devices: 44.4 us -> none  [the longest x1 26.7 us: shards(): lax.all_to_all(outgoing, 'wide', split_axis=0, concat_axis=0, tiled=True)]
    psum x1 -> x0, waiting for transfers between devices: 36.5 us -> none  [shards(): lax.psum(partial_value.astype(jnp.bfloat16), 'narrow').astype(jnp.float32)]
    all_to_all x3 -> x0, starting transfers between devices: 32.3 us -> none  [the longest x1 13.6 us: shards(): lax.all_to_all(sent, 'wide', split_axis=0, concat_axis=0, tiled=True)]
    dot_general x16 -> x0, matrix products: 29.4 us -> none  [the longest x4 12.7 us: owner_softmax(): lax.dot_general(query_rows, key_rows, (((1,), (1,)), ((), ())), preferred...]
    ppermute x1 -> x21, starting transfers between devices: 4.59 us -> 28.1 us  [the longest x15 21.7 us: around(): lax.ppermute(value, 'narrow', [(i, (i + steps) % count) for i in range(co...]
    reduce_scatter x1 -> x0, waiting for transfers between devices: 20.7 us -> none  [shards(): lax.psum_scatter(partial2.astype(jnp.bfloat16), 'narrow', scatter_dimensi...]
    ppermute x1 -> x21, waiting for transfers between devices: 2.34 us -> 19.8 us  [the longest x15 17.6 us: around(): lax.ppermute(value, 'narrow', [(i, (i + steps) % count) for i in range(co...]
  transfers between devices with their start and end apart: 6 -> 21, of which waited for: 5 -> 9; matrix products, arithmetic and copies ran while one was open for 8% -> 1% of each run, Pallas kernels for 0% -> 1%
where the time goes in v1:
time: 113 us
  blocking collectives  50.6 us (45%)
  starting transfers between devices  28.1 us (25%)
  waiting for transfers between devices  19.8 us (18%)
  Pallas kernels  9.93 us (9%)
  local copies, waits for them, and re-layouts  4.27 us (4%)
    all_to_all x1, blocking collectives, shards(): lax.all_to_all(outgoing.reshape(wide_count, per_pair, 2 * HEAD_DIM), 'wid...  32 us
    ppermute x15, starting transfers between devices, around(): lax.ppermute(value, 'narrow', [(i, (i + steps) % count) for i in range(co...  21.7 us
    all_to_all x1, blocking collectives, shards(): lax.all_to_all(answers.reshape(wide_count, per_pair, HEAD_DIM), 'wide', 0...  18.7 us
    ppermute x15, waiting for transfers between devices, around(): lax.ppermute(value, 'narrow', [(i, (i + steps) % count) for i in range(co...  17.6 us
    pallas_call x7, Pallas kernels, call(): pl.pallas_call(body, out_shape=outs, in_specs=whole, out_specs=jax.tree.m...  9.93 us
    ppermute x1, starting transfers between devices, shards(): lax.ppermute(tails, 'wide', [(i, i + 1) for i in range(wide_count - 1)])  4.6 us
    unnamed x18, local copies, waits for them, and re-layouts  3.39 us
  transfers between devices with their start and end apart: 21, of which 9 were waited for; matrix products, arithmetic and copies ran while one was open for 1% of the time, Pallas kernels for 1%

profile of v1, /device:TPU:1, one launch (start us, length us, event | category | flops | bytes accessed | tf_op | source)
XLA Modules:
  0.0 113.1 jit_solution(492659835721809292)
XLA Ops:
  0.0 1.3 %copy-done.1 = bf16[512,1024]{1,0:T(8,128)(2,1)S(1)} copy-done((bf16[512,1024]{1,0:T(8,128)(2,1)S(1)}, bf16[512,1024]{1,0:T(8,128)(2,1)}, u32[]{:S(2)}) %copy-start.1) | copy-done | bytes 1048600
  1.3 1.0 copy-done.3
  2.3 1.0 copy-done.4
  3.4 0.8 shard_map.82
  4.2 4.6 %collective-permute-start = (bf16[2,256,256]{2,1,0:T(8,128)(2,1)S(1)}, bf16[2,256,256]{2,1,0:T(8,128)(2,1)S(1)}, u32[]{:S(2)}, u32[]{:S(2)}) collective-permute-start(bf16[2,256,256]{2,1,0:T(8,128)(2,1)S(1)} %get-tuple-element.14), channel_id=1, source_target_pairs={{0,4},{4,8},{8,12},{12,16},{16,20},{20,24},{24,28},{28,32},{32,36}... | collective-permute-start | bytes 786440 | tf_op jit(solution)/shard_map/ppermute | solution.py:301
  8.9 2.6 %collective-permute-start.6 = (bf16[2,64,1024]{2,1,0:T(8,128)(2,1)S(1)}, bf16[2,64,1024]{2,1,0:T(8,128)(2,1)S(1)}, u32[]{:S(2)}, u32[]{:S(2)}) collective-permute-start(bf16[2,64,1024]{2,1,0:T(8,128)(2,1)S(1)} %bitcast.29), channel_id=1, source_target_pairs={{0,3},{1,0},{2,1},{3,2},{4,7},{5,4},{6,5},{7,6},{8,11},{9,8},{10,9... | collective-permute-start | bytes 786440 | tf_op jit(solution)/shard_map/ppermute | solution.py:256
  11.5 0.0 collective-permute-start.5
  11.5 0.7 collective-permute-done.before_ref
  12.1 1.0 shard_map.83.own_ref
  13.1 0.0 copy-start.2
  13.1 1.3 %collective-permute-start.1 = (bf16[2,512,128]{2,1,0:T(8,128)(2,1)S(1)}, bf16[2,512,128]{2,1,0:T(8,128)(2,1)S(1)}, u32[]{:S(2)}, u32[]{:S(2)}) collective-permute-start(bf16[2,512,128]{2,1,0:T(8,128)(2,1)S(1)} %shard_map.83.own_ref), channel_id=1, source_target_pairs={{0,1},{1,2},{2,3},{3,0},{4,5},{5,6},{6,7},{7,4},{8,9},{9,10},{10,1... | collective-permute-start | bytes 786440 | tf_op jit(solution)/shard_map/ppermute | solution.py:256
  14.4 2.5 %collective-permute-done.6 = bf16[2,64,1024]{2,1,0:T(8,128)(2,1)S(1)} collective-permute-done((bf16[2,64,1024]{2,1,0:T(8,128)(2,1)S(1)}, bf16[2,64,1024]{2,1,0:T(8,128)(2,1)S(1)}, u32[]{:S(2)}, u32[]{:S(2)}) %collective-permute-start.6) | collective-permute-done | bytes 262176 | tf_op jit(solution)/shard_map/ppermute | solution.py:256
  17.0 2.9 %collective-permute-start.8 = (bf16[64,1024]{1,0:T(8,128)(2,1)S(1)}, bf16[64,1024]{1,0:T(8,128)(2,1)S(1)}, u32[]{:S(2)}, u32[]{:S(2)}) collective-permute-start(bf16[64,1024]{1,0:T(8,128)(2,1)S(1)} %slice_bitcast_fusion.2), channel_id=1, source_target_pairs={{0,3},{1,0},{2,1},{3,2},{4,7},{5,4},{6,5},{7,6},{8,11},{9,8},{10,9... | collective-permute-start | bytes 393224 | tf_op jit(solution)/shard_map/ppermute | solution.py:256
  19.9 1.0 collective-permute-done.5
  20.9 0.1 collective-permute-start.7
  21.0 0.1 collective-permute-start.9
  21.1 2.6 %collective-permute-start.2 = (bf16[2,512,128]{2,1,0:T(8,128)(2,1)S(1)}, bf16[2,512,128]{2,1,0:T(8,128)(2,1)S(1)}, u32[]{:S(2)}, u32[]{:S(2)}) collective-permute-start(bf16[2,512,128]{2,1,0:T(8,128)(2,1)S(1)} %shard_map.83.own_ref), channel_id=1, source_target_pairs={{0,3},{1,0},{2,1},{3,2},{4,7},{5,4},{6,5},{7,6},{8,11},{9,8},{10,9... | collective-permute-start | bytes 786440 | tf_op jit(solution)/shard_map/ppermute | solution.py:256
  23.7 0.8 collective-permute-start.10
  24.5 4.0 %collective-permute-done.7 = bf16[64,1024]{1,0:T(8,128)(2,1)S(1)} collective-permute-done((bf16[64,1024]{1,0:T(8,128)(2,1)S(1)}, bf16[64,1024]{1,0:T(8,128)(2,1)S(1)}, u32[]{:S(2)}, u32[]{:S(2)}) %collective-permute-start.7) | collective-permute-done | bytes 131104 | tf_op jit(solution)/shard_map/ppermute | solution.py:256
  28.5 0.2 collective-permute-start.11
  28.7 0.0 collective-permute-done.1.left_ref
  28.7 0.4 collective-permute-start.12
  29.2 0.0 copy-start.7
  29.2 0.0 collective-permute-done.2.right_ref
  29.2 0.1 collective-permute-start.3
  29.3 0.0 collective-permute-done.9.x_own_ref
  29.3 3.2 %collective-permute-start.4 = (bf16[512,128]{1,0:T(8,128)(2,1)S(1)}, bf16[512,128]{1,0:T(8,128)(2,1)S(1)}, u32[]{:S(2)}, u32[]{:S(2)}) collective-permute-start(bf16[512,128]{1,0:T(8,128)(2,1)S(1)} %slice_bitcast_fusion.4), channel_id=1, source_target_pairs={{0,3},{1,0},{2,1},{3,2},{4,7},{5,4},{6,5},{7,6},{8,11},{9,8},{10,9... | collective-permute-start | bytes 393224 | tf_op jit(solution)/shard_map/ppermute | solution.py:256
  32.6 0.5 shard_map.84
  33.1 1.5 %collective-permute-done.3.far0_ref = bf16[512,128]{1,0:T(8,128)(2,1)S(1)} collective-permute-done((bf16[512,128]{1,0:T(8,128)(2,1)S(1)}, bf16[512,128]{1,0:T(8,128)(2,1)S(1)}, u32[]{:S(2)}, u32[]{:S(2)}) %collective-permute-start.3) | collective-permute-done | bytes 131104 | tf_op jit(solution)/shard_map/ppermute | solution.py:256
  34.7 2.4 %shard_map.85 = (bf16[512,1024]{1,0:T(8,128)(2,1)S(1)}, bf16[2,512,256]{2,1,0:T(8,128)(2,1)S(1)}) custom-call(s32[1]{0:T(128)} %bitcast.core_ref, bf16[512,1024]{1,0:T(8,128)(2,1)S(1)} %copy-done.2, bf16[2,512,128]{2,1,0:T(8,128)(2,1)S(1)} %shard_map.83.own_ref, bf16[2,512,128]{2,1,0:T(8,128)(2,1)S(1)} %collective-permute-done.1.left_ref, ...), custom_call_target="tpu_custom_call" | custom-call | flops 2147483648 | bytes 8388608 | tf_op jit(solution)/shard_map/pallas_call | solution.py:26
  37.1 32.0 %all_to_all.10 = bf16[64,16,256]{2,1,0:T(8,128)(2,1)S(1)} all-to-all(bf16[64,16,256]{2,1,0:T(8,128)(2,1)S(1)} %bitcast.28), channel_id=1, replica_groups=mesh['wide'=64,'narrow'=4] {'wide'}, dimensions={0} | all-to-all | bytes 1048576 | tf_op jit(solution)/shard_map/all_to_all | solution.py:332
  69.1 0.4 collective-permute-start.13
  69.5 0.1 pad_add_fusion.info_ref
  69.5 1.5 %collective-permute-done.13.other_ref = bf16[1024,256]{1,0:T(8,128)(2,1)S(1)} collective-permute-done((bf16[1024,256]{1,0:T(8,128)(2,1)S(1)}, bf16[1024,256]{1,0:T(8,128)(2,1)S(1)}, u32[]{:S(2)}, u32[]{:S(2)}) %collective-permute-start.13) | collective-permute-done | bytes 524320 | tf_op jit(solution)/shard_map/ppermute | solution.py:261
  71.0 3.4 %shard_map.86 = bf16[1024,128]{1,0:T(8,128)(2,1)S(1)} custom-call(s32[2]{0:T(128)S(1)} %pad_add_fusion.info_ref, bf16[1024,256]{1,0:T(8,128)(2,1)S(1)} %bitcast.27, bf16[1024,256]{1,0:T(8,128)(2,1)S(1)} %collective-permute-done.13.other_ref), custom_call_target="tpu_custom_call" | custom-call | flops 1073741824 | bytes 2097152 | tf_op jit(solution)/shard_map/pallas_call | solution.py:26
  74.4 18.7 %all_to_all.11 = bf16[64,16,128]{2,1,0:T(8,128)(2,1)S(1)} all-to-all(bf16[64,16,128]{2,1,0:T(8,128)(2,1)S(1)} %bitcast.33), channel_id=1, replica_groups=mesh['wide'=64,'narrow'=4] {'wide'}, dimensions={0} | all-to-all | bytes 524288 | tf_op jit(solution)/shard_map/all_to_all | solution.py:351
  93.0 0.5 shard_map.87.own_ref
  93.6 1.2 %collective-permute-start.14 = (bf16[2,512,128]{2,1,0:T(8,128)(2,1)S(1)}, bf16[2,512,128]{2,1,0:T(8,128)(2,1)S(1)}, u32[]{:S(2)}, u32[]{:S(2)}) collective-permute-start(bf16[2,512,128]{2,1,0:T(8,128)(2,1)S(1)} %shard_map.87.own_ref), channel_id=1, source_target_pairs={{0,1},{1,2},{2,3},{3,0},{4,5},{5,6},{6,7},{7,4},{8,9},{9,10},{10,1... | collective-permute-start | bytes 786440 | tf_op jit(solution)/shard_map/ppermute | solution.py:256
  94.8 2.0 %collective-permute-start.15 = (bf16[2,512,128]{2,1,0:T(8,128)(2,1)S(1)}, bf16[2,512,128]{2,1,0:T(8,128)(2,1)S(1)}, u32[]{:S(2)}, u32[]{:S(2)}) collective-permute-start(bf16[2,512,128]{2,1,0:T(8,128)(2,1)S(1)} %shard_map.87.own_ref), channel_id=1, source_target_pairs={{0,3},{1,0},{2,1},{3,2},{4,7},{5,4},{6,5},{7,6},{8,11},{9,8},{10,9... | collective-permute-start | bytes 786440 | tf_op jit(solution)/shard_map/ppermute | solution.py:256
  96.7 0.8 constant_dynamic-slice_fusion.1
  97.5 2.7 %collective-permute-start.19 = (bf16[256,256]{1,0:T(8,128)(2,1)}, bf16[256,256]{1,0:T(8,128)(2,1)S(1)}, u32[]{:S(2)}, u32[]{:S(2)}) collective-permute-start(bf16[256,256]{1,0:T(8,128)(2,1)} %get-tuple-element.22), channel_id=1, source_target_pairs={{0,3},{1,0},{2,1},{3,2},{4,7},{5,4},{6,5},{7,6},{8,11},{9,8},{10,9... | collective-permute-start | bytes 393224 | tf_op jit(solution)/shard_map/ppermute | solution.py:256
  100.2 0.3 collective-permute-start.20
  100.5 2.6 %collective-permute-done.14.left_ref = bf16[2,512,128]{2,1,0:T(8,128)(2,1)S(1)} collective-permute-done((bf16[2,512,128]{2,1,0:T(8,128)(2,1)S(1)}, bf16[2,512,128]{2,1,0:T(8,128)(2,1)S(1)}, u32[]{:S(2)}, u32[]{:S(2)}) %collective-permute-start.14) | collective-permute-done | bytes 262176 | tf_op jit(solution)/shard_map/ppermute | solution.py:256
  103.1 0.1 collective-permute-start.16
  103.2 2.7 %collective-permute-start.17 = (bf16[512,128]{1,0:T(8,128)(2,1)S(1)}, bf16[512,128]{1,0:T(8,128)(2,1)S(1)}, u32[]{:S(2)}, u32[]{:S(2)}) collective-permute-start(bf16[512,128]{1,0:T(8,128)(2,1)S(1)} %slice_bitcast_fusion), channel_id=1, source_target_pairs={{0,3},{1,0},{2,1},{3,2},{4,7},{5,4},{6,5},{7,6},{8,11},{9,8},{10,9... | collective-permute-start | bytes 393224 | tf_op jit(solution)/shard_map/ppermute | solution.py:256
  106.0 3.6 %collective-permute-done.20.w_far_ref = bf16[256,256]{1,0:T(8,128)(2,1)S(1)} collective-permute-done((bf16[256,256]{1,0:T(8,128)(2,1)S(1)}, bf16[256,256]{1,0:T(8,128)(2,1)S(1)}, u32[]{:S(2)}, u32[]{:S(2)}) %collective-permute-start.20) | collective-permute-done | bytes 131104 | tf_op jit(solution)/shard_map/ppermute | solution.py:256
  109.6 2.3 %collective-permute-done.16.far0_ref = bf16[512,128]{1,0:T(8,128)(2,1)S(1)} collective-permute-done((bf16[512,128]{1,0:T(8,128)(2,1)S(1)}, bf16[512,128]{1,0:T(8,128)(2,1)S(1)}, u32[]{:S(2)}, u32[]{:S(2)}) %collective-permute-start.16) | collective-permute-done | bytes 131104 | tf_op jit(solution)/shard_map/ppermute | solution.py:256
  111.9 1.2 %shard_map.88 = f32[512,256]{1,0:T(8,128)} custom-call(bf16[2,512,128]{2,1,0:T(8,128)(2,1)S(1)} %shard_map.87.own_ref, bf16[2,512,128]{2,1,0:T(8,128)(2,1)S(1)} %collective-permute-done.14.left_ref, bf16[2,512,128]{2,1,0:T(8,128)(2,1)S(1)} %collective-permute-done.15.right_ref, bf16[512,128]{1,0:T(8,128)(2,1)S(1)} %collective-permute-done.16.far0_ref, ...), custom_call_target="tpu_custom_call" | custom-call | flops 536870912 | bytes 2097152 | tf_op jit(solution)/shard_map/pallas_call | solution.py:26
  (32 shorter events, 0.2 us)
Async XLA Ops:
  0.0 8.9 %copy-start = (bf16[256,1024]{1,0:T(8,128)(2,1)S(1)}, bf16[256,1024]{1,0:T(8,128)(2,1)}, u32[]{:S(2)}) copy-start(bf16[256,1024]{1,0:T(8,128)(2,1)} %param.11) | copy-start | bytes 1572868
  0.0 1.3 %copy-start.1 = (bf16[512,1024]{1,0:T(8,128)(2,1)S(1)}, bf16[512,1024]{1,0:T(8,128)(2,1)}, u32[]{:S(2)}) copy-start(bf16[512,1024]{1,0:T(8,128)(2,1)} %tokens_ref.3) | copy-start | bytes 3145732
  1.3 1.0 copy-start.3
  2.3 1.0 copy-start.4
  4.2 7.9 %collective-permute-start = (bf16[2,256,256]{2,1,0:T(8,128)(2,1)S(1)}, bf16[2,256,256]{2,1,0:T(8,128)(2,1)S(1)}, u32[]{:S(2)}, u32[]{:S(2)}) collective-permute-start(bf16[2,256,256]{2,1,0:T(8,128)(2,1)S(1)} %get-tuple-element.14), channel_id=1, source_target_pairs={{0,4},{4,8},{8,12},{12,16},{16,20},{20,24},{24,28},{28,32},{32,36}... | collective-permute-start | bytes 786440 | tf_op jit(solution)/shard_map/ppermute | solution.py:301
  8.9 8.1 %collective-permute-start.6 = (bf16[2,64,1024]{2,1,0:T(8,128)(2,1)S(1)}, bf16[2,64,1024]{2,1,0:T(8,128)(2,1)S(1)}, u32[]{:S(2)}, u32[]{:S(2)}) collective-permute-start(bf16[2,64,1024]{2,1,0:T(8,128)(2,1)S(1)} %bitcast.29), channel_id=1, source_target_pairs={{0,3},{1,0},{2,1},{3,2},{4,7},{5,4},{6,5},{7,6},{8,11},{9,8},{10,9... | collective-permute-start | bytes 786440 | tf_op jit(solution)/shard_map/ppermute | solution.py:256
  11.5 9.5 %collective-permute-start.5 = (bf16[2,64,1024]{2,1,0:T(8,128)(2,1)S(1)}, bf16[2,64,1024]{2,1,0:T(8,128)(2,1)S(1)}, u32[]{:S(2)}, u32[]{:S(2)}) collective-permute-start(bf16[2,64,1024]{2,1,0:T(8,128)(2,1)S(1)} %bitcast.30), channel_id=1, source_target_pairs={{0,1},{1,2},{2,3},{3,0},{4,5},{5,6},{6,7},{7,4},{8,9},{9,10},{10,1... | collective-permute-start | bytes 786440 | tf_op jit(solution)/shard_map/ppermute | solution.py:256
  12.1 22.5 %copy-start.6 = (bf16[1024,256]{1,0:T(8,128)(2,1)S(1)}, bf16[1024,256]{1,0:T(8,128)(2,1)}, u32[]{:S(2)}) copy-start(bf16[1024,256]{1,0:T(8,128)(2,1)} %w_value_ref.3) | copy-start | bytes 1572868
  13.1 21.5 %copy-start.2 = (bf16[512,1024]{1,0:T(8,128)(2,1)S(1)}, bf16[512,1024]{1,0:T(8,128)(2,1)}, u32[]{:S(2)}) copy-start(bf16[512,1024]{1,0:T(8,128)(2,1)} %tokens_ref.3) | copy-start | bytes 3145732
  13.1 15.6 %collective-permute-start.1 = (bf16[2,512,128]{2,1,0:T(8,128)(2,1)S(1)}, bf16[2,512,128]{2,1,0:T(8,128)(2,1)S(1)}, u32[]{:S(2)}, u32[]{:S(2)}) collective-permute-start(bf16[2,512,128]{2,1,0:T(8,128)(2,1)S(1)} %shard_map.83.own_ref), channel_id=1, source_target_pairs={{0,1},{1,2},{2,3},{3,0},{4,5},{5,6},{6,7},{7,4},{8,9},{9,10},{10,1... | collective-permute-start | bytes 786440 | tf_op jit(solution)/shard_map/ppermute | solution.py:256
  17.0 6.7 %collective-permute-start.8 = (bf16[64,1024]{1,0:T(8,128)(2,1)S(1)}, bf16[64,1024]{1,0:T(8,128)(2,1)S(1)}, u32[]{:S(2)}, u32[]{:S(2)}) collective-permute-start(bf16[64,1024]{1,0:T(8,128)(2,1)S(1)} %slice_bitcast_fusion.2), channel_id=1, source_target_pairs={{0,3},{1,0},{2,1},{3,2},{4,7},{5,4},{6,5},{7,6},{8,11},{9,8},{10,9... | collective-permute-start | bytes 393224 | tf_op jit(solution)/shard_map/ppermute | solution.py:256
  20.9 7.6 %collective-permute-start.7 = (bf16[64,1024]{1,0:T(8,128)(2,1)S(1)}, bf16[64,1024]{1,0:T(8,128)(2,1)S(1)}, u32[]{:S(2)}, u32[]{:S(2)}) collective-permute-start(bf16[64,1024]{1,0:T(8,128)(2,1)S(1)} %slice_bitcast_fusion.3), channel_id=1, source_target_pairs={{0,1},{1,2},{2,3},{3,0},{4,5},{5,6},{6,7},{7,4},{8,9},{9,10},{10,1... | collective-permute-start | bytes 393224 | tf_op jit(solution)/shard_map/ppermute | solution.py:256
  21.0 8.3 %collective-permute-start.9 = (bf16[128,1024]{1,0:T(8,128)(2,1)S(1)}, bf16[128,1024]{1,0:T(8,128)(2,1)S(1)}, u32[]{:S(2)}, u32[]{:S(2)}) collective-permute-start(bf16[128,1024]{1,0:T(8,128)(2,1)S(1)} %constant_dynamic-slice_fusion.5.w_own_ref), channel_id=1, source_target_pairs={{0,4},{4,0},{8,12},{12,8},{16,20},{20,16},{24,28},{28,24},{32,36},... | collective-permute-start | bytes 786440 | tf_op jit(solution)/shard_map/ppermute | solution.py:261
  21.1 8.1 %collective-permute-start.2 = (bf16[2,512,128]{2,1,0:T(8,128)(2,1)S(1)}, bf16[2,512,128]{2,1,0:T(8,128)(2,1)S(1)}, u32[]{:S(2)}, u32[]{:S(2)}) collective-permute-start(bf16[2,512,128]{2,1,0:T(8,128)(2,1)S(1)} %shard_map.83.own_ref), channel_id=1, source_target_pairs={{0,3},{1,0},{2,1},{3,2},{4,7},{5,4},{6,5},{7,6},{8,11},{9,8},{10,9... | collective-permute-start | bytes 786440 | tf_op jit(solution)/shard_map/ppermute | solution.py:256
  23.7 9.4 %collective-permute-start.10 = (bf16[128,1024]{1,0:T(8,128)(2,1)S(1)}, bf16[128,1024]{1,0:T(8,128)(2,1)S(1)}, u32[]{:S(2)}, u32[]{:S(2)}) collective-permute-start(bf16[128,1024]{1,0:T(8,128)(2,1)S(1)} %bitcast.36), channel_id=1, source_target_pairs={{0,4},{4,0},{8,12},{12,8},{16,20},{20,16},{24,28},{28,24},{32,36},... | collective-permute-start | bytes 786440 | tf_op jit(solution)/shard_map/ppermute | solution.py:261
  28.5 4.6 %collective-permute-start.11 = (bf16[128,1024]{1,0:T(8,128)(2,1)S(1)}, bf16[128,1024]{1,0:T(8,128)(2,1)S(1)}, u32[]{:S(2)}, u32[]{:S(2)}) collective-permute-start(bf16[128,1024]{1,0:T(8,128)(2,1)S(1)} %bitcast.34), channel_id=1, source_target_pairs={{0,4},{4,0},{8,12},{12,8},{16,20},{20,16},{24,28},{28,24},{32,36},... | collective-permute-start | bytes 786440 | tf_op jit(solution)/shard_map/ppermute | solution.py:261
  28.7 6.0 %copy-start.5 = (bf16[1024,256]{1,0:T(8,128)(2,1)S(1)}, bf16[1024,256]{1,0:T(8,128)(2,1)}, u32[]{:S(2)}) copy-start(bf16[1024,256]{1,0:T(8,128)(2,1)} %w_qk_ref.3) | copy-start | bytes 1572868
  28.7 5.9 %collective-permute-start.12 = (bf16[128,1024]{1,0:T(8,128)(2,1)S(1)}, bf16[128,1024]{1,0:T(8,128)(2,1)S(1)}, u32[]{:S(2)}, u32[]{:S(2)}) collective-permute-start(bf16[128,1024]{1,0:T(8,128)(2,1)S(1)} %bitcast.31), channel_id=1, source_target_pairs={{0,4},{4,0},{8,12},{12,8},{16,20},{20,16},{24,28},{28,24},{32,36},... | collective-permute-start | bytes 786440 | tf_op jit(solution)/shard_map/ppermute | solution.py:261
  29.2 3.4 %copy-start.7 = (s32[2,512]{1,0:T(2,128)S(1)}, s32[2,512]{1,0:T(2,128)}, u32[]{:S(2)}) copy-start(s32[2,512]{1,0:T(2,128)} %ids_ref.1) | copy-start | bytes 12292
  29.2 5.4 %collective-permute-start.3 = (bf16[512,128]{1,0:T(8,128)(2,1)S(1)}, bf16[512,128]{1,0:T(8,128)(2,1)S(1)}, u32[]{:S(2)}, u32[]{:S(2)}) collective-permute-start(bf16[512,128]{1,0:T(8,128)(2,1)S(1)} %slice_bitcast_fusion.5), channel_id=1, source_target_pairs={{0,1},{1,2},{2,3},{3,0},{4,5},{5,6},{6,7},{7,4},{8,9},{9,10},{10,1... | collective-permute-start | bytes 393224 | tf_op jit(solution)/shard_map/ppermute | solution.py:256
  29.3 5.3 %collective-permute-start.4 = (bf16[512,128]{1,0:T(8,128)(2,1)S(1)}, bf16[512,128]{1,0:T(8,128)(2,1)S(1)}, u32[]{:S(2)}, u32[]{:S(2)}) collective-permute-start(bf16[512,128]{1,0:T(8,128)(2,1)S(1)} %slice_bitcast_fusion.4), channel_id=1, source_target_pairs={{0,3},{1,0},{2,1},{3,2},{4,7},{5,4},{6,5},{7,6},{8,11},{9,8},{10,9... | collective-permute-start | bytes 393224 | tf_op jit(solution)/shard_map/ppermute | solution.py:256
  69.1 1.9 %collective-permute-start.13 = (bf16[1024,256]{1,0:T(8,128)(2,1)S(1)}, bf16[1024,256]{1,0:T(8,128)(2,1)S(1)}, u32[]{:S(2)}, u32[]{:S(2)}) collective-permute-start(bf16[1024,256]{1,0:T(8,128)(2,1)S(1)} %bitcast.26), channel_id=1, source_target_pairs={{0,4},{4,0},{8,12},{12,8},{16,20},{20,16},{24,28},{28,24},{32,36},... | collective-permute-start | bytes 1572872 | tf_op jit(solution)/shard_map/ppermute | solution.py:261
  93.0 3.7 %copy-start.8 = (bf16[256,1024]{1,0:T(8,128)(2,1)S(1)}, bf16[256,1024]{1,0:T(8,128)(2,1)}, u32[]{:S(2)}) copy-start(bf16[256,1024]{1,0:T(8,128)(2,1)} %param.14) | copy-start | bytes 1572868
  93.6 9.5 %collective-permute-start.14 = (bf16[2,512,128]{2,1,0:T(8,128)(2,1)S(1)}, bf16[2,512,128]{2,1,0:T(8,128)(2,1)S(1)}, u32[]{:S(2)}, u32[]{:S(2)}) collective-permute-start(bf16[2,512,128]{2,1,0:T(8,128)(2,1)S(1)} %shard_map.87.own_ref), channel_id=1, source_target_pairs={{0,1},{1,2},{2,3},{3,0},{4,5},{5,6},{6,7},{7,4},{8,9},{9,10},{10,1... | collective-permute-start | bytes 786440 | tf_op jit(solution)/shard_map/ppermute | solution.py:256
  94.8 8.4 %collective-permute-start.15 = (bf16[2,512,128]{2,1,0:T(8,128)(2,1)S(1)}, bf16[2,512,128]{2,1,0:T(8,128)(2,1)S(1)}, u32[]{:S(2)}, u32[]{:S(2)}) collective-permute-start(bf16[2,512,128]{2,1,0:T(8,128)(2,1)S(1)} %shard_map.87.own_ref), channel_id=1, source_target_pairs={{0,3},{1,0},{2,1},{3,2},{4,7},{5,4},{6,5},{7,6},{8,11},{9,8},{10,9... | collective-permute-start | bytes 786440 | tf_op jit(solution)/shard_map/ppermute | solution.py:256
  97.5 8.5 %collective-permute-start.18 = (bf16[256,256]{1,0:T(8,128)(2,1)}, bf16[256,256]{1,0:T(8,128)(2,1)S(1)}, u32[]{:S(2)}, u32[]{:S(2)}) collective-permute-start(bf16[256,256]{1,0:T(8,128)(2,1)} %get-tuple-element.20), channel_id=1, source_target_pairs={{0,1},{1,2},{2,3},{3,0},{4,5},{5,6},{6,7},{7,4},{8,9},{9,10},{10,1... | collective-permute-start | bytes 393224 | tf_op jit(solution)/shard_map/ppermute | solution.py:256
  97.5 8.5 %collective-permute-start.19 = (bf16[256,256]{1,0:T(8,128)(2,1)}, bf16[256,256]{1,0:T(8,128)(2,1)S(1)}, u32[]{:S(2)}, u32[]{:S(2)}) collective-permute-start(bf16[256,256]{1,0:T(8,128)(2,1)} %get-tuple-element.22), channel_id=1, source_target_pairs={{0,3},{1,0},{2,1},{3,2},{4,7},{5,4},{6,5},{7,6},{8,11},{9,8},{10,9... | collective-permute-start | bytes 393224 | tf_op jit(solution)/shard_map/ppermute | solution.py:256
  100.2 9.4 %collective-permute-start.20 = (bf16[256,256]{1,0:T(8,128)(2,1)S(1)}, bf16[256,256]{1,0:T(8,128)(2,1)S(1)}, u32[]{:S(2)}, u32[]{:S(2)}) collective-permute-start(bf16[256,256]{1,0:T(8,128)(2,1)S(1)} %get-tuple-element.19), channel_id=1, source_target_pairs={{0,2},{1,3},{2,0},{3,1},{4,6},{5,7},{6,4},{7,5},{8,10},{9,11},{10,... | collective-permute-start | bytes 393224 | tf_op jit(solution)/shard_map/ppermute | solution.py:256
  103.1 8.8 %collective-permute-start.16 = (bf16[512,128]{1,0:T(8,128)(2,1)S(1)}, bf16[512,128]{1,0:T(8,128)(2,1)S(1)}, u32[]{:S(2)}, u32[]{:S(2)}) collective-permute-start(bf16[512,128]{1,0:T(8,128)(2,1)S(1)} %slice_bitcast_fusion.1), channel_id=1, source_target_pairs={{0,1},{1,2},{2,3},{3,0},{4,5},{5,6},{6,7},{7,4},{8,9},{9,10},{10,1... | collective-permute-start | bytes 393224 | tf_op jit(solution)/shard_map/ppermute | solution.py:256
  103.2 8.7 %collective-permute-start.17 = (bf16[512,128]{1,0:T(8,128)(2,1)S(1)}, bf16[512,128]{1,0:T(8,128)(2,1)S(1)}, u32[]{:S(2)}, u32[]{:S(2)}) collective-permute-start(bf16[512,128]{1,0:T(8,128)(2,1)S(1)} %slice_bitcast_fusion), channel_id=1, source_target_pairs={{0,3},{1,0},{2,1},{3,2},{4,7},{5,4},{6,5},{7,6},{8,11},{9,8},{10,9... | collective-permute-start | bytes 393224 | tf_op jit(solution)/shard_map/ppermute | solution.py:256

commit v2 on v1

--- a/solution.py
+++ b/solution.py
@@ -19,9 +19,12 @@
 F32 = jnp.float32
 
 
-def call(body, outs, args, scratch=(), prefetch=0, flops=0, bytes_accessed=0):
+def call(
+    body, outs, args, scratch=(), prefetch=0, flops=0, bytes_accessed=0, space=pltpu.VMEM,
+    mib=20,
+):
     whole = [pl.BlockSpec(memory_space=pltpu.SMEM)] * prefetch + [
-        pl.BlockSpec(memory_space=pltpu.VMEM)
+        pl.BlockSpec(memory_space=space)
     ] * (len(args) - prefetch)
     return pl.pallas_call(
         body,
@@ -29,7 +32,7 @@
         in_specs=whole,
         out_specs=jax.tree.map(lambda _: pl.BlockSpec(memory_space=pltpu.VMEM), outs),
         scratch_shapes=list(scratch),
-        compiler_params=pltpu.CompilerParams(vmem_limit_bytes=40 * 2**20),
+        compiler_params=pltpu.CompilerParams(vmem_limit_bytes=mib * 2**20),
         cost_estimate=pl.CostEstimate(
             flops=flops, bytes_accessed=bytes_accessed, transcendentals=0
         ),
@@ -49,15 +52,36 @@
     return lax.dot_general(query, keys, (((1,), (1,)), ((), ())), preferred_element_type=F32)
 
 
-def front_body(tokens_ref, w_qk_ref, w_value_ref, qk_ref, value_ref, tail_ref):
-    normed = rms_round(tokens_ref[...].astype(F32))
-    qk = matmul(normed, w_qk_ref[...]).astype(BF16)
-    value = matmul(normed, w_value_ref[...]).astype(BF16)
-    length = qk.shape[0]
-    qk_ref[...] = qk
-    value_ref[...] = value
-    tail_ref[0] = qk[length - WINDOW :]
-    tail_ref[1] = value[length - WINDOW :]
+def front_body(
+    tokens_any, w_qk_any, w_value_any, qk_ref, value_ref, tail_ref,
+    tokens_ref, w_qk_ref, w_value_ref, sems,
+):
+    length = tokens_ref.shape[0]
+    parts = 2
+    step = length // parts
+    spans = [slice(part * step, (part + 1) * step) for part in range(parts)]
+    token_copies = [
+        pltpu.make_async_copy(tokens_any.at[span], tokens_ref.at[span], sems.at[2 + part])
+        for part, span in enumerate(spans)
+    ]
+    qk_copy = pltpu.make_async_copy(w_qk_any, w_qk_ref, sems.at[0])
+    value_copy = pltpu.make_async_copy(w_value_any, w_value_ref, sems.at[1])
+    for copy in (token_copies[0], qk_copy, value_copy, *token_copies[1:]):
+        copy.start()
+    for part, span in enumerate(spans):
+        token_copies[part].wait()
+        normed = rms_round(tokens_ref[span].astype(F32))
+        if part == 0:
+            qk_copy.wait()
+        qk = matmul(normed, w_qk_ref[...]).astype(BF16)
+        if part == 0:
+            value_copy.wait()
+        value = matmul(normed, w_value_ref[...]).astype(BF16)
+        qk_ref[span] = qk
+        value_ref[span] = value
+        if part == parts - 1:
+            tail_ref[0] = qk[step - WINDOW :]
+            tail_ref[1] = value[step - WINDOW :]
 
 
 def window_body(first_ref, qk_ref, value_ref, before_ref, out_ref):
@@ -84,12 +108,27 @@
             top = jnp.max(scores, axis=-1, keepdims=True)
             weights = jnp.exp2((scores - top) * EXP2_FACTOR).astype(BF16)
             mixed = matmul(weights, jnp.concatenate([values, ones], axis=1))
-            out_ref[head, part * tile : (part + 1) * tile] = (
+            out_ref[part * tile : (part + 1) * tile, cols] = (
                 mixed[:, :HEAD_DIM] / mixed[:, HEAD_DIM:]
             ).astype(BF16)
 
 
-def place_body(ids_ref, place_ref, place_col_ref):
+def place_body(
+    ids_any, w_out_any, w_qk_any, w_value_any,
+    place_ref, place_col_ref, w_out_ref, w_qk_ref, w_value_ref, ids_ref, sems,
+):
+    copies = [
+        pltpu.make_async_copy(source, target, sems.at[index])
+        for index, (source, target) in enumerate(
+            (
+                (ids_any, ids_ref), (w_out_any, w_out_ref),
+                (w_qk_any, w_qk_ref), (w_value_any, w_value_ref),
+            )
+        )
+    ]
+    for copy in copies:
+        copy.start()
+    copies[0].wait()
     length = ids_ref.shape[1]
     earlier = (
         lax.broadcasted_iota(jnp.int32, (length, length), 0)
@@ -124,44 +163,39 @@
         place_ref[head : head + 1, :] = place.astype(jnp.int32)
         column = jnp.sum(jnp.where(same, place, 0.0), axis=1, keepdims=True)
         place_col_ref[:, head : head + 1] = column.astype(jnp.int32)
+    for copy in copies[1:]:
+        copy.wait()
 
 
 def middle_body(
     core_ref,
     tokens_ref,
     own_ref,
-    left_ref,
-    right_ref,
-    far0_ref,
-    far1_ref,
+    first_ref,
+    second_ref,
+    far_ref,
     w_own_ref,
-    w_left_ref,
-    w_right_ref,
-    w_far_ref,
-    x_own_ref,
-    x_left_ref,
-    x_right_ref,
-    x_far_ref,
+    w_first_ref,
+    w_second_ref,
+    w_far_mine_ref,
+    w_far_other_ref,
     w_qk_ref,
     w_value_ref,
     place_ref,
     hidden_ref,
     out_ref,
-    far_ref,
 ):
-    core = core_ref[0]
-    far_ref[0] = far0_ref[...]
-    far_ref[1] = far1_ref[...]
-    left_side = []
-    right_side = []
-    for att, mine, other in (
-        (own_ref, w_own_ref, x_own_ref),
-        (left_ref, w_left_ref, x_left_ref),
-        (right_ref, w_right_ref, x_right_ref),
-        (far_ref, w_far_ref, x_far_ref),
-    ):
-        left_side += [att[core], att[1 - core]]
-        right_side += [mine[...], other[...]]
+    even = core_ref[0] == 0
+    far_mine = w_far_mine_ref[...]
+    far_other = w_far_other_ref[...]
+    left_side = [own_ref[...], first_ref[...], second_ref[...], far_ref[...]]
+    right_side = [
+        w_own_ref[...],
+        w_first_ref[...],
+        w_second_ref[...],
+        jnp.where(even, far_mine, far_other),
+        jnp.where(even, far_other, far_mine),
+    ]
     mixed = matmul(jnp.concatenate(left_side, axis=1), jnp.concatenate(right_side, axis=0))
     hidden = (tokens_ref[...].astype(F32) + mixed).astype(BF16)
     hidden_ref[...] = hidden
@@ -230,25 +264,32 @@
         out_ref[here, :] = (mixed[:, :HEAD_DIM] / mixed[:, HEAD_DIM:]).astype(BF16)
 
 
-def back_body(returned_ref, place_col_ref, out_ref):
+def back_body(
+    narrow_ref, returned_ref, place_col_ref, weight_ref, own_ref, next_ref, last_ref, far_ref
+):
     length = place_col_ref.shape[0]
+    parts = []
     for head in range(2):
         spot = lax.broadcasted_iota(jnp.int32, (length, SLOTS), 1)
         pick = (spot == place_col_ref[:, head : head + 1]).astype(F32).astype(BF16)
-        out_ref[head] = matmul(pick, returned_ref[head]).astype(BF16)
-
-
-def last_body(
-    own_ref, left_ref, right_ref, far0_ref, far1_ref, w_own_ref, w_left_ref, w_right_ref,
-    w_far_ref, hidden_ref, out_ref,
-):
-    left_side = [
-        own_ref[0], own_ref[1], left_ref[0], left_ref[1],
-        right_ref[0], right_ref[1], far0_ref[...], far1_ref[...],
-    ]
-    right_side = [w_own_ref[...], w_left_ref[...], w_right_ref[...], w_far_ref[...]]
-    mixed = matmul(jnp.concatenate(left_side, axis=1), jnp.concatenate(right_side, axis=0))
-    out_ref[...] = hidden_ref[...].astype(F32) + mixed
+        parts.append(matmul(pick, returned_ref[head]).astype(BF16))
+    attended = jnp.concatenate(parts, axis=1)
+    width = own_ref.shape[1]
+    groups = weight_ref.shape[1] // width
+    for steps, target in ((1, next_ref), (groups - 1, last_ref), (2, far_ref), (0, own_ref)):
+        group = lax.rem(narrow_ref[0] + steps, groups)
+        columns = pl.ds(pl.multiple_of(group * width, width), width)
+        term = matmul(attended, weight_ref[:, columns])
+        target[...] = term.astype(target.dtype)
+
+
+def last_body(narrow_ref, own_ref, one_ref, two_ref, three_ref, hidden_ref, out_ref):
+    width = own_ref.shape[1]
+    columns = pl.ds(pl.multiple_of(narrow_ref[0] * width, width), width)
+    mixed = own_ref[...].astype(F32)
+    for term_ref in (one_ref, two_ref, three_ref):
+        mixed += term_ref[...].astype(F32)
+    out_ref[...] = hidden_ref[:, columns].astype(F32) + mixed
 
 
 def around(value, steps):
@@ -256,17 +297,19 @@
     return lax.ppermute(value, "narrow", [(i, (i + steps) % count) for i in range(count)])
 
 
+def around_by_core(value, steps):
+    count = lax.axis_size("narrow")
+    pairs = [
+        (w * count + n, w * count + (n + (steps if w % 2 == 0 else -steps)) % count)
+        for w in range(lax.axis_size("wide"))
+        for n in range(count)
+    ]
+    return lax.ppermute(value, ("wide", "narrow"), pairs)
+
+
 def swap_cores(value):
     count = lax.axis_size("wide")
     return lax.ppermute(value, "wide", [(i, i ^ 1) for i in range(count)])
-
-
-def gather_pair(value):
-    left = around(value, 1)
-    right = around(value, -1)
-    far0 = around(left[0], 1)
-    far1 = around(right[1], -1)
-    return left, right, far0, far1
 
 
 def shards(tokens, w_qk1, w_value1, w_out1, w_qk2, w_value2, w_out2, cluster_ids):
@@ -275,17 +318,11 @@
     wide = lax.axis_index("wide")
     narrow = lax.axis_index("narrow")
     wide_count = lax.axis_size("wide")
-    groups = lax.axis_size("narrow")
-    core = wide % 2
+    core = wide & 1
     group_width = w_qk1.shape[1]
 
-    half = lax.dynamic_slice_in_dim(w_out1, core * HEAD_DIM, HEAD_DIM, 0)
-    half = half.reshape(2, HEAD_DIM // 2, width)
-    w_left, w_right, w_far0, w_far1 = gather_pair(half)
-    w_mine = [
-        item.reshape(HEAD_DIM, width)
-        for item in (half, w_left, w_right, jnp.stack([w_far0, w_far1]))
-    ]
+    w_first = around_by_core(w_out1, 1)
+    w_half = lax.dynamic_slice_in_dim(w_out1, core * HEAD_DIM, HEAD_DIM, 0)
 
     qk1, value1, tails = call(
         front_body,
@@ -295,35 +332,59 @@
             shape((2, WINDOW, group_width), BF16),
         ),
         (tokens, w_qk1, w_value1),
+        scratch=(
+            pltpu.VMEM((length, width), BF16),
+            pltpu.VMEM((width, group_width), BF16),
+            pltpu.VMEM((width, group_width), BF16),
+            pltpu.SemaphoreType.DMA((4,)),
+        ),
         flops=2 * length * width * group_width * 2,
         bytes_accessed=3 * 2**20,
-    )
+        space=pltpu.HBM,
+        mib=53,
+    )
+    tails, w_half = lax.optimization_barrier((tails, w_half))
+    w_far_mine = around(w_half, 2)
     before = lax.ppermute(tails, "wide", [(i, i + 1) for i in range(wide_count - 1)])
-    place, place_col = call(
-        place_body,
-        (shape((2, length), jnp.int32), shape((length, 2), jnp.int32)),
-        (cluster_ids,),
-        flops=2**26,
-        bytes_accessed=2**18,
-    )
     attended1 = call(
         window_body,
-        shape((2, length, HEAD_DIM), BF16),
+        shape((length, group_width), BF16),
         (wide.reshape(1), qk1, value1, before),
         prefetch=1,
         flops=2**28,
         bytes_accessed=2**20,
     )
-    w_other = [swap_cores(item) for item in w_mine]
-    left, right, far0, far1 = gather_pair(attended1)
+    attended1, cluster_ids, w_out1_later, w_qk2, w_value2 = lax.optimization_barrier(
+        (attended1, cluster_ids, w_out1, w_qk2, w_value2)
+    )
+    w_second = swap_cores(w_first)
+    w_far_other = swap_cores(w_far_mine)
+    far = around(attended1, 2)
+    first = around_by_core(attended1, 1)
+    second = around_by_core(attended1, -1)
+    place, place_col, w_out1_near, w_qk2_near, w_value2_near = call(
+        place_body,
+        (
+            shape((2, length), jnp.int32),
+            shape((length, 2), jnp.int32),
+            shape(w_out1.shape, BF16),
+            shape(w_qk2.shape, BF16),
+            shape(w_value2.shape, BF16),
+        ),
+        (cluster_ids, w_out1_later, w_qk2, w_value2),
+        scratch=(pltpu.VMEM((2, length), jnp.int32), pltpu.SemaphoreType.DMA((4,))),
+        flops=2**26,
+        bytes_accessed=2**18,
+        space=pltpu.HBM,
+    )
     hidden, outgoing = call(
         middle_body,
         (shape((length, width), BF16), shape((2, SLOTS, 2 * HEAD_DIM), BF16)),
         (
-            core.reshape(1), tokens, attended1, left, right, far0, far1,
-            *w_mine, *w_other, w_qk2, w_value2, place,
-        ),
-        scratch=(pltpu.VMEM((2, length, HEAD_DIM), BF16),),
+            core.reshape(1), tokens, attended1, first, second, far,
+            w_out1_near, w_first, w_second, w_far_mine, w_far_other,
+            w_qk2_near, w_value2_near, place,
+        ),
         prefetch=1,
         flops=2**31,
         bytes_accessed=2**23,
@@ -333,7 +394,7 @@
         outgoing.reshape(wide_count, per_pair, 2 * HEAD_DIM), "wide", 0, 0, tiled=True
     ).reshape(2 * SLOTS, 2 * HEAD_DIM)
     other = swap_cores(arrived)
-    info = jnp.stack([core, ((wide // 2) % 16 < 8).astype(jnp.int32)])
+    info = jnp.stack([core, (((wide >> 1) & 15) < 8).astype(jnp.int32)])
     rows = 2 * SLOTS
     answers = call(
         cluster_body,
@@ -351,31 +412,24 @@
     returned = lax.all_to_all(
         answers.reshape(wide_count, per_pair, HEAD_DIM), "wide", 0, 0, tiled=True
     ).reshape(2, SLOTS, HEAD_DIM)
-    attended2 = call(
+    block = shape((length, group_width), BF16)
+    own, to_next, to_last, to_far = call(
         back_body,
-        shape((2, length, HEAD_DIM), BF16),
-        (returned, place_col),
-        flops=2**27,
-        bytes_accessed=2**20,
-    )
-    left, right, far0, far1 = gather_pair(attended2)
-
-    def columns_for(steps):
-        target = (narrow + steps) % groups
-        return lax.dynamic_slice_in_dim(w_out2, target * group_width, group_width, 1)
-
-    w_own2 = columns_for(0)
-    w_left2 = around(columns_for(1), 1)
-    w_right2 = around(columns_for(-1), -1)
-    w_far2 = around(columns_for(2), 2)
-    hidden_own = lax.dynamic_slice_in_dim(hidden, narrow * group_width, group_width, 1)
+        (block, block, block, block),
+        (narrow.reshape(1), returned, place_col, w_out2),
+        prefetch=1,
+        flops=2**29,
+        bytes_accessed=2**21,
+    )
     return call(
         last_body,
         shape((length, group_width), F32),
         (
-            attended2, left, right, far0, far1, w_own2, w_left2, w_right2, w_far2, hidden_own,
-        ),
-        flops=2**29,
+            narrow.reshape(1), own, around(to_far, 2), around(to_next, 1),
+            around(to_last, -1), hidden,
+        ),
+        prefetch=1,
+        flops=2**22,
         bytes_accessed=2**21,
     )
 

time: 113 us -> 106 us (0.938)
  blocking collectives: 50.6 us -> 25.1 us
  waiting for transfers between devices: 19.8 us -> 38.1 us
  local copies, waits for them, and re-layouts: 4.27 us -> 0.06 us
  Pallas kernels: 9.93 us -> 12.7 us
    all_to_all x1 -> x0, blocking collectives: 18.7 us -> none  [shards(): lax.all_to_all(answers.reshape(wide_count, per_pair, HEAD_DIM), 'wide', 0...]
    ppermute x15 -> x5, starting transfers between devices: 21.7 us -> 6.05 us  [around(): lax.ppermute(value, 'narrow', [(i, (i + steps) % count) for i in range(co...]
    all_to_all x0 -> x1, waiting for transfers between devices: none -> 13.2 us  [shards(): lax.all_to_all(answers.reshape(wide_count, per_pair, HEAD_DIM), 'wide', 0...]
    all_to_all x1, blocking collectives: 32 us -> 25.1 us  [shards(): lax.all_to_all(outgoing.reshape(wide_count, per_pair, 2 * HEAD_DIM), 'wid...]
    ppermute x5 -> x3, starting transfers between devices: 1.87 us -> 8.45 us  [swap_cores(): return lax.ppermute(value, 'wide', [(i, i ^ 1) for i in range(count)])]
    ppermute x0 -> x3, starting transfers between devices: none -> 6.08 us  [around_by_core(): return lax.ppermute(value, ('wide', 'narrow'), pairs)]
    all_to_all x0 -> x1, starting transfers between devices: none -> 5.84 us  [shards(): lax.all_to_all(answers.reshape(wide_count, per_pair, HEAD_DIM), 'wide', 0...]
    ppermute x0 -> x3, waiting for transfers between devices: none -> 5.54 us  [around_by_core(): return lax.ppermute(value, ('wide', 'narrow'), pairs)]
  transfers between devices with their start and end apart: 21 -> 13, of which waited for: 9 -> 6; matrix products, arithmetic and copies ran while one was open for 1% -> 0% of each run, Pallas kernels for 1% -> 4%
where the time goes in v2:
time: 106 us; the launch traced here: 105 us
  waiting for transfers between devices  38.1 us (36%)
  starting transfers between devices  29.2 us (28%)
  blocking collectives  25.1 us (24%)
  Pallas kernels  12.7 us (12%)
    all_to_all x1, blocking collectives, shards(): lax.all_to_all(outgoing.reshape(wide_count, per_pair, 2 * HEAD_DIM), 'wid...  25.1 us
    ppermute x5, waiting for transfers between devices, around(): lax.ppermute(value, 'narrow', [(i, (i + steps) % count) for i in range(co...  18 us
    all_to_all x1, waiting for transfers between devices, shards(): lax.all_to_all(answers.reshape(wide_count, per_pair, HEAD_DIM), 'wide', 0...  13.2 us
    pallas_call x7, Pallas kernels, call(): pl.pallas_call(body, out_shape=outs, in_specs=whole, out_specs=jax.tree.m...  12.7 us
    ppermute x3, starting transfers between devices, swap_cores(): return lax.ppermute(value, 'wide', [(i, i ^ 1) for i in range(count)])  8.45 us
    ppermute x3, starting transfers between devices, around_by_core(): return lax.ppermute(value, ('wide', 'narrow'), pairs)  6.08 us
    ppermute x5, starting transfers between devices, around(): lax.ppermute(value, 'narrow', [(i, (i + steps) % count) for i in range(co...  6.05 us
    all_to_all x1, starting transfers between devices, shards(): lax.all_to_all(answers.reshape(wide_count, per_pair, HEAD_DIM), 'wide', 0...  5.84 us
  transfers between devices with their start and end apart: 13, of which 6 were waited for; matrix products, arithmetic and copies ran while one was open for 0% of the time, Pallas kernels for 4%

profile of v2, /device:TPU:1, one launch (start us, length us, event | category | flops | bytes accessed | tf_op | source)
XLA Modules:
  0.0 105.4 jit_solution(4849141969102675563)
XLA Ops:
  0.0 3.3 %collective-permute-start.4 = (bf16[256,1024]{1,0:T(8,128)(2,1)}, bf16[256,1024]{1,0:T(8,128)(2,1)S(1)}, u32[]{:S(2)}, u32[]{:S(2)}) collective-permute-start(bf16[256,1024]{1,0:T(8,128)(2,1)} %w_out_any), channel_id=1, source_target_pairs={{0,1},{1,2},{2,3},{3,0},{4,7},{5,4},{6,5},{7,6},{8,9},{9,10},{10,1... | collective-permute-start | bytes 1572872 | tf_op jit(solution)/shard_map/ppermute | solution.py:307
  3.3 0.0 copy-start
  3.3 2.7 %shard_map.82 = (bf16[512,256]{1,0:T(8,128)(2,1)S(1)}, bf16[512,256]{1,0:T(8,128)(2,1)S(1)}, bf16[2,256,256]{2,1,0:T(8,128)(2,1)S(1)}) custom-call(bf16[512,1024]{1,0:T(8,128)(2,1)} %tokens_ref.1, bf16[1024,256]{1,0:T(8,128)(2,1)} %w_qk_any.1, bf16[1024,256]{1,0:T(8,128)(2,1)} %w_value_any.1), custom_call_target="tpu_custom_call" | custom-call | flops 536870912 | bytes 3145728 | tf_op jit(solution)/shard_map/pallas_call | solution.py:29
  6.0 0.0 copy-done
  6.0 0.0 copy-start.4
  6.1 2.8 %collective-permute-start = (bf16[2,256,256]{2,1,0:T(8,128)(2,1)S(1)}, bf16[2,256,256]{2,1,0:T(8,128)(2,1)S(1)}, u32[]{:S(2)}, u32[]{:S(2)}) collective-permute-start(bf16[2,256,256]{2,1,0:T(8,128)(2,1)S(1)} %get-tuple-element.29), channel_id=1, source_target_pairs={{0,4},{4,8},{8,12},{12,16},{16,20},{20,24},{24,28},{28,32},{32,36}... | collective-permute-start | bytes 786440 | tf_op jit(solution)/shard_map/ppermute | solution.py:348
  8.9 2.5 %collective-permute-start.6 = (bf16[128,1024]{1,0:T(8,128)(2,1)S(1)}, bf16[128,1024]{1,0:T(8,128)(2,1)S(1)}, u32[]{:S(2)}, u32[]{:S(2)}) collective-permute-start(bf16[128,1024]{1,0:T(8,128)(2,1)S(1)} %constant_dynamic-slice_fusion), channel_id=1, source_target_pairs={{0,2},{1,3},{2,0},{3,1},{4,6},{5,7},{6,4},{7,5},{8,10},{9,11},{10,... | collective-permute-start | bytes 786440 | tf_op jit(solution)/shard_map/ppermute | solution.py:297
  11.4 0.0 collective-permute-done.4.w_first_ref
  11.4 8.1 %collective-permute-start.5 = (bf16[256,1024]{1,0:T(8,128)(2,1)S(1)}, bf16[256,1024]{1,0:T(8,128)(2,1)S(1)}, u32[]{:S(2)}, u32[]{:S(2)}) collective-permute-start(bf16[256,1024]{1,0:T(8,128)(2,1)S(1)} %collective-permute-done.4.w_first_ref), channel_id=1, source_target_pairs={{0,4},{4,0},{8,12},{12,8},{16,20},{20,16},{24,28},{28,24},{32,36},... | collective-permute-start | bytes 1572872 | tf_op jit(solution)/shard_map/ppermute | solution.py:312
  19.5 0.0 collective-permute-done.before_ref
  19.5 0.0 copy-start.2
  19.5 0.0 copy-start.3
  19.5 1.0 shard_map.83.own_ref
  20.5 0.0 copy-start.1
  20.5 0.1 collective-permute-start.3
  20.6 0.1 collective-permute-start.2
  20.7 2.7 %collective-permute-start.1 = (bf16[512,256]{1,0:T(8,128)(2,1)S(1)}, bf16[512,256]{1,0:T(8,128)(2,1)S(1)}, u32[]{:S(2)}, u32[]{:S(2)}) collective-permute-start(bf16[512,256]{1,0:T(8,128)(2,1)S(1)} %shard_map.83.own_ref), channel_id=1, source_target_pairs={{0,1},{1,2},{2,3},{3,0},{4,7},{5,4},{6,5},{7,6},{8,9},{9,10},{10,1... | collective-permute-start | bytes 786440 | tf_op jit(solution)/shard_map/ppermute | solution.py:307
  23.4 0.0 collective-permute-done.6.w_far_mine_ref
  23.4 0.0 collective-permute-start.7
  23.4 0.0 copy-done.4
  23.4 0.0 copy-done.2
  23.4 0.0 copy-done.3
  23.4 0.7 shard_map.84
  24.1 5.9 %collective-permute-done.3.far_ref = bf16[512,256]{1,0:T(8,128)(2,1)S(1)} collective-permute-done((bf16[512,256]{1,0:T(8,128)(2,1)S(1)}, bf16[512,256]{1,0:T(8,128)(2,1)S(1)}, u32[]{:S(2)}, u32[]{:S(2)}) %collective-permute-start.3) | collective-permute-done | bytes 262176 | tf_op jit(solution)/shard_map/ppermute | solution.py:297
  30.0 5.5 %collective-permute-done.2.second_ref = bf16[512,256]{1,0:T(8,128)(2,1)S(1)} collective-permute-done((bf16[512,256]{1,0:T(8,128)(2,1)S(1)}, bf16[512,256]{1,0:T(8,128)(2,1)S(1)}, u32[]{:S(2)}, u32[]{:S(2)}) %collective-permute-start.2) | collective-permute-done | bytes 262176 | tf_op jit(solution)/shard_map/ppermute | solution.py:307
  35.6 0.0 collective-permute-done.1.first_ref
  35.6 0.0 collective-permute-done.7.w_far_other_ref
  35.6 0.0 collective-permute-done.5.w_second_ref
  35.6 0.0 copy-done.1
  35.6 2.4 %shard_map.85 = (bf16[512,1024]{1,0:T(8,128)(2,1)S(1)}, bf16[2,512,256]{2,1,0:T(8,128)(2,1)S(1)}) custom-call(s32[1]{0:T(128)} %bitcast.1.core_ref, bf16[512,1024]{1,0:T(8,128)(2,1)S(1)} %copy-done.1, bf16[512,256]{1,0:T(8,128)(2,1)S(1)} %shard_map.83.own_ref, bf16[512,256]{1,0:T(8,128)(2,1)S(1)} %collective-permute-done.1.first_ref, ...), custom_call_target="tpu_custom_call" | custom-call | flops 2147483648 | bytes 8388608 | tf_op jit(solution)/shard_map/pallas_call | solution.py:29
  38.1 25.1 %all_to_all.10 = bf16[64,16,256]{2,1,0:T(8,128)(2,1)S(1)} all-to-all(bf16[64,16,256]{2,1,0:T(8,128)(2,1)S(1)} %bitcast.10), channel_id=1, replica_groups=mesh['wide'=64,'narrow'=4] {'wide'}, dimensions={0} | all-to-all | bytes 1048576 | tf_op jit(solution)/shard_map/all_to_all | solution.py:393
  63.1 0.4 collective-permute-start.8
  63.5 0.1 pad_add_fusion.info_ref
  63.6 1.5 %collective-permute-done.8.other_ref = bf16[1024,256]{1,0:T(8,128)(2,1)S(1)} collective-permute-done((bf16[1024,256]{1,0:T(8,128)(2,1)S(1)}, bf16[1024,256]{1,0:T(8,128)(2,1)S(1)}, u32[]{:S(2)}, u32[]{:S(2)}) %collective-permute-start.8) | collective-permute-done | bytes 524320 | tf_op jit(solution)/shard_map/ppermute | solution.py:312
  65.1 4.1 %shard_map.86 = bf16[1024,128]{1,0:T(8,128)(2,1)} custom-call(s32[2]{0:T(128)S(1)} %pad_add_fusion.info_ref, bf16[1024,256]{1,0:T(8,128)(2,1)S(1)} %bitcast.9, bf16[1024,256]{1,0:T(8,128)(2,1)S(1)} %collective-permute-done.8.other_ref), custom_call_target="tpu_custom_call" | custom-call | flops 1073741824 | bytes 2097152 | tf_op jit(solution)/shard_map/pallas_call | solution.py:29
  69.1 0.0 copy-start.5
  69.1 5.8 %all-to-all-start.1 = ((bf16[64,16,128]{2,1,0:T(8,128)(2,1)}), bf16[64,16,128]{2,1,0:T(8,128)(2,1)S(1)}, u32[]{:S(2)}, u32[]{:S(2)}) async-start(bf16[64,16,128]{2,1,0:T(8,128)(2,1)} %bitcast.6), calls=%async_computation.1 | async-start | bytes 524288 | tf_op jit(solution)/shard_map/all_to_all | solution.py:412
  75.0 13.2 %all-to-all-done.1 = bf16[64,16,128]{2,1,0:T(8,128)(2,1)S(1)} async-done(((bf16[64,16,128]{2,1,0:T(8,128)(2,1)}), bf16[64,16,128]{2,1,0:T(8,128)(2,1)S(1)}, u32[]{:S(2)}, u32[]{:S(2)}) %all-to-all-start.1) | async-done | bytes 262176 | tf_op jit(solution)/shard_map/all_to_all | solution.py:412
  88.1 0.0 copy-done.5
  88.1 0.8 shard_map.87
  89.0 0.7 collective-permute-start.9
  89.7 2.3 %collective-permute-start.10 = (bf16[512,256]{1,0:T(8,128)(2,1)S(1)}, bf16[512,256]{1,0:T(8,128)(2,1)S(1)}, u32[]{:S(2)}, u32[]{:S(2)}) collective-permute-start(bf16[512,256]{1,0:T(8,128)(2,1)S(1)} %get-tuple-element.44), channel_id=1, source_target_pairs={{0,1},{1,2},{2,3},{3,0},{4,5},{5,6},{6,7},{7,4},{8,9},{9,10},{10,1... | collective-permute-start | bytes 786440 | tf_op jit(solution)/shard_map/ppermute | solution.py:297
  92.0 0.4 collective-permute-start.11
  92.4 5.9 %collective-permute-done.9.one_ref = bf16[512,256]{1,0:T(8,128)(2,1)S(1)} collective-permute-done((bf16[512,256]{1,0:T(8,128)(2,1)S(1)}, bf16[512,256]{1,0:T(8,128)(2,1)S(1)}, u32[]{:S(2)}, u32[]{:S(2)}) %collective-permute-start.9) | collective-permute-done | bytes 262176 | tf_op jit(solution)/shard_map/ppermute | solution.py:297
  98.2 6.2 %collective-permute-done.10.two_ref = bf16[512,256]{1,0:T(8,128)(2,1)S(1)} collective-permute-done((bf16[512,256]{1,0:T(8,128)(2,1)S(1)}, bf16[512,256]{1,0:T(8,128)(2,1)S(1)}, u32[]{:S(2)}, u32[]{:S(2)}) %collective-permute-start.10) | collective-permute-done | bytes 262176 | tf_op jit(solution)/shard_map/ppermute | solution.py:297
  104.4 0.0 collective-permute-done.11.three_ref
  104.4 1.0 shard_map.88
  (1 shorter events, 0.0 us)
Async XLA Ops:
  0.0 11.4 %collective-permute-start.4 = (bf16[256,1024]{1,0:T(8,128)(2,1)}, bf16[256,1024]{1,0:T(8,128)(2,1)S(1)}, u32[]{:S(2)}, u32[]{:S(2)}) collective-permute-start(bf16[256,1024]{1,0:T(8,128)(2,1)} %w_out_any), channel_id=1, source_target_pairs={{0,1},{1,2},{2,3},{3,0},{4,7},{5,4},{6,5},{7,6},{8,9},{9,10},{10,1... | collective-permute-start | bytes 1572872 | tf_op jit(solution)/shard_map/ppermute | solution.py:307
  3.3 2.7 %copy-start = (bf16[256,1024]{1,0:T(8,128)(2,1)S(1)}, bf16[256,1024]{1,0:T(8,128)(2,1)}, u32[]{:S(2)}) copy-start(bf16[256,1024]{1,0:T(8,128)(2,1)} %w_out_any) | copy-start | bytes 1572868
  6.0 17.3 %copy-start.4 = (s32[2,512]{1,0:T(2,128)S(1)}, s32[2,512]{1,0:T(2,128)}, u32[]{:S(2)}) copy-start(s32[2,512]{1,0:T(2,128)} %ids_any) | copy-start | bytes 12292
  6.1 13.4 %collective-permute-start = (bf16[2,256,256]{2,1,0:T(8,128)(2,1)S(1)}, bf16[2,256,256]{2,1,0:T(8,128)(2,1)S(1)}, u32[]{:S(2)}, u32[]{:S(2)}) collective-permute-start(bf16[2,256,256]{2,1,0:T(8,128)(2,1)S(1)} %get-tuple-element.29), channel_id=1, source_target_pairs={{0,4},{4,8},{8,12},{12,16},{16,20},{20,24},{24,28},{28,32},{32,36}... | collective-permute-start | bytes 786440 | tf_op jit(solution)/shard_map/ppermute | solution.py:348
  8.9 14.5 %collective-permute-start.6 = (bf16[128,1024]{1,0:T(8,128)(2,1)S(1)}, bf16[128,1024]{1,0:T(8,128)(2,1)S(1)}, u32[]{:S(2)}, u32[]{:S(2)}) collective-permute-start(bf16[128,1024]{1,0:T(8,128)(2,1)S(1)} %constant_dynamic-slice_fusion), channel_id=1, source_target_pairs={{0,2},{1,3},{2,0},{3,1},{4,6},{5,7},{6,4},{7,5},{8,10},{9,11},{10,... | collective-permute-start | bytes 786440 | tf_op jit(solution)/shard_map/ppermute | solution.py:297
  11.4 24.2 %collective-permute-start.5 = (bf16[256,1024]{1,0:T(8,128)(2,1)S(1)}, bf16[256,1024]{1,0:T(8,128)(2,1)S(1)}, u32[]{:S(2)}, u32[]{:S(2)}) collective-permute-start(bf16[256,1024]{1,0:T(8,128)(2,1)S(1)} %collective-permute-done.4.w_first_ref), channel_id=1, source_target_pairs={{0,4},{4,0},{8,12},{12,8},{16,20},{20,16},{24,28},{28,24},{32,36},... | collective-permute-start | bytes 1572872 | tf_op jit(solution)/shard_map/ppermute | solution.py:312
  19.5 3.9 %copy-start.2 = (bf16[1024,256]{1,0:T(8,128)(2,1)S(1)}, bf16[1024,256]{1,0:T(8,128)(2,1)}, u32[]{:S(2)}) copy-start(bf16[1024,256]{1,0:T(8,128)(2,1)} %w_qk_any.2) | copy-start | bytes 1572868
  19.5 3.9 %copy-start.3 = (bf16[1024,256]{1,0:T(8,128)(2,1)S(1)}, bf16[1024,256]{1,0:T(8,128)(2,1)}, u32[]{:S(2)}) copy-start(bf16[1024,256]{1,0:T(8,128)(2,1)} %w_value_any.2) | copy-start | bytes 1572868
  20.5 15.1 %copy-start.1 = (bf16[512,1024]{1,0:T(8,128)(2,1)S(1)}, bf16[512,1024]{1,0:T(8,128)(2,1)}, u32[]{:S(2)}) copy-start(bf16[512,1024]{1,0:T(8,128)(2,1)} %tokens_ref.1) | copy-start | bytes 3145732
  20.5 9.6 %collective-permute-start.3 = (bf16[512,256]{1,0:T(8,128)(2,1)S(1)}, bf16[512,256]{1,0:T(8,128)(2,1)S(1)}, u32[]{:S(2)}, u32[]{:S(2)}) collective-permute-start(bf16[512,256]{1,0:T(8,128)(2,1)S(1)} %shard_map.83.own_ref), channel_id=1, source_target_pairs={{0,2},{1,3},{2,0},{3,1},{4,6},{5,7},{6,4},{7,5},{8,10},{9,11},{10,... | collective-permute-start | bytes 786440 | tf_op jit(solution)/shard_map/ppermute | solution.py:297
  20.6 15.0 %collective-permute-start.2 = (bf16[512,256]{1,0:T(8,128)(2,1)S(1)}, bf16[512,256]{1,0:T(8,128)(2,1)S(1)}, u32[]{:S(2)}, u32[]{:S(2)}) collective-permute-start(bf16[512,256]{1,0:T(8,128)(2,1)S(1)} %shard_map.83.own_ref), channel_id=1, source_target_pairs={{0,3},{1,0},{2,1},{3,2},{4,5},{5,6},{6,7},{7,4},{8,11},{9,8},{10,9... | collective-permute-start | bytes 786440 | tf_op jit(solution)/shard_map/ppermute | solution.py:307
  20.7 14.9 %collective-permute-start.1 = (bf16[512,256]{1,0:T(8,128)(2,1)S(1)}, bf16[512,256]{1,0:T(8,128)(2,1)S(1)}, u32[]{:S(2)}, u32[]{:S(2)}) collective-permute-start(bf16[512,256]{1,0:T(8,128)(2,1)S(1)} %shard_map.83.own_ref), channel_id=1, source_target_pairs={{0,1},{1,2},{2,3},{3,0},{4,7},{5,4},{6,5},{7,6},{8,9},{9,10},{10,1... | collective-permute-start | bytes 786440 | tf_op jit(solution)/shard_map/ppermute | solution.py:307
  23.4 12.2 %collective-permute-start.7 = (bf16[128,1024]{1,0:T(8,128)(2,1)S(1)}, bf16[128,1024]{1,0:T(8,128)(2,1)S(1)}, u32[]{:S(2)}, u32[]{:S(2)}) collective-permute-start(bf16[128,1024]{1,0:T(8,128)(2,1)S(1)} %collective-permute-done.6.w_far_mine_ref), channel_id=1, source_target_pairs={{0,4},{4,0},{8,12},{12,8},{16,20},{20,16},{24,28},{28,24},{32,36},... | collective-permute-start | bytes 786440 | tf_op jit(solution)/shard_map/ppermute | solution.py:312
  63.1 1.9 %collective-permute-start.8 = (bf16[1024,256]{1,0:T(8,128)(2,1)S(1)}, bf16[1024,256]{1,0:T(8,128)(2,1)S(1)}, u32[]{:S(2)}, u32[]{:S(2)}) collective-permute-start(bf16[1024,256]{1,0:T(8,128)(2,1)S(1)} %bitcast.8), channel_id=1, source_target_pairs={{0,4},{4,0},{8,12},{12,8},{16,20},{20,16},{24,28},{28,24},{32,36},... | collective-permute-start | bytes 1572872 | tf_op jit(solution)/shard_map/ppermute | solution.py:312
  69.1 19.0 %copy-start.5 = (bf16[256,1024]{1,0:T(8,128)(2,1)S(1)}, bf16[256,1024]{1,0:T(8,128)(2,1)}, u32[]{:S(2)}) copy-start(bf16[256,1024]{1,0:T(8,128)(2,1)} %weight_ref.1) | copy-start | bytes 1572868
  69.1 19.0 %all-to-all-start.1 = ((bf16[64,16,128]{2,1,0:T(8,128)(2,1)}), bf16[64,16,128]{2,1,0:T(8,128)(2,1)S(1)}, u32[]{:S(2)}, u32[]{:S(2)}) async-start(bf16[64,16,128]{2,1,0:T(8,128)(2,1)} %bitcast.6), calls=%async_computation.1 | async-start | bytes 524288 | tf_op jit(solution)/shard_map/all_to_all | solution.py:412
  89.0 9.3 %collective-permute-start.9 = (bf16[512,256]{1,0:T(8,128)(2,1)S(1)}, bf16[512,256]{1,0:T(8,128)(2,1)S(1)}, u32[]{:S(2)}, u32[]{:S(2)}) collective-permute-start(bf16[512,256]{1,0:T(8,128)(2,1)S(1)} %get-tuple-element.43), channel_id=1, source_target_pairs={{0,2},{1,3},{2,0},{3,1},{4,6},{5,7},{6,4},{7,5},{8,10},{9,11},{10,... | collective-permute-start | bytes 786440 | tf_op jit(solution)/shard_map/ppermute | solution.py:297
  89.7 14.7 %collective-permute-start.10 = (bf16[512,256]{1,0:T(8,128)(2,1)S(1)}, bf16[512,256]{1,0:T(8,128)(2,1)S(1)}, u32[]{:S(2)}, u32[]{:S(2)}) collective-permute-start(bf16[512,256]{1,0:T(8,128)(2,1)S(1)} %get-tuple-element.44), channel_id=1, source_target_pairs={{0,1},{1,2},{2,3},{3,0},{4,5},{5,6},{6,7},{7,4},{8,9},{9,10},{10,1... | collective-permute-start | bytes 786440 | tf_op jit(solution)/shard_map/ppermute | solution.py:297
  92.0 12.4 %collective-permute-start.11 = (bf16[512,256]{1,0:T(8,128)(2,1)S(1)}, bf16[512,256]{1,0:T(8,128)(2,1)S(1)}, u32[]{:S(2)}, u32[]{:S(2)}) collective-permute-start(bf16[512,256]{1,0:T(8,128)(2,1)S(1)} %get-tuple-element.45), channel_id=1, source_target_pairs={{0,3},{1,0},{2,1},{3,2},{4,7},{5,4},{6,5},{7,6},{8,11},{9,8},{10,9... | collective-permute-start | bytes 786440 | tf_op jit(solution)/shard_map/ppermute | solution.py:297

commit v3 on v2

--- a/solution.py
+++ b/solution.py
@@ -211,57 +211,81 @@
         out_ref[head] = matmul(pick, rows).astype(BF16)
 
 
-def cluster_body(info_ref, mine_ref, other_ref, out_ref, keys_ref, values_ref, query_ref):
+def segments(tile, which, whole):
+    slot = (lax.broadcasted_iota(jnp.int32, (tile, HEAD_DIM), 0) & 15) + 16 * which
+    found = jnp.where(slot >= 24, 2, jnp.where(slot >= 12, 1, 0))
+    return jnp.where(whole, 0, found)
+
+
+def side_scores(query_ref, key_ref, part, tile, core, key_core, whole, keep):
+    lane = lax.broadcasted_iota(jnp.int32, (tile, HEAD_DIM), 1)
+    fence = jnp.where(lane == segments(tile, core, whole), 0.0, MASKED).astype(BF16)
+    member = jnp.where(lane == segments(tile, key_core, whole), 1.0, 0.0).astype(BF16)
+    here = slice(part * tile, (part + 1) * tile)
+    query = jnp.concatenate([query_ref[here, :HEAD_DIM], fence], axis=1)
+    groups = []
+    for past in range(part + 1):
+        span = slice(past * tile, (past + 1) * tile)
+        keys = jnp.concatenate([key_ref[span, :HEAD_DIM], member], axis=1)
+        scores = scores_of(query, keys)
+        if past == part:
+            scores = jnp.where(keep, scores, MASKED)
+        groups.append(scores)
+    return groups
+
+
+def row_tops(groups):
+    joined = functools.reduce(jnp.maximum, groups)
+    return jnp.max(joined, axis=-1, keepdims=True)
+
+
+def weigh(groups, top, value_ref, tile):
+    ones = jnp.ones((tile, HEAD_DIM), BF16)
+    mixed = None
+    for past, scores in enumerate(groups):
+        weights = jnp.exp2((scores - top) * EXP2_FACTOR).astype(BF16)
+        values = value_ref[past * tile : (past + 1) * tile, HEAD_DIM:]
+        term = matmul(weights, jnp.concatenate([values, ones], axis=1))
+        mixed = term if mixed is None else mixed + term
+    return mixed
+
+
+def own_side_body(info_ref, mine_ref, mixed_ref, top_ref):
     core = info_ref[0]
     whole = info_ref[1] == 1
-    rows = mine_ref.shape[0]
-    lane = lax.broadcasted_iota(jnp.int32, (rows, HEAD_DIM), 1)
-    row = lax.broadcasted_iota(jnp.int32, (rows, HEAD_DIM), 0) & 15
-
-    def segment(which):
-        slot = row + 16 * which
-        found = jnp.where(slot >= 24, 2, jnp.where(slot >= 12, 1, 0))
-        return jnp.where(whole, 0, found)
-
-    seg_mine = segment(core)
-    seg_other = segment(1 - core)
-    query_ref[:, :HEAD_DIM] = mine_ref[:, :HEAD_DIM]
-    query_ref[:, HEAD_DIM:] = jnp.where(lane == seg_mine, 0.0, MASKED).astype(BF16)
-    for side, (source, seg) in enumerate(((mine_ref, seg_mine), (other_ref, seg_other))):
-        keys_ref[side, :, :HEAD_DIM] = source[:, :HEAD_DIM]
-        keys_ref[side, :, HEAD_DIM:] = jnp.where(lane == seg, 1.0, 0.0).astype(BF16)
-        values_ref[side, :, :HEAD_DIM] = source[:, HEAD_DIM:]
-        values_ref[side, :, HEAD_DIM:] = jnp.ones((rows, HEAD_DIM), BF16)
     tile = 256
-    near_row = lax.broadcasted_iota(jnp.int32, (tile, tile), 0)
-    near_col = lax.broadcasted_iota(jnp.int32, (tile, tile), 1)
-    earlier = near_col < near_row
-    block_row = near_row >> 4
-    block_col = near_col >> 4
-    earlier_other = block_col < block_row + core
-    slot = (near_row & 15) + 16 * core
+    row = lax.broadcasted_iota(jnp.int32, (tile, tile), 0)
+    col = lax.broadcasted_iota(jnp.int32, (tile, tile), 1)
+    earlier = col < row
+    slot = (row & 15) + 16 * core
     opens = (slot == 0) | (jnp.logical_not(whole) & ((slot == 12) | (slot == 24)))
-    alone = (near_row == near_col) & opens & (near_row < 16)
-    for part in range(rows // tile):
+    alone = (row == col) & opens & (row < 16)
+    for part in range(mine_ref.shape[0] // tile):
         here = slice(part * tile, (part + 1) * tile)
-        query = query_ref[here, :]
         keep = (earlier | alone) if part == 0 else earlier
-        groups = []
-        for side in range(2):
-            if part > 0:
-                past = slice(0, part * tile)
-                groups.append((scores_of(query, keys_ref[side, past, :]), side, past))
-            near = scores_of(query, keys_ref[side, here, :])
-            near = jnp.where(keep if side == 0 else earlier_other, near, MASKED)
-            groups.append((near, side, here))
-        top = functools.reduce(
-            jnp.maximum, [jnp.max(scores, axis=-1, keepdims=True) for scores, _, _ in groups]
-        )
-        mixed = jnp.zeros((tile, 2 * HEAD_DIM), F32)
-        for scores, side, span in groups:
-            weights = jnp.exp2((scores - top) * EXP2_FACTOR).astype(BF16)
-            mixed += matmul(weights, values_ref[side, span, :])
-        out_ref[here, :] = (mixed[:, :HEAD_DIM] / mixed[:, HEAD_DIM:]).astype(BF16)
+        groups = side_scores(mine_ref, mine_ref, part, tile, core, core, whole, keep)
+        top = row_tops(groups)
+        mixed_ref[here, :] = weigh(groups, top, mine_ref, tile)
+        top_ref[here, :] = jnp.broadcast_to(top, (tile, HEAD_DIM))
+
+
+def other_side_body(info_ref, mine_ref, other_ref, mixed_ref, top_ref, out_ref):
+    core = info_ref[0]
+    whole = info_ref[1] == 1
+    tile = 256
+    row = lax.broadcasted_iota(jnp.int32, (tile, tile), 0)
+    col = lax.broadcasted_iota(jnp.int32, (tile, tile), 1)
+    earlier = (col >> 4) < (row >> 4) + core
+    for part in range(mine_ref.shape[0] // tile):
+        here = slice(part * tile, (part + 1) * tile)
+        groups = side_scores(mine_ref, other_ref, part, tile, core, 1 - core, whole, earlier)
+        own_top = top_ref[here, :]
+        top = jnp.maximum(jnp.broadcast_to(row_tops(groups), (tile, HEAD_DIM)), own_top)
+        shrink = jnp.exp2((own_top - top) * EXP2_FACTOR)
+        mixed = weigh(groups, jnp.concatenate([top, top], axis=1), other_ref, tile)
+        total = mixed[:, HEAD_DIM:] + mixed_ref[here, HEAD_DIM:] * shrink
+        sums = mixed[:, :HEAD_DIM] + mixed_ref[here, :HEAD_DIM] * shrink
+        out_ref[here, :] = (sums / total).astype(BF16)
 
 
 def back_body(
@@ -396,15 +420,18 @@
     other = swap_cores(arrived)
     info = jnp.stack([core, (((wide >> 1) & 15) < 8).astype(jnp.int32)])
     rows = 2 * SLOTS
+    own_mixed, own_top = call(
+        own_side_body,
+        (shape((rows, 2 * HEAD_DIM), F32), shape((rows, HEAD_DIM), F32)),
+        (info, arrived),
+        prefetch=1,
+        flops=2**30,
+        bytes_accessed=2**21,
+    )
     answers = call(
-        cluster_body,
+        other_side_body,
         shape((rows, HEAD_DIM), BF16),
-        (info, arrived, other),
-        scratch=(
-            pltpu.VMEM((2, rows, 2 * HEAD_DIM), BF16),
-            pltpu.VMEM((2, rows, 2 * HEAD_DIM), BF16),
-            pltpu.VMEM((rows, 2 * HEAD_DIM), BF16),
-        ),
+        (info, arrived, other, own_mixed, own_top),
         prefetch=1,
         flops=2**30,
         bytes_accessed=2**21,

time: 106 us -> 105 us (level)
  waiting for transfers between devices: 38.1 us -> 36.7 us
    ppermute x3, waiting for transfers between devices: 1.47 us -> 0.01 us  [swap_cores(): return lax.ppermute(value, 'wide', [(i, i ^ 1) for i in range(count)])]
    pallas_call x7 -> x8, Pallas kernels: 12.7 us -> 13.6 us  [call(): pl.pallas_call(body, out_shape=outs, in_specs=whole, out_specs=jax.tree.m...]
  transfers between devices with their start and end apart: 13 -> 13, of which waited for: 6 -> 5; matrix products, arithmetic and copies ran while one was open for 0% -> 0% of each run, Pallas kernels for 4% -> 6%
where the time goes in v3:
time: 105 us
  waiting for transfers between devices  36.7 us (35%)
  starting transfers between devices  28.9 us (28%)
  blocking collectives  25.1 us (24%)
  Pallas kernels  13.6 us (13%)
    all_to_all x1, blocking collectives, shards(): lax.all_to_all(outgoing.reshape(wide_count, per_pair, 2 * HEAD_DIM), 'wid...  25.1 us
    ppermute x5, waiting for transfers between devices, around(): lax.ppermute(value, 'narrow', [(i, (i + steps) % count) for i in range(co...  18 us
    pallas_call x8, Pallas kernels, call(): pl.pallas_call(body, out_shape=outs, in_specs=whole, out_specs=jax.tree.m...  13.6 us
    all_to_all x1, waiting for transfers between devices, shards(): lax.all_to_all(answers.reshape(wide_count, per_pair, HEAD_DIM), 'wide', 0...  13.2 us
    ppermute x3, starting transfers between devices, swap_cores(): return lax.ppermute(value, 'wide', [(i, i ^ 1) for i in range(count)])  8.45 us
    ppermute x3, starting transfers between devices, around_by_core(): return lax.ppermute(value, ('wide', 'narrow'), pairs)  6.08 us
    ppermute x5, starting transfers between devices, around(): lax.ppermute(value, 'narrow', [(i, (i + steps) % count) for i in range(co...  6.05 us
    all_to_all x1, starting transfers between devices, shards(): lax.all_to_all(answers.reshape(wide_count, per_pair, HEAD_DIM), 'wide', 0...  5.57 us
  transfers between devices with their start and end apart: 13, of which 5 were waited for; matrix products, arithmetic and copies ran while one was open for 0% of the time, Pallas kernels for 6%

profile of v3, /device:TPU:1, one launch (start us, length us, event | category | flops | bytes accessed | tf_op | source)
XLA Modules:
  0.0 104.6 jit_solution(18263371691526582177)
XLA Ops:
  0.0 3.3 %collective-permute-start.4 = (bf16[256,1024]{1,0:T(8,128)(2,1)}, bf16[256,1024]{1,0:T(8,128)(2,1)S(1)}, u32[]{:S(2)}, u32[]{:S(2)}) collective-permute-start(bf16[256,1024]{1,0:T(8,128)(2,1)} %w_out_any), channel_id=1, source_target_pairs={{0,1},{1,2},{2,3},{3,0},{4,7},{5,4},{6,5},{7,6},{8,9},{9,10},{10,1... | collective-permute-start | bytes 1572872 | tf_op jit(solution)/shard_map/ppermute | solution.py:331
  3.3 0.0 copy-start
  3.3 2.7 %shard_map.82 = (bf16[512,256]{1,0:T(8,128)(2,1)S(1)}, bf16[512,256]{1,0:T(8,128)(2,1)S(1)}, bf16[2,256,256]{2,1,0:T(8,128)(2,1)S(1)}) custom-call(bf16[512,1024]{1,0:T(8,128)(2,1)} %tokens_ref.1, bf16[1024,256]{1,0:T(8,128)(2,1)} %w_qk_any.1, bf16[1024,256]{1,0:T(8,128)(2,1)} %w_value_any.1), custom_call_target="tpu_custom_call" | custom-call | flops 536870912 | bytes 3145728 | tf_op jit(solution)/shard_map/pallas_call | solution.py:29
  6.0 0.0 copy-done
  6.0 0.0 copy-start.4
  6.1 2.8 %collective-permute-start = (bf16[2,256,256]{2,1,0:T(8,128)(2,1)S(1)}, bf16[2,256,256]{2,1,0:T(8,128)(2,1)S(1)}, u32[]{:S(2)}, u32[]{:S(2)}) collective-permute-start(bf16[2,256,256]{2,1,0:T(8,128)(2,1)S(1)} %get-tuple-element.31), channel_id=1, source_target_pairs={{0,4},{4,8},{8,12},{12,16},{16,20},{20,24},{24,28},{28,32},{32,36}... | collective-permute-start | bytes 786440 | tf_op jit(solution)/shard_map/ppermute | solution.py:372
  8.9 2.5 %collective-permute-start.6 = (bf16[128,1024]{1,0:T(8,128)(2,1)S(1)}, bf16[128,1024]{1,0:T(8,128)(2,1)S(1)}, u32[]{:S(2)}, u32[]{:S(2)}) collective-permute-start(bf16[128,1024]{1,0:T(8,128)(2,1)S(1)} %constant_dynamic-slice_fusion), channel_id=1, source_target_pairs={{0,2},{1,3},{2,0},{3,1},{4,6},{5,7},{6,4},{7,5},{8,10},{9,11},{10,... | collective-permute-start | bytes 786440 | tf_op jit(solution)/shard_map/ppermute | solution.py:321
  11.4 0.0 collective-permute-done.4.w_first_ref
  11.4 8.1 %collective-permute-start.5 = (bf16[256,1024]{1,0:T(8,128)(2,1)S(1)}, bf16[256,1024]{1,0:T(8,128)(2,1)S(1)}, u32[]{:S(2)}, u32[]{:S(2)}) collective-permute-start(bf16[256,1024]{1,0:T(8,128)(2,1)S(1)} %collective-permute-done.4.w_first_ref), channel_id=1, source_target_pairs={{0,4},{4,0},{8,12},{12,8},{16,20},{20,16},{24,28},{28,24},{32,36},... | collective-permute-start | bytes 1572872 | tf_op jit(solution)/shard_map/ppermute | solution.py:336
  19.5 0.0 collective-permute-done.before_ref
  19.5 0.0 copy-start.2
  19.5 0.0 copy-start.3
  19.5 1.0 shard_map.83.own_ref
  20.5 0.0 copy-start.1
  20.5 0.1 collective-permute-start.3
  20.6 0.1 collective-permute-start.2
  20.7 2.7 %collective-permute-start.1 = (bf16[512,256]{1,0:T(8,128)(2,1)S(1)}, bf16[512,256]{1,0:T(8,128)(2,1)S(1)}, u32[]{:S(2)}, u32[]{:S(2)}) collective-permute-start(bf16[512,256]{1,0:T(8,128)(2,1)S(1)} %shard_map.83.own_ref), channel_id=1, source_target_pairs={{0,1},{1,2},{2,3},{3,0},{4,7},{5,4},{6,5},{7,6},{8,9},{9,10},{10,1... | collective-permute-start | bytes 786440 | tf_op jit(solution)/shard_map/ppermute | solution.py:331
  23.4 0.0 collective-permute-done.6.w_far_mine_ref
  23.4 0.0 collective-permute-start.7
  23.4 0.0 copy-done.4
  23.4 0.0 copy-done.2
  23.4 0.0 copy-done.3
  23.4 0.7 shard_map.84
  24.1 5.9 %collective-permute-done.3.far_ref = bf16[512,256]{1,0:T(8,128)(2,1)S(1)} collective-permute-done((bf16[512,256]{1,0:T(8,128)(2,1)S(1)}, bf16[512,256]{1,0:T(8,128)(2,1)S(1)}, u32[]{:S(2)}, u32[]{:S(2)}) %collective-permute-start.3) | collective-permute-done | bytes 262176 | tf_op jit(solution)/shard_map/ppermute | solution.py:321
  30.0 5.5 %collective-permute-done.2.second_ref = bf16[512,256]{1,0:T(8,128)(2,1)S(1)} collective-permute-done((bf16[512,256]{1,0:T(8,128)(2,1)S(1)}, bf16[512,256]{1,0:T(8,128)(2,1)S(1)}, u32[]{:S(2)}, u32[]{:S(2)}) %collective-permute-start.2) | collective-permute-done | bytes 262176 | tf_op jit(solution)/shard_map/ppermute | solution.py:331
  35.6 0.0 collective-permute-done.1.first_ref
  35.6 0.0 collective-permute-done.7.w_far_other_ref
  35.6 0.0 collective-permute-done.5.w_second_ref
  35.6 0.0 copy-done.1
  35.6 2.4 %shard_map.85 = (bf16[512,1024]{1,0:T(8,128)(2,1)S(1)}, bf16[2,512,256]{2,1,0:T(8,128)(2,1)S(1)}) custom-call(s32[1]{0:T(128)} %bitcast.1.core_ref, bf16[512,1024]{1,0:T(8,128)(2,1)S(1)} %copy-done.1, bf16[512,256]{1,0:T(8,128)(2,1)S(1)} %shard_map.83.own_ref, bf16[512,256]{1,0:T(8,128)(2,1)S(1)} %collective-permute-done.1.first_ref, ...), custom_call_target="tpu_custom_call" | custom-call | flops 2147483648 | bytes 8388608 | tf_op jit(solution)/shard_map/pallas_call | solution.py:29
  38.1 25.1 %all_to_all.10 = bf16[64,16,256]{2,1,0:T(8,128)(2,1)S(1)} all-to-all(bf16[64,16,256]{2,1,0:T(8,128)(2,1)S(1)} %bitcast.11), channel_id=1, replica_groups=mesh['wide'=64,'narrow'=4] {'wide'}, dimensions={0} | all-to-all | bytes 1048576 | tf_op jit(solution)/shard_map/all_to_all | solution.py:417
  63.1 0.4 collective-permute-start.8
  63.5 0.1 pad_add_fusion.info_ref
  63.6 2.1 %shard_map.86 = (f32[1024,256]{1,0:T(8,128)S(1)}, f32[1024,128]{1,0:T(8,128)S(1)}) custom-call(s32[2]{0:T(128)S(1)} %pad_add_fusion.info_ref, bf16[1024,256]{1,0:T(8,128)(2,1)S(1)} %bitcast.9), custom_call_target="tpu_custom_call" | custom-call | flops 1073741824 | bytes 2097152 | tf_op jit(solution)/shard_map/pallas_call | solution.py:29
  65.7 0.0 collective-permute-done.8.other_ref
  65.7 2.9 %shard_map.87 = bf16[1024,128]{1,0:T(8,128)(2,1)} custom-call(s32[2]{0:T(128)S(1)} %pad_add_fusion.info_ref, bf16[1024,256]{1,0:T(8,128)(2,1)S(1)} %bitcast.10, bf16[1024,256]{1,0:T(8,128)(2,1)S(1)} %collective-permute-done.8.other_ref, f32[1024,256]{1,0:T(8,128)S(1)} %get-tuple-element.43.mixed_ref, f32[1024,128]{1,0:T(8,128)S(1)} %get-tuple-element.44.top_ref), custom_call_target="tpu_custom_call" | custom-call | flops 1073741824 | bytes 2097152 | tf_op jit(solution)/shard_map/pallas_call | solution.py:29
  68.6 0.0 copy-start.5
  68.6 5.6 %all-to-all-start.1 = ((bf16[64,16,128]{2,1,0:T(8,128)(2,1)}), bf16[64,16,128]{2,1,0:T(8,128)(2,1)S(1)}, u32[]{:S(2)}, u32[]{:S(2)}) async-start(bf16[64,16,128]{2,1,0:T(8,128)(2,1)} %bitcast.6), calls=%async_computation.1 | async-start | bytes 524288 | tf_op jit(solution)/shard_map/all_to_all | solution.py:439
  74.2 13.2 %all-to-all-done.1 = bf16[64,16,128]{2,1,0:T(8,128)(2,1)S(1)} async-done(((bf16[64,16,128]{2,1,0:T(8,128)(2,1)}), bf16[64,16,128]{2,1,0:T(8,128)(2,1)S(1)}, u32[]{:S(2)}, u32[]{:S(2)}) %all-to-all-start.1) | async-done | bytes 262176 | tf_op jit(solution)/shard_map/all_to_all | solution.py:439
  87.4 0.0 copy-done.5
  87.4 0.8 shard_map.88
  88.2 0.7 collective-permute-start.9
  88.9 2.3 %collective-permute-start.10 = (bf16[512,256]{1,0:T(8,128)(2,1)S(1)}, bf16[512,256]{1,0:T(8,128)(2,1)S(1)}, u32[]{:S(2)}, u32[]{:S(2)}) collective-permute-start(bf16[512,256]{1,0:T(8,128)(2,1)S(1)} %get-tuple-element.48), channel_id=1, source_target_pairs={{0,1},{1,2},{2,3},{3,0},{4,5},{5,6},{6,7},{7,4},{8,9},{9,10},{10,1... | collective-permute-start | bytes 786440 | tf_op jit(solution)/shard_map/ppermute | solution.py:321
  91.2 0.4 collective-permute-start.11
  91.6 5.9 %collective-permute-done.9.one_ref = bf16[512,256]{1,0:T(8,128)(2,1)S(1)} collective-permute-done((bf16[512,256]{1,0:T(8,128)(2,1)S(1)}, bf16[512,256]{1,0:T(8,128)(2,1)S(1)}, u32[]{:S(2)}, u32[]{:S(2)}) %collective-permute-start.9) | collective-permute-done | bytes 262176 | tf_op jit(solution)/shard_map/ppermute | solution.py:321
  97.5 6.2 %collective-permute-done.10.two_ref = bf16[512,256]{1,0:T(8,128)(2,1)S(1)} collective-permute-done((bf16[512,256]{1,0:T(8,128)(2,1)S(1)}, bf16[512,256]{1,0:T(8,128)(2,1)S(1)}, u32[]{:S(2)}, u32[]{:S(2)}) %collective-permute-start.10) | collective-permute-done | bytes 262176 | tf_op jit(solution)/shard_map/ppermute | solution.py:321
  103.6 0.0 collective-permute-done.11.three_ref
  103.6 1.0 shard_map.89
  (1 shorter events, 0.0 us)
Async XLA Ops:
  0.0 11.4 %collective-permute-start.4 = (bf16[256,1024]{1,0:T(8,128)(2,1)}, bf16[256,1024]{1,0:T(8,128)(2,1)S(1)}, u32[]{:S(2)}, u32[]{:S(2)}) collective-permute-start(bf16[256,1024]{1,0:T(8,128)(2,1)} %w_out_any), channel_id=1, source_target_pairs={{0,1},{1,2},{2,3},{3,0},{4,7},{5,4},{6,5},{7,6},{8,9},{9,10},{10,1... | collective-permute-start | bytes 1572872 | tf_op jit(solution)/shard_map/ppermute | solution.py:331
  3.3 2.7 %copy-start = (bf16[256,1024]{1,0:T(8,128)(2,1)S(1)}, bf16[256,1024]{1,0:T(8,128)(2,1)}, u32[]{:S(2)}) copy-start(bf16[256,1024]{1,0:T(8,128)(2,1)} %w_out_any) | copy-start | bytes 1572868
  6.0 17.3 %copy-start.4 = (s32[2,512]{1,0:T(2,128)S(1)}, s32[2,512]{1,0:T(2,128)}, u32[]{:S(2)}) copy-start(s32[2,512]{1,0:T(2,128)} %ids_any) | copy-start | bytes 12292
  6.1 13.4 %collective-permute-start = (bf16[2,256,256]{2,1,0:T(8,128)(2,1)S(1)}, bf16[2,256,256]{2,1,0:T(8,128)(2,1)S(1)}, u32[]{:S(2)}, u32[]{:S(2)}) collective-permute-start(bf16[2,256,256]{2,1,0:T(8,128)(2,1)S(1)} %get-tuple-element.31), channel_id=1, source_target_pairs={{0,4},{4,8},{8,12},{12,16},{16,20},{20,24},{24,28},{28,32},{32,36}... | collective-permute-start | bytes 786440 | tf_op jit(solution)/shard_map/ppermute | solution.py:372
  8.9 14.5 %collective-permute-start.6 = (bf16[128,1024]{1,0:T(8,128)(2,1)S(1)}, bf16[128,1024]{1,0:T(8,128)(2,1)S(1)}, u32[]{:S(2)}, u32[]{:S(2)}) collective-permute-start(bf16[128,1024]{1,0:T(8,128)(2,1)S(1)} %constant_dynamic-slice_fusion), channel_id=1, source_target_pairs={{0,2},{1,3},{2,0},{3,1},{4,6},{5,7},{6,4},{7,5},{8,10},{9,11},{10,... | collective-permute-start | bytes 786440 | tf_op jit(solution)/shard_map/ppermute | solution.py:321
  11.4 24.2 %collective-permute-start.5 = (bf16[256,1024]{1,0:T(8,128)(2,1)S(1)}, bf16[256,1024]{1,0:T(8,128)(2,1)S(1)}, u32[]{:S(2)}, u32[]{:S(2)}) collective-permute-start(bf16[256,1024]{1,0:T(8,128)(2,1)S(1)} %collective-permute-done.4.w_first_ref), channel_id=1, source_target_pairs={{0,4},{4,0},{8,12},{12,8},{16,20},{20,16},{24,28},{28,24},{32,36},... | collective-permute-start | bytes 1572872 | tf_op jit(solution)/shard_map/ppermute | solution.py:336
  19.5 3.9 %copy-start.2 = (bf16[1024,256]{1,0:T(8,128)(2,1)S(1)}, bf16[1024,256]{1,0:T(8,128)(2,1)}, u32[]{:S(2)}) copy-start(bf16[1024,256]{1,0:T(8,128)(2,1)} %w_qk_any.2) | copy-start | bytes 1572868
  19.5 3.9 %copy-start.3 = (bf16[1024,256]{1,0:T(8,128)(2,1)S(1)}, bf16[1024,256]{1,0:T(8,128)(2,1)}, u32[]{:S(2)}) copy-start(bf16[1024,256]{1,0:T(8,128)(2,1)} %w_value_any.2) | copy-start | bytes 1572868
  20.5 15.1 %copy-start.1 = (bf16[512,1024]{1,0:T(8,128)(2,1)S(1)}, bf16[512,1024]{1,0:T(8,128)(2,1)}, u32[]{:S(2)}) copy-start(bf16[512,1024]{1,0:T(8,128)(2,1)} %tokens_ref.1) | copy-start | bytes 3145732
  20.5 9.6 %collective-permute-start.3 = (bf16[512,256]{1,0:T(8,128)(2,1)S(1)}, bf16[512,256]{1,0:T(8,128)(2,1)S(1)}, u32[]{:S(2)}, u32[]{:S(2)}) collective-permute-start(bf16[512,256]{1,0:T(8,128)(2,1)S(1)} %shard_map.83.own_ref), channel_id=1, source_target_pairs={{0,2},{1,3},{2,0},{3,1},{4,6},{5,7},{6,4},{7,5},{8,10},{9,11},{10,... | collective-permute-start | bytes 786440 | tf_op jit(solution)/shard_map/ppermute | solution.py:321
  20.6 15.0 %collective-permute-start.2 = (bf16[512,256]{1,0:T(8,128)(2,1)S(1)}, bf16[512,256]{1,0:T(8,128)(2,1)S(1)}, u32[]{:S(2)}, u32[]{:S(2)}) collective-permute-start(bf16[512,256]{1,0:T(8,128)(2,1)S(1)} %shard_map.83.own_ref), channel_id=1, source_target_pairs={{0,3},{1,0},{2,1},{3,2},{4,5},{5,6},{6,7},{7,4},{8,11},{9,8},{10,9... | collective-permute-start | bytes 786440 | tf_op jit(solution)/shard_map/ppermute | solution.py:331
  20.7 14.9 %collective-permute-start.1 = (bf16[512,256]{1,0:T(8,128)(2,1)S(1)}, bf16[512,256]{1,0:T(8,128)(2,1)S(1)}, u32[]{:S(2)}, u32[]{:S(2)}) collective-permute-start(bf16[512,256]{1,0:T(8,128)(2,1)S(1)} %shard_map.83.own_ref), channel_id=1, source_target_pairs={{0,1},{1,2},{2,3},{3,0},{4,7},{5,4},{6,5},{7,6},{8,9},{9,10},{10,1... | collective-permute-start | bytes 786440 | tf_op jit(solution)/shard_map/ppermute | solution.py:331
  23.4 12.2 %collective-permute-start.7 = (bf16[128,1024]{1,0:T(8,128)(2,1)S(1)}, bf16[128,1024]{1,0:T(8,128)(2,1)S(1)}, u32[]{:S(2)}, u32[]{:S(2)}) collective-permute-start(bf16[128,1024]{1,0:T(8,128)(2,1)S(1)} %collective-permute-done.6.w_far_mine_ref), channel_id=1, source_target_pairs={{0,4},{4,0},{8,12},{12,8},{16,20},{20,16},{24,28},{28,24},{32,36},... | collective-permute-start | bytes 786440 | tf_op jit(solution)/shard_map/ppermute | solution.py:336
  63.1 2.6 %collective-permute-start.8 = (bf16[1024,256]{1,0:T(8,128)(2,1)S(1)}, bf16[1024,256]{1,0:T(8,128)(2,1)S(1)}, u32[]{:S(2)}, u32[]{:S(2)}) collective-permute-start(bf16[1024,256]{1,0:T(8,128)(2,1)S(1)} %bitcast.8), channel_id=1, source_target_pairs={{0,4},{4,0},{8,12},{12,8},{16,20},{20,16},{24,28},{28,24},{32,36},... | collective-permute-start | bytes 1572872 | tf_op jit(solution)/shard_map/ppermute | solution.py:336
  68.6 18.7 %copy-start.5 = (bf16[256,1024]{1,0:T(8,128)(2,1)S(1)}, bf16[256,1024]{1,0:T(8,128)(2,1)}, u32[]{:S(2)}) copy-start(bf16[256,1024]{1,0:T(8,128)(2,1)} %weight_ref.1) | copy-start | bytes 1572868
  68.6 18.7 %all-to-all-start.1 = ((bf16[64,16,128]{2,1,0:T(8,128)(2,1)}), bf16[64,16,128]{2,1,0:T(8,128)(2,1)S(1)}, u32[]{:S(2)}, u32[]{:S(2)}) async-start(bf16[64,16,128]{2,1,0:T(8,128)(2,1)} %bitcast.6), calls=%async_computation.1 | async-start | bytes 524288 | tf_op jit(solution)/shard_map/all_to_all | solution.py:439
  88.2 9.3 %collective-permute-start.9 = (bf16[512,256]{1,0:T(8,128)(2,1)S(1)}, bf16[512,256]{1,0:T(8,128)(2,1)S(1)}, u32[]{:S(2)}, u32[]{:S(2)}) collective-permute-start(bf16[512,256]{1,0:T(8,128)(2,1)S(1)} %get-tuple-element.47), channel_id=1, source_target_pairs={{0,2},{1,3},{2,0},{3,1},{4,6},{5,7},{6,4},{7,5},{8,10},{9,11},{10,... | collective-permute-start | bytes 786440 | tf_op jit(solution)/shard_map/ppermute | solution.py:321
  88.9 14.7 %collective-permute-start.10 = (bf16[512,256]{1,0:T(8,128)(2,1)S(1)}, bf16[512,256]{1,0:T(8,128)(2,1)S(1)}, u32[]{:S(2)}, u32[]{:S(2)}) collective-permute-start(bf16[512,256]{1,0:T(8,128)(2,1)S(1)} %get-tuple-element.48), channel_id=1, source_target_pairs={{0,1},{1,2},{2,3},{3,0},{4,5},{5,6},{6,7},{7,4},{8,9},{9,10},{10,1... | collective-permute-start | bytes 786440 | tf_op jit(solution)/shard_map/ppermute | solution.py:321
  91.2 12.4 %collective-permute-start.11 = (bf16[512,256]{1,0:T(8,128)(2,1)S(1)}, bf16[512,256]{1,0:T(8,128)(2,1)S(1)}, u32[]{:S(2)}, u32[]{:S(2)}) collective-permute-start(bf16[512,256]{1,0:T(8,128)(2,1)S(1)} %get-tuple-element.49), channel_id=1, source_target_pairs={{0,3},{1,0},{2,1},{3,2},{4,7},{5,4},{6,5},{7,6},{8,11},{9,8},{10,9... | collective-permute-start | bytes 786440 | tf_op jit(solution)/shard_map/ppermute | solution.py:321

commit v4 on v3

--- a/solution.py
+++ b/solution.py
@@ -22,6 +22,7 @@
 def call(
     body, outs, args, scratch=(), prefetch=0, flops=0, bytes_accessed=0, space=pltpu.VMEM,
     mib=20,
+    out_space=pltpu.VMEM,
 ):
     whole = [pl.BlockSpec(memory_space=pltpu.SMEM)] * prefetch + [
         pl.BlockSpec(memory_space=space)
@@ -30,7 +31,7 @@
         body,
         out_shape=outs,
         in_specs=whole,
-        out_specs=jax.tree.map(lambda _: pl.BlockSpec(memory_space=pltpu.VMEM), outs),
+        out_specs=jax.tree.map(lambda _: pl.BlockSpec(memory_space=out_space), outs),
         scratch_shapes=list(scratch),
         compiler_params=pltpu.CompilerParams(vmem_limit_bytes=mib * 2**20),
         cost_estimate=pl.CostEstimate(
@@ -94,23 +95,25 @@
     first_band = (jnp.logical_not(at_start) & band) | (at_start & opening)
     length = qk_ref.shape[0]
     ones = jnp.ones((2 * tile, HEAD_DIM), BF16)
+    pieces = []
     for head in range(2):
         cols = slice(head * HEAD_DIM, (head + 1) * HEAD_DIM)
         for part in range(length // tile):
-            query = qk_ref[part * tile : (part + 1) * tile, cols]
+            here = slice(part * tile, (part + 1) * tile)
+            query = qk_ref[here, cols]
             if part == 0:
                 keys = jnp.concatenate([before_ref[0, :, cols], query], axis=0)
                 values = jnp.concatenate([before_ref[1, :, cols], value_ref[:tile, cols]], axis=0)
             else:
                 keys = qk_ref[(part - 1) * tile : (part + 1) * tile, cols]
                 values = value_ref[(part - 1) * tile : (part + 1) * tile, cols]
-            scores = jnp.where(first_band if part == 0 else band, scores_of(query, keys), MASKED)
-            top = jnp.max(scores, axis=-1, keepdims=True)
-            weights = jnp.exp2((scores - top) * EXP2_FACTOR).astype(BF16)
-            mixed = matmul(weights, jnp.concatenate([values, ones], axis=1))
-            out_ref[part * tile : (part + 1) * tile, cols] = (
-                mixed[:, :HEAD_DIM] / mixed[:, HEAD_DIM:]
-            ).astype(BF16)
+            keep = first_band if part == 0 else band
+            scores = jnp.where(keep, scores_of(query, keys), MASKED)
+            pieces.append((here, cols, values, scores, jnp.max(scores, axis=-1, keepdims=True)))
+    for here, cols, values, scores, top in pieces:
+        weights = jnp.exp2((scores - top) * EXP2_FACTOR).astype(BF16)
+        mixed = matmul(weights, jnp.concatenate([values, ones], axis=1))
+        out_ref[here, cols] = (mixed[:, :HEAD_DIM] / mixed[:, HEAD_DIM:]).astype(BF16)
 
 
 def place_body(
@@ -167,37 +170,37 @@
         copy.wait()
 
 
+def begin_mixed_body(
+    core_ref, tokens_ref, own_ref, far_ref, w_own_ref, w_far_mine_ref, w_far_other_ref, started_ref
+):
+    even = core_ref[0] == 0
+    far_mine = w_far_mine_ref[...]
+    far_other = w_far_other_ref[...]
+    left_side = jnp.concatenate([own_ref[...], far_ref[...]], axis=1)
+    right_side = [
+        w_own_ref[...],
+        jnp.where(even, far_mine, far_other),
+        jnp.where(even, far_other, far_mine),
+    ]
+    mixed = matmul(left_side, jnp.concatenate(right_side, axis=0))
+    started_ref[...] = tokens_ref[...].astype(F32) + mixed
+
+
 def middle_body(
-    core_ref,
-    tokens_ref,
-    own_ref,
+    started_ref,
     first_ref,
     second_ref,
-    far_ref,
-    w_own_ref,
     w_first_ref,
     w_second_ref,
-    w_far_mine_ref,
-    w_far_other_ref,
     w_qk_ref,
     w_value_ref,
     place_ref,
     hidden_ref,
     out_ref,
 ):
-    even = core_ref[0] == 0
-    far_mine = w_far_mine_ref[...]
-    far_other = w_far_other_ref[...]
-    left_side = [own_ref[...], first_ref[...], second_ref[...], far_ref[...]]
-    right_side = [
-        w_own_ref[...],
-        w_first_ref[...],
-        w_second_ref[...],
-        jnp.where(even, far_mine, far_other),
-        jnp.where(even, far_other, far_mine),
-    ]
-    mixed = matmul(jnp.concatenate(left_side, axis=1), jnp.concatenate(right_side, axis=0))
-    hidden = (tokens_ref[...].astype(F32) + mixed).astype(BF16)
+    left_side = jnp.concatenate([first_ref[...], second_ref[...]], axis=1)
+    right_side = jnp.concatenate([w_first_ref[...], w_second_ref[...]], axis=0)
+    hidden = (started_ref[...] + matmul(left_side, right_side)).astype(BF16)
     hidden_ref[...] = hidden
     normed = rms_round(hidden.astype(F32))
     qk = matmul(normed, w_qk_ref[...]).astype(BF16)
@@ -260,12 +263,19 @@
     slot = (row & 15) + 16 * core
     opens = (slot == 0) | (jnp.logical_not(whole) & ((slot == 12) | (slot == 24)))
     alone = (row == col) & opens & (row < 16)
-    for part in range(mine_ref.shape[0] // tile):
+    parts = range(mine_ref.shape[0] // tile)
+    scored = [
+        side_scores(
+            mine_ref, mine_ref, part, tile, core, core, whole,
+            (earlier | alone) if part == 0 else earlier,
+        )
+        for part in parts
+    ]
+    tops = [row_tops(groups) for groups in scored]
+    for part in parts:
         here = slice(part * tile, (part + 1) * tile)
-        keep = (earlier | alone) if part == 0 else earlier
-        groups = side_scores(mine_ref, mine_ref, part, tile, core, core, whole, keep)
-        top = row_tops(groups)
-        mixed_ref[here, :] = weigh(groups, top, mine_ref, tile)
+        top = tops[part]
+        mixed_ref[here, :] = weigh(scored[part], top, mine_ref, tile)
         top_ref[here, :] = jnp.broadcast_to(top, (tile, HEAD_DIM))
 
 
@@ -276,13 +286,18 @@
     row = lax.broadcasted_iota(jnp.int32, (tile, tile), 0)
     col = lax.broadcasted_iota(jnp.int32, (tile, tile), 1)
     earlier = (col >> 4) < (row >> 4) + core
-    for part in range(mine_ref.shape[0] // tile):
+    parts = range(mine_ref.shape[0] // tile)
+    scored = [
+        side_scores(mine_ref, other_ref, part, tile, core, 1 - core, whole, earlier)
+        for part in parts
+    ]
+    tops = [row_tops(groups) for groups in scored]
+    for part in parts:
         here = slice(part * tile, (part + 1) * tile)
-        groups = side_scores(mine_ref, other_ref, part, tile, core, 1 - core, whole, earlier)
         own_top = top_ref[here, :]
-        top = jnp.maximum(jnp.broadcast_to(row_tops(groups), (tile, HEAD_DIM)), own_top)
+        top = jnp.maximum(jnp.broadcast_to(tops[part], (tile, HEAD_DIM)), own_top)
         shrink = jnp.exp2((own_top - top) * EXP2_FACTOR)
-        mixed = weigh(groups, jnp.concatenate([top, top], axis=1), other_ref, tile)
+        mixed = weigh(scored[part], jnp.concatenate([top, top], axis=1), other_ref, tile)
         total = mixed[:, HEAD_DIM:] + mixed_ref[here, HEAD_DIM:] * shrink
         sums = mixed[:, :HEAD_DIM] + mixed_ref[here, :HEAD_DIM] * shrink
         out_ref[here, :] = (sums / total).astype(BF16)
@@ -307,13 +322,25 @@
         target[...] = term.astype(target.dtype)
 
 
-def last_body(narrow_ref, own_ref, one_ref, two_ref, three_ref, hidden_ref, out_ref):
-    width = own_ref.shape[1]
+def last_body(
+    narrow_ref, own_ref, one_ref, two_ref, three_ref, hidden_ref, out_any, out_ref, sems
+):
+    length, width = own_ref.shape
     columns = pl.ds(pl.multiple_of(narrow_ref[0] * width, width), width)
-    mixed = own_ref[...].astype(F32)
-    for term_ref in (one_ref, two_ref, three_ref):
-        mixed += term_ref[...].astype(F32)
-    out_ref[...] = hidden_ref[:, columns].astype(F32) + mixed
+    parts = 4
+    step = length // parts
+    copies = []
+    for part in range(parts):
+        here = slice(part * step, (part + 1) * step)
+        mixed = own_ref[here, :].astype(F32)
+        for term_ref in (one_ref, two_ref, three_ref):
+            mixed += term_ref[here, :].astype(F32)
+        out_ref[here, :] = hidden_ref[here, columns].astype(F32) + mixed
+        copy = pltpu.make_async_copy(out_ref.at[here], out_any.at[here], sems.at[part])
+        copy.start()
+        copies.append(copy)
+    for copy in copies:
+        copy.wait()
 
 
 def around(value, steps):
@@ -401,15 +428,20 @@
         bytes_accessed=2**18,
         space=pltpu.HBM,
     )
+    started = call(
+        begin_mixed_body,
+        shape((length, width), F32),
+        (core.reshape(1), tokens, attended1, far, w_out1_near, w_far_mine, w_far_other),
+        prefetch=1,
+        flops=2**30,
+        bytes_accessed=2**22,
+    )
     hidden, outgoing = call(
         middle_body,
         (shape((length, width), BF16), shape((2, SLOTS, 2 * HEAD_DIM), BF16)),
         (
-            core.reshape(1), tokens, attended1, first, second, far,
-            w_out1_near, w_first, w_second, w_far_mine, w_far_other,
-            w_qk2_near, w_value2_near, place,
-        ),
-        prefetch=1,
+            started, first, second, w_first, w_second, w_qk2_near, w_value2_near, place,
+        ),
         flops=2**31,
         bytes_accessed=2**23,
     )
@@ -455,6 +487,11 @@
             narrow.reshape(1), own, around(to_far, 2), around(to_next, 1),
             around(to_last, -1), hidden,
         ),
+        scratch=(
+            pltpu.VMEM((length, group_width), F32),
+            pltpu.SemaphoreType.DMA((4,)),
+        ),
+        out_space=pl.ANY,
         prefetch=1,
         flops=2**22,
         bytes_accessed=2**21,

time: 105 us -> 103 us (0.981)
    ppermute x3, starting transfers between devices: 6.08 us -> 4.93 us  [around_by_core(): return lax.ppermute(value, ('wide', 'narrow'), pairs)]
    pallas_call x8 -> x9, Pallas kernels: 13.6 us -> 12.8 us  [call(): pl.pallas_call(body, out_shape=outs, in_specs=whole, out_specs=jax.tree.m...]
  transfers between devices with their start and end apart: 13 -> 13, of which waited for: 5 -> 5; matrix products, arithmetic and copies ran while one was open for 0% -> 0% of each run, Pallas kernels for 6% -> 7%
where the time goes in v4:
time: 103 us
  waiting for transfers between devices  37.3 us (36%)
  starting transfers between devices  28 us (27%)
  blocking collectives  24.7 us (24%)
  Pallas kernels  12.8 us (12%)
    all_to_all x1, blocking collectives, shards(): lax.all_to_all(outgoing.reshape(wide_count, per_pair, 2 * HEAD_DIM), 'wid...  24.7 us
    ppermute x5, waiting for transfers between devices, around(): lax.ppermute(value, 'narrow', [(i, (i + steps) % count) for i in range(co...  19 us
    all_to_all x1, waiting for transfers between devices, shards(): lax.all_to_all(answers.reshape(wide_count, per_pair, HEAD_DIM), 'wide', 0...  13.2 us
    pallas_call x9, Pallas kernels, call(): pl.pallas_call(body, out_shape=outs, in_specs=whole, out_specs=jax.tree.m...  12.8 us
    ppermute x3, starting transfers between devices, swap_cores(): return lax.ppermute(value, 'wide', [(i, i ^ 1) for i in range(count)])  8.45 us
    ppermute x5, starting transfers between devices, around(): lax.ppermute(value, 'narrow', [(i, (i + steps) % count) for i in range(co...  6.21 us
    all_to_all x1, starting transfers between devices, shards(): lax.all_to_all(answers.reshape(wide_count, per_pair, HEAD_DIM), 'wide', 0...  5.46 us
    ppermute x3, waiting for transfers between devices, around_by_core(): return lax.ppermute(value, ('wide', 'narrow'), pairs)  5.2 us
  transfers between devices with their start and end apart: 13, of which 5 were waited for; matrix products, arithmetic and copies ran while one was open for 0% of the time, Pallas kernels for 7%

profile of v4, /device:TPU:1, one launch (start us, length us, event | category | flops | bytes accessed | tf_op | source)
XLA Modules:
  0.0 103.2 jit_solution(13975077540071941006)
XLA Ops:
  0.0 0.0 copy-start.1
  0.0 0.0 copy-start.4
  0.0 0.0 copy-start.3
  0.0 3.4 %collective-permute-start.6 = (bf16[256,1024]{1,0:T(8,128)(2,1)}, bf16[256,1024]{1,0:T(8,128)(2,1)S(1)}, u32[]{:S(2)}, u32[]{:S(2)}) collective-permute-start(bf16[256,1024]{1,0:T(8,128)(2,1)} %w_out_any), channel_id=1, source_target_pairs={{0,1},{1,2},{2,3},{3,0},{4,7},{5,4},{6,5},{7,6},{8,9},{9,10},{10,1... | collective-permute-start | bytes 1572872 | tf_op jit(solution)/shard_map/ppermute | solution.py:358
  3.4 2.6 %shard_map.82 = (bf16[512,256]{1,0:T(8,128)(2,1)S(1)}, bf16[512,256]{1,0:T(8,128)(2,1)S(1)}, bf16[2,256,256]{2,1,0:T(8,128)(2,1)S(1)}) custom-call(bf16[512,1024]{1,0:T(8,128)(2,1)} %tokens_ref.1, bf16[1024,256]{1,0:T(8,128)(2,1)} %w_qk_any.1, bf16[1024,256]{1,0:T(8,128)(2,1)} %w_value_any.1), custom_call_target="tpu_custom_call" | custom-call | flops 536870912 | bytes 3145728 | tf_op jit(solution)/shard_map/pallas_call | solution.py:30
  6.1 0.0 copy-done.1
  6.1 0.0 copy-start
  6.1 2.9 %collective-permute-start = (bf16[2,256,256]{2,1,0:T(8,128)(2,1)S(1)}, bf16[2,256,256]{2,1,0:T(8,128)(2,1)S(1)}, u32[]{:S(2)}, u32[]{:S(2)}) collective-permute-start(bf16[2,256,256]{2,1,0:T(8,128)(2,1)S(1)} %get-tuple-element.31), channel_id=1, source_target_pairs={{0,4},{4,8},{8,12},{12,16},{16,20},{20,24},{24,28},{28,32},{32,36}... | collective-permute-start | bytes 786440 | tf_op jit(solution)/shard_map/ppermute | solution.py:399
  9.0 2.5 %collective-permute-start.2 = (bf16[128,1024]{1,0:T(8,128)(2,1)S(1)}, bf16[128,1024]{1,0:T(8,128)(2,1)S(1)}, u32[]{:S(2)}, u32[]{:S(2)}) collective-permute-start(bf16[128,1024]{1,0:T(8,128)(2,1)S(1)} %constant_dynamic-slice_fusion), channel_id=1, source_target_pairs={{0,2},{1,3},{2,0},{3,1},{4,6},{5,7},{6,4},{7,5},{8,10},{9,11},{10,... | collective-permute-start | bytes 786440 | tf_op jit(solution)/shard_map/ppermute | solution.py:348
  11.6 0.0 collective-permute-done.6.w_first_ref
  11.6 8.0 %collective-permute-start.7 = (bf16[256,1024]{1,0:T(8,128)(2,1)S(1)}, bf16[256,1024]{1,0:T(8,128)(2,1)S(1)}, u32[]{:S(2)}, u32[]{:S(2)}) collective-permute-start(bf16[256,1024]{1,0:T(8,128)(2,1)S(1)} %collective-permute-done.6.w_first_ref), channel_id=1, source_target_pairs={{0,4},{4,0},{8,12},{12,8},{16,20},{20,16},{24,28},{28,24},{32,36},... | collective-permute-start | bytes 1572872 | tf_op jit(solution)/shard_map/ppermute | solution.py:363
  19.5 0.0 collective-permute-done.before_ref
  19.5 0.9 shard_map.83.own_ref
  20.5 0.1 collective-permute-start.1
  20.6 0.0 collective-permute-done.2.w_far_mine_ref
  20.6 0.1 collective-permute-start.3
  20.7 0.4 collective-permute-start.4
  21.1 1.1 %collective-permute-start.5 = (bf16[512,256]{1,0:T(8,128)(2,1)S(1)}, bf16[512,256]{1,0:T(8,128)(2,1)S(1)}, u32[]{:S(2)}, u32[]{:S(2)}) collective-permute-start(bf16[512,256]{1,0:T(8,128)(2,1)S(1)} %shard_map.83.own_ref), channel_id=1, source_target_pairs={{0,3},{1,0},{2,1},{3,2},{4,5},{5,6},{6,7},{7,4},{8,11},{9,8},{10,9... | collective-permute-start | bytes 786440 | tf_op jit(solution)/shard_map/ppermute | solution.py:358
  22.3 0.0 copy-done.4
  22.3 0.0 copy-done.2
  22.3 0.0 copy-done.3
  22.3 0.7 shard_map.84
  23.0 7.1 %collective-permute-done.1.far_ref = bf16[512,256]{1,0:T(8,128)(2,1)S(1)} collective-permute-done((bf16[512,256]{1,0:T(8,128)(2,1)S(1)}, bf16[512,256]{1,0:T(8,128)(2,1)S(1)}, u32[]{:S(2)}, u32[]{:S(2)}) %collective-permute-start.1) | collective-permute-done | bytes 262176 | tf_op jit(solution)/shard_map/ppermute | solution.py:348
  30.1 0.0 collective-permute-done.3.w_far_other_ref
  30.1 0.0 copy-done
  30.1 0.7 shard_map.85.started_ref
  30.8 0.0 collective-permute-done.4.first_ref
  30.8 5.2 %collective-permute-done.5.second_ref = bf16[512,256]{1,0:T(8,128)(2,1)S(1)} collective-permute-done((bf16[512,256]{1,0:T(8,128)(2,1)S(1)}, bf16[512,256]{1,0:T(8,128)(2,1)S(1)}, u32[]{:S(2)}, u32[]{:S(2)}) %collective-permute-start.5) | collective-permute-done | bytes 262176 | tf_op jit(solution)/shard_map/ppermute | solution.py:358
  36.0 0.0 collective-permute-done.7.w_second_ref
  36.0 1.9 %shard_map.86 = (bf16[512,1024]{1,0:T(8,128)(2,1)S(1)}, bf16[2,512,256]{2,1,0:T(8,128)(2,1)S(1)}) custom-call(f32[512,1024]{1,0:T(8,128)S(1)} %shard_map.85.started_ref, bf16[512,256]{1,0:T(8,128)(2,1)S(1)} %collective-permute-done.4.first_ref, bf16[512,256]{1,0:T(8,128)(2,1)S(1)} %collective-permute-done.5.second_ref, ...), custom_call_target="tpu_custom_call" | custom-call | flops 2147483648 | bytes 8388608 | tf_op jit(solution)/shard_map/pallas_call | solution.py:30
  37.9 24.7 %all_to_all.10 = bf16[64,16,256]{2,1,0:T(8,128)(2,1)S(1)} all-to-all(bf16[64,16,256]{2,1,0:T(8,128)(2,1)S(1)} %bitcast.11), channel_id=1, replica_groups=mesh['wide'=64,'narrow'=4] {'wide'}, dimensions={0} | all-to-all | bytes 1048576 | tf_op jit(solution)/shard_map/all_to_all | solution.py:449
  62.6 0.4 collective-permute-start.8
  63.0 0.1 pad_add_fusion.info_ref
  63.0 1.7 %shard_map.87 = (f32[1024,256]{1,0:T(8,128)S(1)}, f32[1024,128]{1,0:T(8,128)S(1)}) custom-call(s32[2]{0:T(128)S(1)} %pad_add_fusion.info_ref, bf16[1024,256]{1,0:T(8,128)(2,1)S(1)} %bitcast.9), custom_call_target="tpu_custom_call" | custom-call | flops 1073741824 | bytes 2097152 | tf_op jit(solution)/shard_map/pallas_call | solution.py:30
  64.8 0.0 collective-permute-done.8.other_ref
  64.8 0.0 copy-start.5
  64.8 2.5 %shard_map.88 = bf16[1024,128]{1,0:T(8,128)(2,1)} custom-call(s32[2]{0:T(128)S(1)} %pad_add_fusion.info_ref, bf16[1024,256]{1,0:T(8,128)(2,1)S(1)} %bitcast.10, bf16[1024,256]{1,0:T(8,128)(2,1)S(1)} %collective-permute-done.8.other_ref, f32[1024,256]{1,0:T(8,128)S(1)} %get-tuple-element.43.mixed_ref, f32[1024,128]{1,0:T(8,128)S(1)} %get-tuple-element.44.top_ref), custom_call_target="tpu_custom_call" | custom-call | flops 1073741824 | bytes 2097152 | tf_op jit(solution)/shard_map/pallas_call | solution.py:30
  67.3 5.5 %all-to-all-start.1 = ((bf16[64,16,128]{2,1,0:T(8,128)(2,1)}), bf16[64,16,128]{2,1,0:T(8,128)(2,1)S(1)}, u32[]{:S(2)}, u32[]{:S(2)}) async-start(bf16[64,16,128]{2,1,0:T(8,128)(2,1)} %bitcast.6), calls=%async_computation.1 | async-start | bytes 524288 | tf_op jit(solution)/shard_map/all_to_all | solution.py:471
  72.7 13.2 %all-to-all-done.1 = bf16[64,16,128]{2,1,0:T(8,128)(2,1)S(1)} async-done(((bf16[64,16,128]{2,1,0:T(8,128)(2,1)}), bf16[64,16,128]{2,1,0:T(8,128)(2,1)S(1)}, u32[]{:S(2)}, u32[]{:S(2)}) %all-to-all-start.1) | async-done | bytes 262176 | tf_op jit(solution)/shard_map/all_to_all | solution.py:471
  85.9 0.0 copy-done.5
  85.9 0.8 shard_map.89
  86.7 0.9 collective-permute-start.9
  87.6 2.1 %collective-permute-start.10 = (bf16[512,256]{1,0:T(8,128)(2,1)S(1)}, bf16[512,256]{1,0:T(8,128)(2,1)S(1)}, u32[]{:S(2)}, u32[]{:S(2)}) collective-permute-start(bf16[512,256]{1,0:T(8,128)(2,1)S(1)} %get-tuple-element.48), channel_id=1, source_target_pairs={{0,1},{1,2},{2,3},{3,0},{4,5},{5,6},{6,7},{7,4},{8,9},{9,10},{10,1... | collective-permute-start | bytes 786440 | tf_op jit(solution)/shard_map/ppermute | solution.py:348
  89.7 0.6 collective-permute-start.11
  90.3 5.7 %collective-permute-done.9.one_ref = bf16[512,256]{1,0:T(8,128)(2,1)S(1)} collective-permute-done((bf16[512,256]{1,0:T(8,128)(2,1)S(1)}, bf16[512,256]{1,0:T(8,128)(2,1)S(1)}, u32[]{:S(2)}, u32[]{:S(2)}) %collective-permute-start.9) | collective-permute-done | bytes 262176 | tf_op jit(solution)/shard_map/ppermute | solution.py:348
  96.0 6.2 %collective-permute-done.10.two_ref = bf16[512,256]{1,0:T(8,128)(2,1)S(1)} collective-permute-done((bf16[512,256]{1,0:T(8,128)(2,1)S(1)}, bf16[512,256]{1,0:T(8,128)(2,1)S(1)}, u32[]{:S(2)}, u32[]{:S(2)}) %collective-permute-start.10) | collective-permute-done | bytes 262176 | tf_op jit(solution)/shard_map/ppermute | solution.py:348
  102.2 0.0 collective-permute-done.11.three_ref
  102.2 0.9 shard_map.90
  (2 shorter events, 0.0 us)
Async XLA Ops:
  0.0 6.1 %copy-start.1 = (bf16[256,1024]{1,0:T(8,128)(2,1)S(1)}, bf16[256,1024]{1,0:T(8,128)(2,1)}, u32[]{:S(2)}) copy-start(bf16[256,1024]{1,0:T(8,128)(2,1)} %w_out_any) | copy-start | bytes 1572868
  0.0 22.2 %copy-start.4 = (s32[2,512]{1,0:T(2,128)S(1)}, s32[2,512]{1,0:T(2,128)}, u32[]{:S(2)}) copy-start(s32[2,512]{1,0:T(2,128)} %ids_any) | copy-start | bytes 12292
  0.0 22.3 %copy-start.2 = (bf16[1024,256]{1,0:T(8,128)(2,1)S(1)}, bf16[1024,256]{1,0:T(8,128)(2,1)}, u32[]{:S(2)}) copy-start(bf16[1024,256]{1,0:T(8,128)(2,1)} %w_qk_any.2) | copy-start | bytes 1572868
  0.0 22.2 %copy-start.3 = (bf16[1024,256]{1,0:T(8,128)(2,1)S(1)}, bf16[1024,256]{1,0:T(8,128)(2,1)}, u32[]{:S(2)}) copy-start(bf16[1024,256]{1,0:T(8,128)(2,1)} %w_value_any.2) | copy-start | bytes 1572868
  0.0 11.6 %collective-permute-start.6 = (bf16[256,1024]{1,0:T(8,128)(2,1)}, bf16[256,1024]{1,0:T(8,128)(2,1)S(1)}, u32[]{:S(2)}, u32[]{:S(2)}) collective-permute-start(bf16[256,1024]{1,0:T(8,128)(2,1)} %w_out_any), channel_id=1, source_target_pairs={{0,1},{1,2},{2,3},{3,0},{4,7},{5,4},{6,5},{7,6},{8,9},{9,10},{10,1... | collective-permute-start | bytes 1572872 | tf_op jit(solution)/shard_map/ppermute | solution.py:358
  6.1 24.0 %copy-start = (bf16[512,1024]{1,0:T(8,128)(2,1)S(1)}, bf16[512,1024]{1,0:T(8,128)(2,1)}, u32[]{:S(2)}) copy-start(bf16[512,1024]{1,0:T(8,128)(2,1)} %tokens_ref.1) | copy-start | bytes 3145732
  6.1 13.4 %collective-permute-start = (bf16[2,256,256]{2,1,0:T(8,128)(2,1)S(1)}, bf16[2,256,256]{2,1,0:T(8,128)(2,1)S(1)}, u32[]{:S(2)}, u32[]{:S(2)}) collective-permute-start(bf16[2,256,256]{2,1,0:T(8,128)(2,1)S(1)} %get-tuple-element.31), channel_id=1, source_target_pairs={{0,4},{4,8},{8,12},{12,16},{16,20},{20,24},{24,28},{28,32},{32,36}... | collective-permute-start | bytes 786440 | tf_op jit(solution)/shard_map/ppermute | solution.py:399
  9.0 11.6 %collective-permute-start.2 = (bf16[128,1024]{1,0:T(8,128)(2,1)S(1)}, bf16[128,1024]{1,0:T(8,128)(2,1)S(1)}, u32[]{:S(2)}, u32[]{:S(2)}) collective-permute-start(bf16[128,1024]{1,0:T(8,128)(2,1)S(1)} %constant_dynamic-slice_fusion), channel_id=1, source_target_pairs={{0,2},{1,3},{2,0},{3,1},{4,6},{5,7},{6,4},{7,5},{8,10},{9,11},{10,... | collective-permute-start | bytes 786440 | tf_op jit(solution)/shard_map/ppermute | solution.py:348
  11.6 24.4 %collective-permute-start.7 = (bf16[256,1024]{1,0:T(8,128)(2,1)S(1)}, bf16[256,1024]{1,0:T(8,128)(2,1)S(1)}, u32[]{:S(2)}, u32[]{:S(2)}) collective-permute-start(bf16[256,1024]{1,0:T(8,128)(2,1)S(1)} %collective-permute-done.6.w_first_ref), channel_id=1, source_target_pairs={{0,4},{4,0},{8,12},{12,8},{16,20},{20,16},{24,28},{28,24},{32,36},... | collective-permute-start | bytes 1572872 | tf_op jit(solution)/shard_map/ppermute | solution.py:363
  20.5 9.6 %collective-permute-start.1 = (bf16[512,256]{1,0:T(8,128)(2,1)S(1)}, bf16[512,256]{1,0:T(8,128)(2,1)S(1)}, u32[]{:S(2)}, u32[]{:S(2)}) collective-permute-start(bf16[512,256]{1,0:T(8,128)(2,1)S(1)} %shard_map.83.own_ref), channel_id=1, source_target_pairs={{0,2},{1,3},{2,0},{3,1},{4,6},{5,7},{6,4},{7,5},{8,10},{9,11},{10,... | collective-permute-start | bytes 786440 | tf_op jit(solution)/shard_map/ppermute | solution.py:348
  20.6 9.5 %collective-permute-start.3 = (bf16[128,1024]{1,0:T(8,128)(2,1)S(1)}, bf16[128,1024]{1,0:T(8,128)(2,1)S(1)}, u32[]{:S(2)}, u32[]{:S(2)}) collective-permute-start(bf16[128,1024]{1,0:T(8,128)(2,1)S(1)} %collective-permute-done.2.w_far_mine_ref), channel_id=1, source_target_pairs={{0,4},{4,0},{8,12},{12,8},{16,20},{20,16},{24,28},{28,24},{32,36},... | collective-permute-start | bytes 786440 | tf_op jit(solution)/shard_map/ppermute | solution.py:363
  20.7 10.1 %collective-permute-start.4 = (bf16[512,256]{1,0:T(8,128)(2,1)S(1)}, bf16[512,256]{1,0:T(8,128)(2,1)S(1)}, u32[]{:S(2)}, u32[]{:S(2)}) collective-permute-start(bf16[512,256]{1,0:T(8,128)(2,1)S(1)} %shard_map.83.own_ref), channel_id=1, source_target_pairs={{0,1},{1,2},{2,3},{3,0},{4,7},{5,4},{6,5},{7,6},{8,9},{9,10},{10,1... | collective-permute-start | bytes 786440 | tf_op jit(solution)/shard_map/ppermute | solution.py:358
  21.1 14.9 %collective-permute-start.5 = (bf16[512,256]{1,0:T(8,128)(2,1)S(1)}, bf16[512,256]{1,0:T(8,128)(2,1)S(1)}, u32[]{:S(2)}, u32[]{:S(2)}) collective-permute-start(bf16[512,256]{1,0:T(8,128)(2,1)S(1)} %shard_map.83.own_ref), channel_id=1, source_target_pairs={{0,3},{1,0},{2,1},{3,2},{4,5},{5,6},{6,7},{7,4},{8,11},{9,8},{10,9... | collective-permute-start | bytes 786440 | tf_op jit(solution)/shard_map/ppermute | solution.py:358
  62.6 2.2 %collective-permute-start.8 = (bf16[1024,256]{1,0:T(8,128)(2,1)S(1)}, bf16[1024,256]{1,0:T(8,128)(2,1)S(1)}, u32[]{:S(2)}, u32[]{:S(2)}) collective-permute-start(bf16[1024,256]{1,0:T(8,128)(2,1)S(1)} %bitcast.8), channel_id=1, source_target_pairs={{0,4},{4,0},{8,12},{12,8},{16,20},{20,16},{24,28},{28,24},{32,36},... | collective-permute-start | bytes 1572872 | tf_op jit(solution)/shard_map/ppermute | solution.py:363
  64.8 21.1 %copy-start.5 = (bf16[256,1024]{1,0:T(8,128)(2,1)S(1)}, bf16[256,1024]{1,0:T(8,128)(2,1)}, u32[]{:S(2)}) copy-start(bf16[256,1024]{1,0:T(8,128)(2,1)} %weight_ref.1) | copy-start | bytes 1572868
  67.3 18.6 %all-to-all-start.1 = ((bf16[64,16,128]{2,1,0:T(8,128)(2,1)}), bf16[64,16,128]{2,1,0:T(8,128)(2,1)S(1)}, u32[]{:S(2)}, u32[]{:S(2)}) async-start(bf16[64,16,128]{2,1,0:T(8,128)(2,1)} %bitcast.6), calls=%async_computation.1 | async-start | bytes 524288 | tf_op jit(solution)/shard_map/all_to_all | solution.py:471
  86.7 9.3 %collective-permute-start.9 = (bf16[512,256]{1,0:T(8,128)(2,1)S(1)}, bf16[512,256]{1,0:T(8,128)(2,1)S(1)}, u32[]{:S(2)}, u32[]{:S(2)}) collective-permute-start(bf16[512,256]{1,0:T(8,128)(2,1)S(1)} %get-tuple-element.47), channel_id=1, source_target_pairs={{0,2},{1,3},{2,0},{3,1},{4,6},{5,7},{6,4},{7,5},{8,10},{9,11},{10,... | collective-permute-start | bytes 786440 | tf_op jit(solution)/shard_map/ppermute | solution.py:348
  87.6 14.5 %collective-permute-start.10 = (bf16[512,256]{1,0:T(8,128)(2,1)S(1)}, bf16[512,256]{1,0:T(8,128)(2,1)S(1)}, u32[]{:S(2)}, u32[]{:S(2)}) collective-permute-start(bf16[512,256]{1,0:T(8,128)(2,1)S(1)} %get-tuple-element.48), channel_id=1, source_target_pairs={{0,1},{1,2},{2,3},{3,0},{4,5},{5,6},{6,7},{7,4},{8,9},{9,10},{10,1... | collective-permute-start | bytes 786440 | tf_op jit(solution)/shard_map/ppermute | solution.py:348
  89.7 12.4 %collective-permute-start.11 = (bf16[512,256]{1,0:T(8,128)(2,1)S(1)}, bf16[512,256]{1,0:T(8,128)(2,1)S(1)}, u32[]{:S(2)}, u32[]{:S(2)}) collective-permute-start(bf16[512,256]{1,0:T(8,128)(2,1)S(1)} %get-tuple-element.49), channel_id=1, source_target_pairs={{0,3},{1,0},{2,1},{3,2},{4,7},{5,4},{6,5},{7,6},{8,11},{9,8},{10,9... | collective-permute-start | bytes 786440 | tf_op jit(solution)/shard_map/ppermute | solution.py:348

commit v5 on v4

--- a/solution.py
+++ b/solution.py
@@ -402,7 +402,7 @@
         shape((length, group_width), BF16),
         (wide.reshape(1), qk1, value1, before),
         prefetch=1,
-        flops=2**28,
+        flops=2**20,
         bytes_accessed=2**20,
     )
     attended1, cluster_ids, w_out1_later, w_qk2, w_value2 = lax.optimization_barrier(
@@ -424,7 +424,7 @@
         ),
         (cluster_ids, w_out1_later, w_qk2, w_value2),
         scratch=(pltpu.VMEM((2, length), jnp.int32), pltpu.SemaphoreType.DMA((4,))),
-        flops=2**26,
+        flops=2**33,
         bytes_accessed=2**18,
         space=pltpu.HBM,
     )
@@ -433,7 +433,7 @@
         shape((length, width), F32),
         (core.reshape(1), tokens, attended1, far, w_out1_near, w_far_mine, w_far_other),
         prefetch=1,
-        flops=2**30,
+        flops=2**20,
         bytes_accessed=2**22,
     )
     hidden, outgoing = call(

time: 103 us -> 102 us (level)
  waiting for transfers between devices: 37.3 us -> 29.6 us
  blocking collectives: 24.7 us -> 29.1 us
  starting transfers between devices: 28 us -> 29.9 us
    ppermute x5, waiting for transfers between devices: 19 us -> 12.2 us  [around(): lax.ppermute(value, 'narrow', [(i, (i + steps) % count) for i in range(co...]
    all_to_all x1, blocking collectives: 24.7 us -> 29.1 us  [shards(): lax.all_to_all(outgoing.reshape(wide_count, per_pair, 2 * HEAD_DIM), 'wid...]
    ppermute x5, starting transfers between devices: 6.21 us -> 9.86 us  [around(): lax.ppermute(value, 'narrow', [(i, (i + steps) % count) for i in range(co...]
    ppermute x3, waiting for transfers between devices: 5.2 us -> 3.42 us  [around_by_core(): return lax.ppermute(value, ('wide', 'narrow'), pairs)]
    ppermute x3, starting transfers between devices: 8.45 us -> 6.96 us  [swap_cores(): return lax.ppermute(value, 'wide', [(i, i ^ 1) for i in range(count)])]
  transfers between devices with their start and end apart: 13 -> 13, of which waited for: 5 -> 7; matrix products, arithmetic and copies ran while one was open for 0% -> 0% of each run, Pallas kernels for 7% -> 7%
where the time goes in v5:
time: 102 us
  starting transfers between devices  29.9 us (29%)
  waiting for transfers between devices  29.6 us (29%)
  blocking collectives  29.1 us (29%)
  Pallas kernels  12.8 us (13%)
    all_to_all x1, blocking collectives, shards(): lax.all_to_all(outgoing.reshape(wide_count, per_pair, 2 * HEAD_DIM), 'wid...  29.1 us
    all_to_all x1, waiting for transfers between devices, shards(): lax.all_to_all(answers.reshape(wide_count, per_pair, HEAD_DIM), 'wide', 0...  13.2 us
    pallas_call x9, Pallas kernels, call(): pl.pallas_call(body, out_shape=outs, in_specs=whole, out_specs=jax.tree.m...  12.8 us
    ppermute x5, waiting for transfers between devices, around(): lax.ppermute(value, 'narrow', [(i, (i + steps) % count) for i in range(co...  12.2 us
    ppermute x5, starting transfers between devices, around(): lax.ppermute(value, 'narrow', [(i, (i + steps) % count) for i in range(co...  9.86 us
    ppermute x3, starting transfers between devices, swap_cores(): return lax.ppermute(value, 'wide', [(i, i ^ 1) for i in range(count)])  6.96 us
    all_to_all x1, starting transfers between devices, shards(): lax.all_to_all(answers.reshape(wide_count, per_pair, HEAD_DIM), 'wide', 0...  5.43 us
    ppermute x3, starting transfers between devices, around_by_core(): return lax.ppermute(value, ('wide', 'narrow'), pairs)  4.85 us
  transfers between devices with their start and end apart: 13, of which 7 were waited for; matrix products, arithmetic and copies ran while one was open for 0% of the time, Pallas kernels for 7%

profile of v5, /device:TPU:1, one launch (start us, length us, event | category | flops | bytes accessed | tf_op | source)
XLA Modules:
  0.0 101.8 jit_solution(5174717017989107190)
XLA Ops:
  0.0 0.0 copy-start.1
  0.0 0.0 copy-start.5
  0.0 0.0 copy-start.3
  0.0 3.4 %collective-permute-start.6 = (bf16[256,1024]{1,0:T(8,128)(2,1)}, bf16[256,1024]{1,0:T(8,128)(2,1)S(1)}, u32[]{:S(2)}, u32[]{:S(2)}) collective-permute-start(bf16[256,1024]{1,0:T(8,128)(2,1)} %w_out_any), channel_id=1, source_target_pairs={{0,1},{1,2},{2,3},{3,0},{4,7},{5,4},{6,5},{7,6},{8,9},{9,10},{10,1... | collective-permute-start | bytes 1572872 | tf_op jit(solution)/shard_map/ppermute | solution.py:358
  3.4 2.6 %shard_map.82 = (bf16[512,256]{1,0:T(8,128)(2,1)S(1)}, bf16[512,256]{1,0:T(8,128)(2,1)S(1)}, bf16[2,256,256]{2,1,0:T(8,128)(2,1)S(1)}) custom-call(bf16[512,1024]{1,0:T(8,128)(2,1)} %tokens_ref.1, bf16[1024,256]{1,0:T(8,128)(2,1)} %w_qk_any.1, bf16[1024,256]{1,0:T(8,128)(2,1)} %w_value_any.1), custom_call_target="tpu_custom_call" | custom-call | flops 536870912 | bytes 3145728 | tf_op jit(solution)/shard_map/pallas_call | solution.py:30
  6.1 0.0 copy-done.1
  6.1 2.8 %collective-permute-start = (bf16[2,256,256]{2,1,0:T(8,128)(2,1)S(1)}, bf16[2,256,256]{2,1,0:T(8,128)(2,1)S(1)}, u32[]{:S(2)}, u32[]{:S(2)}) collective-permute-start(bf16[2,256,256]{2,1,0:T(8,128)(2,1)S(1)} %get-tuple-element.31), channel_id=1, source_target_pairs={{0,4},{4,8},{8,12},{12,16},{16,20},{20,24},{24,28},{28,32},{32,36}... | collective-permute-start | bytes 786440 | tf_op jit(solution)/shard_map/ppermute | solution.py:399
  8.9 2.5 %collective-permute-start.2 = (bf16[128,1024]{1,0:T(8,128)(2,1)S(1)}, bf16[128,1024]{1,0:T(8,128)(2,1)S(1)}, u32[]{:S(2)}, u32[]{:S(2)}) collective-permute-start(bf16[128,1024]{1,0:T(8,128)(2,1)S(1)} %constant_dynamic-slice_fusion), channel_id=1, source_target_pairs={{0,2},{1,3},{2,0},{3,1},{4,6},{5,7},{6,4},{7,5},{8,10},{9,11},{10,... | collective-permute-start | bytes 786440 | tf_op jit(solution)/shard_map/ppermute | solution.py:348
  11.4 0.8 collective-permute-done.before_ref
  12.2 0.9 shard_map.83.own_ref
  13.1 0.0 copy-start
  13.1 2.5 %collective-permute-start.1 = (bf16[512,256]{1,0:T(8,128)(2,1)S(1)}, bf16[512,256]{1,0:T(8,128)(2,1)S(1)}, u32[]{:S(2)}, u32[]{:S(2)}) collective-permute-start(bf16[512,256]{1,0:T(8,128)(2,1)S(1)} %shard_map.83.own_ref), channel_id=1, source_target_pairs={{0,2},{1,3},{2,0},{3,1},{4,6},{5,7},{6,4},{7,5},{8,10},{9,11},{10,... | collective-permute-start | bytes 786440 | tf_op jit(solution)/shard_map/ppermute | solution.py:348
  15.7 1.2 %collective-permute-start.4 = (bf16[512,256]{1,0:T(8,128)(2,1)S(1)}, bf16[512,256]{1,0:T(8,128)(2,1)S(1)}, u32[]{:S(2)}, u32[]{:S(2)}) collective-permute-start(bf16[512,256]{1,0:T(8,128)(2,1)S(1)} %shard_map.83.own_ref), channel_id=1, source_target_pairs={{0,1},{1,2},{2,3},{3,0},{4,7},{5,4},{6,5},{7,6},{8,9},{9,10},{10,1... | collective-permute-start | bytes 786440 | tf_op jit(solution)/shard_map/ppermute | solution.py:358
  16.8 0.3 collective-permute-start.5
  17.1 1.6 %collective-permute-done.2.w_far_mine_ref = bf16[128,1024]{1,0:T(8,128)(2,1)S(1)} collective-permute-done((bf16[128,1024]{1,0:T(8,128)(2,1)S(1)}, bf16[128,1024]{1,0:T(8,128)(2,1)S(1)}, u32[]{:S(2)}, u32[]{:S(2)}) %collective-permute-start.2) | collective-permute-done | bytes 262176 | tf_op jit(solution)/shard_map/ppermute | solution.py:348
  18.8 0.7 collective-permute-start.3
  19.4 0.0 collective-permute-done.6.w_first_ref
  19.4 5.9 %collective-permute-start.7 = (bf16[256,1024]{1,0:T(8,128)(2,1)S(1)}, bf16[256,1024]{1,0:T(8,128)(2,1)S(1)}, u32[]{:S(2)}, u32[]{:S(2)}) collective-permute-start(bf16[256,1024]{1,0:T(8,128)(2,1)S(1)} %collective-permute-done.6.w_first_ref), channel_id=1, source_target_pairs={{0,4},{4,0},{8,12},{12,8},{16,20},{20,16},{24,28},{28,24},{32,36},... | collective-permute-start | bytes 1572872 | tf_op jit(solution)/shard_map/ppermute | solution.py:363
  25.3 0.0 copy-done.5
  25.3 0.0 copy-done.2
  25.3 0.0 copy-done.3
  25.3 0.7 shard_map.84
  26.0 0.0 collective-permute-done.1.far_ref
  26.0 0.0 collective-permute-done.3.w_far_other_ref
  26.1 0.0 copy-done
  26.1 0.7 shard_map.85.started_ref
  26.8 2.0 %collective-permute-done.4.first_ref = bf16[512,256]{1,0:T(8,128)(2,1)S(1)} collective-permute-done((bf16[512,256]{1,0:T(8,128)(2,1)S(1)}, bf16[512,256]{1,0:T(8,128)(2,1)S(1)}, u32[]{:S(2)}, u32[]{:S(2)}) %collective-permute-start.4) | collective-permute-done | bytes 262176 | tf_op jit(solution)/shard_map/ppermute | solution.py:358
  28.8 1.4 %collective-permute-done.5.second_ref = bf16[512,256]{1,0:T(8,128)(2,1)S(1)} collective-permute-done((bf16[512,256]{1,0:T(8,128)(2,1)S(1)}, bf16[512,256]{1,0:T(8,128)(2,1)S(1)}, u32[]{:S(2)}, u32[]{:S(2)}) %collective-permute-start.5) | collective-permute-done | bytes 262176 | tf_op jit(solution)/shard_map/ppermute | solution.py:358
  30.2 0.0 collective-permute-done.7.w_second_ref
  30.2 1.9 %shard_map.86 = (bf16[512,1024]{1,0:T(8,128)(2,1)S(1)}, bf16[2,512,256]{2,1,0:T(8,128)(2,1)S(1)}) custom-call(f32[512,1024]{1,0:T(8,128)S(1)} %shard_map.85.started_ref, bf16[512,256]{1,0:T(8,128)(2,1)S(1)} %collective-permute-done.4.first_ref, bf16[512,256]{1,0:T(8,128)(2,1)S(1)} %collective-permute-done.5.second_ref, ...), custom_call_target="tpu_custom_call" | custom-call | flops 2147483648 | bytes 8388608 | tf_op jit(solution)/shard_map/pallas_call | solution.py:30
  32.1 29.1 %all_to_all.10 = bf16[64,16,256]{2,1,0:T(8,128)(2,1)S(1)} all-to-all(bf16[64,16,256]{2,1,0:T(8,128)(2,1)S(1)} %bitcast.11), channel_id=1, replica_groups=mesh['wide'=64,'narrow'=4] {'wide'}, dimensions={0} | all-to-all | bytes 1048576 | tf_op jit(solution)/shard_map/all_to_all | solution.py:449
  61.2 0.4 collective-permute-start.8
  61.6 0.1 pad_add_fusion.info_ref
  61.7 1.7 %shard_map.87 = (f32[1024,256]{1,0:T(8,128)S(1)}, f32[1024,128]{1,0:T(8,128)S(1)}) custom-call(s32[2]{0:T(128)S(1)} %pad_add_fusion.info_ref, bf16[1024,256]{1,0:T(8,128)(2,1)S(1)} %bitcast.9), custom_call_target="tpu_custom_call" | custom-call | flops 1073741824 | bytes 2097152 | tf_op jit(solution)/shard_map/pallas_call | solution.py:30
  63.4 0.0 collective-permute-done.8.other_ref
  63.4 0.0 copy-start.4
  63.5 2.5 %shard_map.88 = bf16[1024,128]{1,0:T(8,128)(2,1)} custom-call(s32[2]{0:T(128)S(1)} %pad_add_fusion.info_ref, bf16[1024,256]{1,0:T(8,128)(2,1)S(1)} %bitcast.10, bf16[1024,256]{1,0:T(8,128)(2,1)S(1)} %collective-permute-done.8.other_ref, f32[1024,256]{1,0:T(8,128)S(1)} %get-tuple-element.43.mixed_ref, f32[1024,128]{1,0:T(8,128)S(1)} %get-tuple-element.44.top_ref), custom_call_target="tpu_custom_call" | custom-call | flops 1073741824 | bytes 2097152 | tf_op jit(solution)/shard_map/pallas_call | solution.py:30
  65.9 5.4 %all-to-all-start.1 = ((bf16[64,16,128]{2,1,0:T(8,128)(2,1)}), bf16[64,16,128]{2,1,0:T(8,128)(2,1)S(1)}, u32[]{:S(2)}, u32[]{:S(2)}) async-start(bf16[64,16,128]{2,1,0:T(8,128)(2,1)} %bitcast.6), calls=%async_computation.1 | async-start | bytes 524288 | tf_op jit(solution)/shard_map/all_to_all | solution.py:471
  71.4 13.2 %all-to-all-done.1 = bf16[64,16,128]{2,1,0:T(8,128)(2,1)S(1)} async-done(((bf16[64,16,128]{2,1,0:T(8,128)(2,1)}), bf16[64,16,128]{2,1,0:T(8,128)(2,1)S(1)}, u32[]{:S(2)}, u32[]{:S(2)}) %all-to-all-start.1) | async-done | bytes 262176 | tf_op jit(solution)/shard_map/all_to_all | solution.py:471
  84.6 0.0 copy-done.4
  84.6 0.8 shard_map.89
  85.4 2.1 %collective-permute-start.9 = (bf16[512,256]{1,0:T(8,128)(2,1)S(1)}, bf16[512,256]{1,0:T(8,128)(2,1)S(1)}, u32[]{:S(2)}, u32[]{:S(2)}) collective-permute-start(bf16[512,256]{1,0:T(8,128)(2,1)S(1)} %get-tuple-element.47), channel_id=1, source_target_pairs={{0,2},{1,3},{2,0},{3,1},{4,6},{5,7},{6,4},{7,5},{8,10},{9,11},{10,... | collective-permute-start | bytes 786440 | tf_op jit(solution)/shard_map/ppermute | solution.py:348
  87.5 0.0 collective-permute-start.10
  87.5 2.7 %collective-permute-start.11 = (bf16[512,256]{1,0:T(8,128)(2,1)S(1)}, bf16[512,256]{1,0:T(8,128)(2,1)S(1)}, u32[]{:S(2)}, u32[]{:S(2)}) collective-permute-start(bf16[512,256]{1,0:T(8,128)(2,1)S(1)} %get-tuple-element.49), channel_id=1, source_target_pairs={{0,3},{1,0},{2,1},{3,2},{4,7},{5,4},{6,5},{7,6},{8,11},{9,8},{10,9... | collective-permute-start | bytes 786440 | tf_op jit(solution)/shard_map/ppermute | solution.py:348
  90.2 4.5 %collective-permute-done.9.one_ref = bf16[512,256]{1,0:T(8,128)(2,1)S(1)} collective-permute-done((bf16[512,256]{1,0:T(8,128)(2,1)S(1)}, bf16[512,256]{1,0:T(8,128)(2,1)S(1)}, u32[]{:S(2)}, u32[]{:S(2)}) %collective-permute-start.9) | collective-permute-done | bytes 262176 | tf_op jit(solution)/shard_map/ppermute | solution.py:348
  94.7 6.2 %collective-permute-done.10.two_ref = bf16[512,256]{1,0:T(8,128)(2,1)S(1)} collective-permute-done((bf16[512,256]{1,0:T(8,128)(2,1)S(1)}, bf16[512,256]{1,0:T(8,128)(2,1)S(1)}, u32[]{:S(2)}, u32[]{:S(2)}) %collective-permute-start.10) | collective-permute-done | bytes 262176 | tf_op jit(solution)/shard_map/ppermute | solution.py:348
  100.8 0.0 collective-permute-done.11.three_ref
  100.8 0.9 shard_map.90
  (2 shorter events, 0.0 us)
Async XLA Ops:
  0.0 6.1 %copy-start.1 = (bf16[256,1024]{1,0:T(8,128)(2,1)S(1)}, bf16[256,1024]{1,0:T(8,128)(2,1)}, u32[]{:S(2)}) copy-start(bf16[256,1024]{1,0:T(8,128)(2,1)} %w_out_any) | copy-start | bytes 1572868
  0.0 25.3 %copy-start.5 = (s32[2,512]{1,0:T(2,128)S(1)}, s32[2,512]{1,0:T(2,128)}, u32[]{:S(2)}) copy-start(s32[2,512]{1,0:T(2,128)} %ids_any) | copy-start | bytes 12292
  0.0 25.3 %copy-start.2 = (bf16[1024,256]{1,0:T(8,128)(2,1)S(1)}, bf16[1024,256]{1,0:T(8,128)(2,1)}, u32[]{:S(2)}) copy-start(bf16[1024,256]{1,0:T(8,128)(2,1)} %w_qk_any.2) | copy-start | bytes 1572868
  0.0 25.3 %copy-start.3 = (bf16[1024,256]{1,0:T(8,128)(2,1)S(1)}, bf16[1024,256]{1,0:T(8,128)(2,1)}, u32[]{:S(2)}) copy-start(bf16[1024,256]{1,0:T(8,128)(2,1)} %w_value_any.2) | copy-start | bytes 1572868
  0.0 19.4 %collective-permute-start.6 = (bf16[256,1024]{1,0:T(8,128)(2,1)}, bf16[256,1024]{1,0:T(8,128)(2,1)S(1)}, u32[]{:S(2)}, u32[]{:S(2)}) collective-permute-start(bf16[256,1024]{1,0:T(8,128)(2,1)} %w_out_any), channel_id=1, source_target_pairs={{0,1},{1,2},{2,3},{3,0},{4,7},{5,4},{6,5},{7,6},{8,9},{9,10},{10,1... | collective-permute-start | bytes 1572872 | tf_op jit(solution)/shard_map/ppermute | solution.py:358
  6.1 6.1 %collective-permute-start = (bf16[2,256,256]{2,1,0:T(8,128)(2,1)S(1)}, bf16[2,256,256]{2,1,0:T(8,128)(2,1)S(1)}, u32[]{:S(2)}, u32[]{:S(2)}) collective-permute-start(bf16[2,256,256]{2,1,0:T(8,128)(2,1)S(1)} %get-tuple-element.31), channel_id=1, source_target_pairs={{0,4},{4,8},{8,12},{12,16},{16,20},{20,24},{24,28},{28,32},{32,36}... | collective-permute-start | bytes 786440 | tf_op jit(solution)/shard_map/ppermute | solution.py:399
  8.9 9.9 %collective-permute-start.2 = (bf16[128,1024]{1,0:T(8,128)(2,1)S(1)}, bf16[128,1024]{1,0:T(8,128)(2,1)S(1)}, u32[]{:S(2)}, u32[]{:S(2)}) collective-permute-start(bf16[128,1024]{1,0:T(8,128)(2,1)S(1)} %constant_dynamic-slice_fusion), channel_id=1, source_target_pairs={{0,2},{1,3},{2,0},{3,1},{4,6},{5,7},{6,4},{7,5},{8,10},{9,11},{10,... | collective-permute-start | bytes 786440 | tf_op jit(solution)/shard_map/ppermute | solution.py:348
  13.1 12.9 %copy-start = (bf16[512,1024]{1,0:T(8,128)(2,1)S(1)}, bf16[512,1024]{1,0:T(8,128)(2,1)}, u32[]{:S(2)}) copy-start(bf16[512,1024]{1,0:T(8,128)(2,1)} %tokens_ref.1) | copy-start | bytes 3145732
  13.1 12.9 %collective-permute-start.1 = (bf16[512,256]{1,0:T(8,128)(2,1)S(1)}, bf16[512,256]{1,0:T(8,128)(2,1)S(1)}, u32[]{:S(2)}, u32[]{:S(2)}) collective-permute-start(bf16[512,256]{1,0:T(8,128)(2,1)S(1)} %shard_map.83.own_ref), channel_id=1, source_target_pairs={{0,2},{1,3},{2,0},{3,1},{4,6},{5,7},{6,4},{7,5},{8,10},{9,11},{10,... | collective-permute-start | bytes 786440 | tf_op jit(solution)/shard_map/ppermute | solution.py:348
  15.7 13.2 %collective-permute-start.4 = (bf16[512,256]{1,0:T(8,128)(2,1)S(1)}, bf16[512,256]{1,0:T(8,128)(2,1)S(1)}, u32[]{:S(2)}, u32[]{:S(2)}) collective-permute-start(bf16[512,256]{1,0:T(8,128)(2,1)S(1)} %shard_map.83.own_ref), channel_id=1, source_target_pairs={{0,1},{1,2},{2,3},{3,0},{4,7},{5,4},{6,5},{7,6},{8,9},{9,10},{10,1... | collective-permute-start | bytes 786440 | tf_op jit(solution)/shard_map/ppermute | solution.py:358
  16.8 13.4 %collective-permute-start.5 = (bf16[512,256]{1,0:T(8,128)(2,1)S(1)}, bf16[512,256]{1,0:T(8,128)(2,1)S(1)}, u32[]{:S(2)}, u32[]{:S(2)}) collective-permute-start(bf16[512,256]{1,0:T(8,128)(2,1)S(1)} %shard_map.83.own_ref), channel_id=1, source_target_pairs={{0,3},{1,0},{2,1},{3,2},{4,5},{5,6},{6,7},{7,4},{8,11},{9,8},{10,9... | collective-permute-start | bytes 786440 | tf_op jit(solution)/shard_map/ppermute | solution.py:358
  18.8 7.3 %collective-permute-start.3 = (bf16[128,1024]{1,0:T(8,128)(2,1)S(1)}, bf16[128,1024]{1,0:T(8,128)(2,1)S(1)}, u32[]{:S(2)}, u32[]{:S(2)}) collective-permute-start(bf16[128,1024]{1,0:T(8,128)(2,1)S(1)} %collective-permute-done.2.w_far_mine_ref), channel_id=1, source_target_pairs={{0,4},{4,0},{8,12},{12,8},{16,20},{20,16},{24,28},{28,24},{32,36},... | collective-permute-start | bytes 786440 | tf_op jit(solution)/shard_map/ppermute | solution.py:363
  19.4 10.8 %collective-permute-start.7 = (bf16[256,1024]{1,0:T(8,128)(2,1)S(1)}, bf16[256,1024]{1,0:T(8,128)(2,1)S(1)}, u32[]{:S(2)}, u32[]{:S(2)}) collective-permute-start(bf16[256,1024]{1,0:T(8,128)(2,1)S(1)} %collective-permute-done.6.w_first_ref), channel_id=1, source_target_pairs={{0,4},{4,0},{8,12},{12,8},{16,20},{20,16},{24,28},{28,24},{32,36},... | collective-permute-start | bytes 1572872 | tf_op jit(solution)/shard_map/ppermute | solution.py:363
  61.2 2.2 %collective-permute-start.8 = (bf16[1024,256]{1,0:T(8,128)(2,1)S(1)}, bf16[1024,256]{1,0:T(8,128)(2,1)S(1)}, u32[]{:S(2)}, u32[]{:S(2)}) collective-permute-start(bf16[1024,256]{1,0:T(8,128)(2,1)S(1)} %bitcast.8), channel_id=1, source_target_pairs={{0,4},{4,0},{8,12},{12,8},{16,20},{20,16},{24,28},{28,24},{32,36},... | collective-permute-start | bytes 1572872 | tf_op jit(solution)/shard_map/ppermute | solution.py:363
  63.4 21.1 %copy-start.4 = (bf16[256,1024]{1,0:T(8,128)(2,1)S(1)}, bf16[256,1024]{1,0:T(8,128)(2,1)}, u32[]{:S(2)}) copy-start(bf16[256,1024]{1,0:T(8,128)(2,1)} %weight_ref.1) | copy-start | bytes 1572868
  65.9 18.6 %all-to-all-start.1 = ((bf16[64,16,128]{2,1,0:T(8,128)(2,1)}), bf16[64,16,128]{2,1,0:T(8,128)(2,1)S(1)}, u32[]{:S(2)}, u32[]{:S(2)}) async-start(bf16[64,16,128]{2,1,0:T(8,128)(2,1)} %bitcast.6), calls=%async_computation.1 | async-start | bytes 524288 | tf_op jit(solution)/shard_map/all_to_all | solution.py:471
  85.4 9.3 %collective-permute-start.9 = (bf16[512,256]{1,0:T(8,128)(2,1)S(1)}, bf16[512,256]{1,0:T(8,128)(2,1)S(1)}, u32[]{:S(2)}, u32[]{:S(2)}) collective-permute-start(bf16[512,256]{1,0:T(8,128)(2,1)S(1)} %get-tuple-element.47), channel_id=1, source_target_pairs={{0,2},{1,3},{2,0},{3,1},{4,6},{5,7},{6,4},{7,5},{8,10},{9,11},{10,... | collective-permute-start | bytes 786440 | tf_op jit(solution)/shard_map/ppermute | solution.py:348
  87.5 13.3 %collective-permute-start.10 = (bf16[512,256]{1,0:T(8,128)(2,1)S(1)}, bf16[512,256]{1,0:T(8,128)(2,1)S(1)}, u32[]{:S(2)}, u32[]{:S(2)}) collective-permute-start(bf16[512,256]{1,0:T(8,128)(2,1)S(1)} %get-tuple-element.48), channel_id=1, source_target_pairs={{0,1},{1,2},{2,3},{3,0},{4,5},{5,6},{6,7},{7,4},{8,9},{9,10},{10,1... | collective-permute-start | bytes 786440 | tf_op jit(solution)/shard_map/ppermute | solution.py:348
  87.5 13.3 %collective-permute-start.11 = (bf16[512,256]{1,0:T(8,128)(2,1)S(1)}, bf16[512,256]{1,0:T(8,128)(2,1)S(1)}, u32[]{:S(2)}, u32[]{:S(2)}) collective-permute-start(bf16[512,256]{1,0:T(8,128)(2,1)S(1)} %get-tuple-element.49), channel_id=1, source_target_pairs={{0,3},{1,0},{2,1},{3,2},{4,7},{5,4},{6,5},{7,6},{8,11},{9,8},{10,9... | collective-permute-start | bytes 786440 | tf_op jit(solution)/shard_map/ppermute | solution.py:348
